TPU v7x, 128 devices: a whole 4x4x4 slice. The times are simulated.
128 devices in a mesh: section: 2 (over core), head: 4 (over y), seq: 16 (over x, z).
Axes of the slice: x: 4, y: 4, z: 4, core: 2. Of those that a mesh axis runs over, the one named last changes fastest.
Arguments:
- x_in: bfloat16 [2, 4096, 1536], P(None, 'seq'), may hold values from -6 to 6
- norm_gain: float32 [2, 1536], P('section'), may hold values from 0.5 to 1.5
- w_zx: bfloat16 [2, 1536, 2, 3072], P('section', None, None, 'head'), may hold values from -0.15625 to 0.15625
- w_bc: bfloat16 [2, 1536, 256], P('section'), may hold values from -0.15625 to 0.15625
- w_dt: bfloat16 [2, 1536, 48], P('section', None, 'head'), may hold values from -0.15625 to 0.15625
- dt_bias: float32 [2, 48], P('section', 'head'), may hold values from -8 to -3
- a_log: float32 [2, 48], P('section', 'head'), may hold values from 0 to 1.5
- d_skip: float32 [2, 48], P('section', 'head'), may hold values from 0.5 to 1.5
- conv_x: bfloat16 [2, 4, 3072], P('section', None, 'head'), may hold values from -3 to 3
- conv_bc: bfloat16 [2, 4, 256], P('section'), may hold values from -3 to 3
- gate_gain: float32 [2, 3072], P('section', 'head'), may hold values from 0.5 to 1.5
- w_out: bfloat16 [2, 3072, 1536], P('section', 'head'), may hold values from -0.109375 to 0.109375
- cotangent: bfloat16 [2, 4096, 1536], P(None, 'seq'), may hold values from -6 to 6
Outputs:
- section_out: bfloat16 [2, 2, 4096, 1536], P('section', None, 'seq')
- grads_in: bfloat16 [2, 2, 4096, 1536], P('section', None, 'seq')
- g_norm_gain: float32 [2, 1536], P('section')
- g_w_zx: float32 [2, 1536, 2, 3072], P('section', None, None, 'head')
- g_w_bc: float32 [2, 1536, 256], P('section')
- g_w_dt: float32 [2, 1536, 48], P('section', None, 'head')
- g_dt_bias: float32 [2, 48], P('section', 'head')
- g_a_log: float32 [2, 48], P('section', 'head')
- g_d_skip: float32 [2, 48], P('section', 'head')
- g_conv_x: float32 [2, 4, 3072], P('section', None, 'head')
- g_conv_bc: float32 [2, 4, 256], P('section')
- g_gate_gain: float32 [2, 3072], P('section', 'head')
- g_w_out: float32 [2, 3072, 1536], P('section', 'head')
All inputs are finite; a program needn't handle non-finite values.
Results may differ from a plain program's by a relative error of at most 0.025.
Values may be sent and summed in bfloat16 or wider, within the bound.
A program may use at most 192 MiB of HBM per device.

v0:
```python
import jax
import jax.numpy as jnp
from jax import lax
from jax.sharding import PartitionSpec as P

INNER = 3072


EPS = 1e-05
HIGH = lax.Precision.HIGHEST


def from_behind(block, axis, distance):
    devices = range(lax.axis_size(axis))
    route = [(i - distance, i) for i in devices if i - distance in devices]
    return lax.ppermute(block, axis, route)


def prefix(shard, axis, join, neutral):
    place = lax.axis_index(axis)
    gathered = jax.tree.map(
        lambda a, kind: lax.all_gather(a.astype(kind), axis), shard, (jnp.bfloat16, jnp.bfloat16)
    )
    state = jax.tree.map(lambda a, e: jnp.zeros_like(a) + jnp.asarray(e, a.dtype), shard, neutral)

    def prefix_one(step, state):
        return join(
            state,
            jax.tree.map(
                lambda a, own: lax.dynamic_index_in_dim(a, step, 0, False).astype(own.dtype),
                gathered,
                shard,
            ),
        )

    return lax.fori_loop(0, place, prefix_one, state)


def entering_2(shard, axis, join, neutral):
    count = lax.axis_size(axis)
    place = lax.axis_index(axis)
    ahead = count - 1 - place
    gathered = jax.tree.map(
        lambda a, kind: lax.all_gather(a.astype(kind), axis),
        shard,
        jax.tree.map(lambda a: jnp.bfloat16 if a.dtype == jnp.float32 else a.dtype, shard),
    )
    state = jax.tree.map(lambda a, e: jnp.zeros_like(a) + jnp.asarray(e, a.dtype), shard, neutral)

    def entering_one(step, state):
        source = count - 1 - step
        return join(
            state,
            jax.tree.map(
                lambda a, own: lax.dynamic_index_in_dim(a, source, 0, False).astype(own.dtype),
                gathered,
                shard,
            ),
        )

    return lax.fori_loop(0, ahead, entering_one, state)


def silu(values):
    return values * jax.nn.sigmoid(values)


def silu_slope(values):
    sigma = jax.nn.sigmoid(values)
    return sigma * (1.0 + values * (1.0 - sigma))


def ssd_block(x_heads, b_rows, c_rows, step_sizes, a_rates, state_in):
    length = x_heads.shape[0]
    log_decay = jnp.cumsum(step_sizes * a_rates[None, :], axis=0)
    places = jnp.arange(length)
    causal = places[:, None] >= places[None, :]
    spans = jnp.where(causal[:, :, None], log_decay[:, None, :] - log_decay[None, :, :], -1e30)
    scores = jnp.dot(c_rows, b_rows.T, precision=HIGH)
    mixing = scores[:, :, None] * jnp.exp(spans) * step_sizes[None, :, :]
    y_inner = jnp.einsum("tsh,shp->thp", mixing, x_heads, precision=HIGH)
    y_carry = jnp.exp(log_decay)[:, :, None] * jnp.einsum(
        "tn,hpn->thp", c_rows, state_in, precision=HIGH
    )
    weights_tail = jnp.exp(log_decay[-1:, :] - log_decay) * step_sizes
    state_out = jnp.exp(log_decay[-1])[:, None, None] * state_in + jnp.einsum(
        "sh,sn,shp->hpn", weights_tail, b_rows, x_heads, precision=HIGH
    )
    return (y_inner + y_carry, state_out)


def block_state(x_heads, b_rows, step_sizes, a_rates):
    log_decay = jnp.cumsum(step_sizes * a_rates[None, :], axis=0)
    weights_tail = jnp.exp(log_decay[-1:, :] - log_decay) * step_sizes
    carried = jnp.einsum("sh,sn,shp->hpn", weights_tail, b_rows, x_heads, precision=HIGH)
    return (jnp.exp(log_decay[-1]), carried)


def chain_join(earlier, later):
    return (earlier[0] * later[0], later[0][:, None, None] * earlier[1] + later[1])


def depth_conv(extended, taps, length):
    total = taps[0] * extended[0:length]
    for offset in range(1, taps.shape[0]):
        total = total + taps[offset] * extended[offset : offset + length]
    return total


def depth_conv_back(extended, taps, length):
    rim_rows = taps.shape[0] - 1
    total = taps[0] * extended[rim_rows : rim_rows + length]
    for offset in range(1, taps.shape[0]):
        total = total + taps[offset] * extended[rim_rows - offset : rim_rows - offset + length]
    return total


def mixer_forward(entering, params):
    norm_gain, w_zx, w_bc, w_dt, dt_bias, a_log, d_skip, conv_x, conv_bc, gate_gain, w_out = params
    length = entering.shape[0]
    rim_rows = conv_x.shape[0] - 1
    inner_dev = w_out.shape[0]
    heads_dev = w_dt.shape[1]
    state_size = w_bc.shape[1] // 2
    x_rows = entering.astype(jnp.float32)
    norm_scale = lax.rsqrt(jnp.mean(x_rows * x_rows, axis=-1, keepdims=True) + EPS)
    normed = (x_rows * norm_scale * norm_gain).astype(jnp.bfloat16)
    zx_rows = jnp.dot(normed, w_zx.reshape(w_zx.shape[0], -1), preferred_element_type=jnp.float32)
    z_part = zx_rows[:, :inner_dev]
    x_pre = zx_rows[:, inner_dev:]
    bc_pre = jnp.dot(normed, w_bc, preferred_element_type=jnp.float32)
    dt_pre = jnp.dot(normed, w_dt, preferred_element_type=jnp.float32)
    prev_x, prev_bc = from_behind(
        (x_pre[length - rim_rows :], bc_pre[length - rim_rows :]), "seq", 1
    )
    x_ext = jnp.concatenate([prev_x, x_pre], axis=0)
    bc_ext = jnp.concatenate([prev_bc, bc_pre], axis=0)
    x_conv = depth_conv(x_ext, conv_x.astype(jnp.float32), length)
    bc_conv = depth_conv(bc_ext, conv_bc.astype(jnp.float32), length)
    x_act = silu(x_conv)
    bc_act = silu(bc_conv)
    step_sizes = jax.nn.softplus(dt_pre + dt_bias)
    a_rates = -jnp.exp(a_log)
    x_heads = x_act.reshape(length, heads_dev, -1)
    b_rows = bc_act[:, :state_size]
    c_rows = bc_act[:, state_size:]
    decay_total, carried = block_state(x_heads, b_rows, step_sizes, a_rates)
    identity = (jnp.ones_like(decay_total), jnp.zeros_like(carried))
    unused_decay, state_in = prefix((decay_total, carried), "seq", chain_join, identity)
    y_state, unused_end = ssd_block(x_heads, b_rows, c_rows, step_sizes, a_rates, state_in)
    ssd_out = (y_state + d_skip[None, :, None] * x_heads).reshape(length, inner_dev)
    gated = ssd_out * silu(z_part)
    square_sum = lax.psum(jnp.sum(gated * gated, axis=-1), "head")
    gate_scale = lax.rsqrt(square_sum[:, None] / INNER + EPS)
    mixed_in = (gated * gate_scale * gate_gain).astype(jnp.bfloat16)
    partial_out = jnp.dot(mixed_in, w_out, preferred_element_type=jnp.float32)
    result = (x_rows + lax.psum(partial_out, "head")).astype(jnp.bfloat16)
    kept_rows = (
        x_rows,
        norm_scale,
        normed,
        z_part,
        x_ext,
        bc_ext,
        x_conv,
        bc_conv,
        dt_pre,
        step_sizes,
        x_heads,
        b_rows,
        c_rows,
        state_in,
        ssd_out,
        gated,
        gate_scale,
        mixed_in,
    )
    return (result, kept_rows)


def mixer_backward(grad_out, kept_rows, params, wide_f32):
    norm_gain, w_zx, w_bc, w_dt, dt_bias, a_log, d_skip, conv_x, conv_bc, gate_gain, w_out = params
    w_bc_f32, w_dt_f32 = wide_f32
    (
        x_rows,
        norm_scale,
        normed,
        z_part,
        x_ext,
        bc_ext,
        x_conv,
        bc_conv,
        dt_pre,
        step_sizes,
        x_heads,
        b_rows,
        c_rows,
        state_in,
        ssd_out,
        gated,
        gate_scale,
        mixed_in,
    ) = kept_rows
    length = grad_out.shape[0]
    rim_rows = conv_x.shape[0] - 1
    inner_dev = w_out.shape[0]
    model_width = x_rows.shape[1]
    contract_last = (((1,), (1,)), ((), ()))
    contract_first = (((0,), (0,)), ((), ()))
    d_mixed = lax.dot_general(grad_out, w_out, contract_last, preferred_element_type=jnp.float32)
    g_w_out = lax.dot_general(
        mixed_in, grad_out, contract_first, preferred_element_type=jnp.float32
    )
    weighted = gate_gain * d_mixed
    g_gate = jnp.sum(gated * gate_scale * d_mixed, axis=0)
    cross_sum = lax.psum(jnp.sum(gated * weighted, axis=-1), "head")
    d_gated = gate_scale * weighted - gated * gate_scale**3 * cross_sum[:, None] / INNER
    d_ssd = d_gated * silu(z_part)
    d_zpart = d_gated * ssd_out * silu_slope(z_part)
    d_heads = d_ssd.reshape(x_heads.shape)
    g_skip = jnp.sum(d_heads * x_heads, axis=(0, 2))
    a_rates = -jnp.exp(a_log)
    log_decay = jnp.cumsum(step_sizes * a_rates[None, :], axis=0)
    own_state = jnp.einsum("th,thp,tn->hpn", jnp.exp(log_decay), d_heads, c_rows, precision=HIGH)
    decay_total = jnp.exp(log_decay[-1])
    identity = (jnp.ones_like(decay_total), jnp.zeros_like(state_in))
    unused_decay, state_grad = entering_2((decay_total, own_state), "seq", chain_join, identity)
    unused_primal, pull_back = jax.vjp(
        ssd_block, x_heads, b_rows, c_rows, step_sizes, a_rates, state_in
    )
    all_terms = pull_back((d_heads, state_grad))
    d_x_heads = all_terms[0] + d_skip[None, :, None] * d_heads
    grad_b = all_terms[1]
    grad_c = all_terms[2]
    d_step = all_terms[3]
    d_rate = all_terms[4]
    d_x_conv = d_x_heads.reshape(length, inner_dev) * silu_slope(x_conv)
    d_bc_conv = jnp.concatenate([grad_b, grad_c], axis=1) * silu_slope(bc_conv)
    next_x, next_bc = from_behind((d_x_conv[:rim_rows], d_bc_conv[:rim_rows]), "seq", -1)
    d_x_pre = depth_conv_back(
        jnp.concatenate([d_x_conv, next_x], axis=0), conv_x.astype(jnp.float32), length
    )
    d_bc_pre = depth_conv_back(
        jnp.concatenate([d_bc_conv, next_bc], axis=0), conv_bc.astype(jnp.float32), length
    )
    g_conv_x = jnp.stack(
        [
            jnp.sum(x_ext[offset : offset + length] * d_x_conv, axis=0)
            for offset in range(rim_rows + 1)
        ]
    )
    g_conv_bc = jnp.stack(
        [
            jnp.sum(bc_ext[offset : offset + length] * d_bc_conv, axis=0)
            for offset in range(rim_rows + 1)
        ]
    )
    d_dt_pre = d_step * jax.nn.sigmoid(dt_pre + dt_bias)
    g_bias = jnp.sum(d_dt_pre, axis=0)
    g_rate = d_rate * a_rates
    d_zx = jnp.concatenate([d_zpart, d_x_pre], axis=1).astype(jnp.bfloat16)
    w_flat = w_zx.reshape(w_zx.shape[0], -1)
    d_normed = lax.dot_general(d_zx, w_flat, contract_last, preferred_element_type=jnp.float32)
    d_normed = (
        d_normed
        + jnp.dot(d_dt_pre, w_dt_f32.T, precision=HIGH)
        + jnp.dot(d_bc_pre, w_bc_f32.T, precision=HIGH)
    )
    normed_f32 = normed.astype(jnp.float32)
    g_zx = lax.dot_general(
        normed, d_zx, contract_first, preferred_element_type=jnp.float32
    ).reshape(w_zx.shape)
    g_dt = jnp.dot(normed_f32.T, d_dt_pre, precision=HIGH)
    g_bc = jnp.dot(normed_f32.T, d_bc_pre, precision=HIGH)
    share = model_width // lax.axis_size("head")
    d_normed = lax.psum(d_normed.astype(jnp.bfloat16), "head").astype(jnp.float32)
    d_scaled = d_normed * norm_gain
    owned = (jnp.arange(model_width) // share == lax.axis_index("head")).astype(jnp.float32)
    g_norm = jnp.sum(x_rows * norm_scale * d_normed, axis=0) * owned
    d_rows = (
        norm_scale * d_scaled
        - x_rows * norm_scale**3 * jnp.mean(x_rows * d_scaled, axis=-1, keepdims=True)
        + grad_out.astype(jnp.float32)
    )
    grads = (g_norm, g_zx, g_bc, g_dt, g_bias, g_rate, g_skip, g_conv_x, g_conv_bc, g_gate, g_w_out)
    return (d_rows, grads)


def on_device(
    x_in,
    norm_gain,
    w_zx,
    w_bc,
    w_dt,
    dt_bias,
    a_log,
    d_skip,
    conv_x,
    conv_bc,
    gate_gain,
    w_out,
    cotangent,
):
    params = (
        norm_gain[0],
        w_zx[0],
        w_bc[0],
        w_dt[0],
        dt_bias[0],
        a_log[0],
        d_skip[0],
        conv_x[0],
        conv_bc[0],
        gate_gain[0],
        w_out[0],
    )
    wide_f32 = (w_bc[0].astype(jnp.float32), w_dt[0].astype(jnp.float32))
    micro_count = x_in.shape[0]
    first_section = lax.axis_index("section") == 0
    received = jnp.zeros_like(x_in[0])
    results = []
    stored = []
    for tick_index in range(micro_count + 1):
        entering = jnp.where(first_section, x_in[min(tick_index, micro_count - 1)], received)
        result, kept_rows = mixer_forward(entering, params)
        results.append(result)
        stored.append(kept_rows)
        if tick_index < micro_count:
            received = from_behind(result, "section", 1)
    returned = jnp.zeros_like(cotangent[0])
    totals = None
    leaving = []
    for tick_index in range(micro_count + 1):
        kept_rows = jax.tree.map(
            lambda left_val, right_val: jnp.where(first_section, left_val, right_val),
            stored[max(tick_index - 1, 0)],
            stored[min(tick_index + 1, micro_count)],
        )
        if tick_index < micro_count:
            from_loss = cotangent[tick_index]
        else:
            from_loss = jnp.zeros_like(cotangent[0])
        grad_out = jnp.where(first_section, returned, from_loss)
        d_rows, grads = mixer_backward(grad_out, kept_rows, params, wide_f32)
        if totals is None:
            totals = grads
        else:
            totals = jax.tree.map(jnp.add, totals, grads)
        sent_rows = d_rows.astype(jnp.bfloat16)
        leaving.append(sent_rows)
        if tick_index < micro_count:
            returned = from_behind(sent_rows, "section", -1)
    section_out = jnp.stack(
        [
            jnp.where(first_section, results[batch_index], results[batch_index + 1])
            for batch_index in range(micro_count)
        ]
    )[None]
    grads_in = jnp.stack(
        [
            jnp.where(first_section, leaving[batch_index + 1], leaving[batch_index])
            for batch_index in range(micro_count)
        ]
    )[None]
    g_norm, g_zx, g_bc, g_dt, g_bias, g_rate, g_skip, g_conv_x, g_conv_bc, g_gate, g_w_out = totals
    seq_sums = (
        lax.psum(g_zx.astype(jnp.bfloat16), "seq").astype(jnp.float32),
        lax.psum(g_dt.astype(jnp.bfloat16), "seq").astype(jnp.float32),
        lax.psum(g_bias.astype(jnp.bfloat16), "seq").astype(jnp.float32),
        lax.psum(g_rate.astype(jnp.bfloat16), "seq").astype(jnp.float32),
        lax.psum(g_skip.astype(jnp.bfloat16), "seq").astype(jnp.float32),
        lax.psum(g_conv_x.astype(jnp.bfloat16), "seq").astype(jnp.float32),
        lax.psum(g_gate.astype(jnp.bfloat16), "seq").astype(jnp.float32),
        lax.psum(g_w_out.astype(jnp.bfloat16), "seq").astype(jnp.float32),
    )
    shared = lax.psum((g_bc, g_conv_bc, g_norm), ("head", "seq"))
    return (
        section_out,
        grads_in,
        shared[2][None],
        seq_sums[0][None],
        shared[0][None],
        seq_sums[1][None],
        seq_sums[2][None],
        seq_sums[3][None],
        seq_sums[4][None],
        seq_sums[5][None],
        shared[1][None],
        seq_sums[6][None],
        seq_sums[7][None],
    )


def solution(mesh):
    in_specs = (
        P(None, "seq", None),
        P("section", None),
        P("section", None, None, "head"),
        P("section", None, None),
        P("section", None, "head"),
        P("section", "head"),
        P("section", "head"),
        P("section", "head"),
        P("section", None, "head"),
        P("section", None, None),
        P("section", "head"),
        P("section", "head", None),
        P(None, "seq", None),
    )
    out_specs = (
        P("section", None, "seq", None),
        P("section", None, "seq", None),
        P("section", None),
        P("section", None, None, "head"),
        P("section", None, None),
        P("section", None, "head"),
        P("section", "head"),
        P("section", "head"),
        P("section", "head"),
        P("section", None, "head"),
        P("section", None, None),
        P("section", "head"),
        P("section", "head", None),
    )
    return jax.shard_map(
        on_device, mesh=mesh, in_specs=in_specs, out_specs=out_specs, check_vma=False
    )
```

profile of v0, /device:TPU:0, one launch (start us, length us, event | category | flops | bytes accessed | tf_op | source)
XLA Modules:
  0.0 1739.0 jit_solution(667464103653302703)
XLA Ops:
  8.9 5.5 copy.301
  36.7 20.4 %all-gather.6 = bf16[16,1,12]{2,1,0:T(2,128)(2,1)S(1)} all-gather(bf16[1,1,12]{2,1,0:T(2,128)(2,1)S(1)} %bitcast.816), channel_id=1, replica_groups=mesh['section'=2,'head'=4,'seq'=16] {'seq'}, dimensions={0}, use_global_device_ids=true | all-gather | bytes 408 | tf_op jit(solution)/shard_map/all_gather | solution.py:22
  60.1 25.0 %all-gather.19.cloned.1.call-done = bf16[192,64,128]{2,1,0:T(8,128)(2,1)} async-done(((bf16[12,64,128]{2,1,0:T(8,128)(2,1)}), bf16[192,64,128]{2,1,0:T(8,128)(2,1)}) %all-gather.19.cloned.1.call-update) | async-done | bytes 3145744 | tf_op jit(solution)/shard_map/all_gather | solution.py:22
  86.8 5.7 fusion.169
  97.0 11.1 psum.161
  112.9 73.5 %all-reduce.19.cloned.1.call-done = f32[256,1536]{1,0:T(8,128)} async-done(((f32[256,1536]{1,0:T(8,128)}), f32[256,1536]{1,0:T(8,128)}) %all-reduce.19.cloned.1.call-update) | async-done | bytes 1572880 | tf_op jit(solution)/shard_map/psum | solution.py:157
  194.1 4.9 fusion.495
  228.3 20.1 %all-gather.7 = bf16[16,1,12]{2,1,0:T(2,128)(2,1)S(1)} all-gather(bf16[1,1,12]{2,1,0:T(2,128)(2,1)S(1)} %bitcast.817), channel_id=1, replica_groups=mesh['section'=2,'head'=4,'seq'=16] {'seq'}, dimensions={0}, use_global_device_ids=true | all-gather | bytes 408 | tf_op jit(solution)/shard_map/all_gather | solution.py:22
  251.1 23.5 %all-gather.21.cloned.1.call-done = bf16[192,64,128]{2,1,0:T(8,128)(2,1)} async-done(((bf16[12,64,128]{2,1,0:T(8,128)(2,1)}), bf16[192,64,128]{2,1,0:T(8,128)(2,1)}) %all-gather.21.cloned.1.call-update) | async-done | bytes 3145744 | tf_op jit(solution)/shard_map/all_gather | solution.py:22
  277.2 6.1 fusion.172
  288.6 11.1 psum.163
  308.0 85.4 %all-reduce.21.cloned.1.call-done = f32[256,1536]{1,0:T(8,128)} async-done(((f32[256,1536]{1,0:T(8,128)}), f32[256,1536]{1,0:T(8,128)}) %all-reduce.21.cloned.1.call-update) | async-done | bytes 1572880 | tf_op jit(solution)/shard_map/psum | solution.py:157
  402.4 5.0 fusion.491
  436.0 20.1 %all-gather.8 = bf16[16,1,12]{2,1,0:T(2,128)(2,1)S(1)} all-gather(bf16[1,1,12]{2,1,0:T(2,128)(2,1)S(1)} %bitcast.818), channel_id=1, replica_groups=mesh['section'=2,'head'=4,'seq'=16] {'seq'}, dimensions={0}, use_global_device_ids=true | all-gather | bytes 408 | tf_op jit(solution)/shard_map/all_gather | solution.py:22
  467.2 16.0 all-gather.23.cloned.1.call-done
  485.8 6.1 fusion.175
  497.2 11.1 all-reduce.7
  517.3 56.3 %all-gather.9 = bf16[16,1,12]{2,1,0:T(2,128)(2,1)S(1)} all-gather(bf16[1,1,12]{2,1,0:T(2,128)(2,1)S(1)} %bitcast.819), channel_id=1, replica_groups=mesh['section'=2,'head'=4,'seq'=16] {'seq'}, dimensions={0}, use_global_device_ids=true | all-gather | bytes 408 | tf_op jit(solution)/shard_map/all_gather | solution.py:44
  581.1 19.0 %all-gather.25.cloned.1.call-done = bf16[192,64,128]{2,1,0:T(8,128)(2,1)} async-done(((bf16[12,64,128]{2,1,0:T(8,128)(2,1)}), bf16[192,64,128]{2,1,0:T(8,128)(2,1)}) %all-gather.25.cloned.1.call-update) | async-done | bytes 3145744 | tf_op jit(solution)/shard_map/all_gather | solution.py:44
  600.9 38.3 %while.81 = (s32[]{:T(128)}, f32[12,64,128]{2,1,0:T(8,128)}, s32[]{:T(128)}, bf16[16,12]{1,0:T(8,128)(2,1)}, bf16[16,12,64,128]{3,2,1,0:T(8,128)(2,1)}, /*index=5*/s32[]{:T(128)}, s32[]{:T(128)}, s32[]{:T(128)}, s32[]{:T(128)}) while((s32[]{:T(128)}, f32[12,64,128]{2,1,0:T(8,128)}, s32[]{:T(128)}, bf16[16,12]{1,0:T(8,128)(2,1)}, ...), condition=%wide.region_29.30_spmd, body=%wide.region_28.29_spmd.sunk | while | flops 294930 | bytes 983307 | solution.py:61
  654.9 7.0 fusion.63
  711.3 37.8 %all-reduce.25.cloned.1.call-done = bf16[256,1536]{1,0:T(8,128)(2,1)} async-done(((bf16[256,1536]{1,0:T(8,128)(2,1)}), bf16[256,1536]{1,0:T(8,128)(2,1)}) %all-reduce.25.cloned.1.call-update) | async-done | bytes 786448 | tf_op jit(solution)/shard_map/psum | solution.py:276
  764.1 10.4 psum.169
  783.3 20.8 %all-gather.10 = bf16[16,1,12]{2,1,0:T(2,128)(2,1)S(1)} all-gather(bf16[1,1,12]{2,1,0:T(2,128)(2,1)S(1)} %bitcast.820), channel_id=1, replica_groups=mesh['section'=2,'head'=4,'seq'=16] {'seq'}, dimensions={0}, use_global_device_ids=true | all-gather | bytes 408 | tf_op jit(solution)/shard_map/all_gather | solution.py:44
  806.7 23.7 %all-gather.27.cloned.1.call-done = bf16[192,64,128]{2,1,0:T(8,128)(2,1)} async-done(((bf16[12,64,128]{2,1,0:T(8,128)(2,1)}), bf16[192,64,128]{2,1,0:T(8,128)(2,1)}) %all-gather.27.cloned.1.call-update) | async-done | bytes 3145744 | tf_op jit(solution)/shard_map/all_gather | solution.py:44
  831.2 38.8 %while.82 = (s32[]{:T(128)}, f32[12,64,128]{2,1,0:T(8,128)}, s32[]{:T(128)}, bf16[16,12]{1,0:T(8,128)(2,1)}, bf16[16,12,64,128]{3,2,1,0:T(8,128)(2,1)}, /*index=5*/s32[]{:T(128)}, s32[]{:T(128)}, s32[]{:T(128)}, s32[]{:T(128)}) while((s32[]{:T(128)}, f32[12,64,128]{2,1,0:T(8,128)}, s32[]{:T(128)}, bf16[16,12]{1,0:T(8,128)(2,1)}, ...), condition=%wide.region_46.47_spmd, body=%wide.region_45.46_spmd.sunk | while | flops 294930 | bytes 983307 | solution.py:61
  879.6 7.0 fusion.65
  918.0 4.7 collective-permute-done.11
  930.1 42.2 %all-reduce.27.cloned.1.call-done = bf16[256,1536]{1,0:T(8,128)(2,1)} async-done(((bf16[256,1536]{1,0:T(8,128)(2,1)}), bf16[256,1536]{1,0:T(8,128)(2,1)}) %all-reduce.27.cloned.1.call-update) | async-done | bytes 786448 | tf_op jit(solution)/shard_map/psum | solution.py:276
  983.8 4.3 multiply_reduce_fusion.6
  988.1 9.7 psum.171
  997.8 6.1 multiply_reduce_fusion.10
  1013.3 20.7 %all-gather.11 = bf16[16,1,12]{2,1,0:T(2,128)(2,1)S(1)} all-gather(bf16[1,1,12]{2,1,0:T(2,128)(2,1)S(1)} %bitcast.821), channel_id=1, replica_groups=mesh['section'=2,'head'=4,'seq'=16] {'seq'}, dimensions={0}, use_global_device_ids=true | all-gather | bytes 408 | tf_op jit(solution)/shard_map/all_gather | solution.py:44
  1035.8 20.5 %all-gather.29.cloned.1.call-done = bf16[192,64,128]{2,1,0:T(8,128)(2,1)} async-done(((bf16[12,64,128]{2,1,0:T(8,128)(2,1)}), bf16[192,64,128]{2,1,0:T(8,128)(2,1)}) %all-gather.29.cloned.1.call-update) | async-done | bytes 3145744 | tf_op jit(solution)/shard_map/all_gather | solution.py:44
  1057.1 39.2 %while.83 = (s32[]{:T(128)}, f32[12,64,128]{2,1,0:T(8,128)}, s32[]{:T(128)}, bf16[16,12]{1,0:T(8,128)(2,1)}, bf16[16,12,64,128]{3,2,1,0:T(8,128)(2,1)}, /*index=5*/s32[]{:T(128)}, s32[]{:T(128)}, s32[]{:T(128)}, s32[]{:T(128)}) while((s32[]{:T(128)}, f32[12,64,128]{2,1,0:T(8,128)}, s32[]{:T(128)}, bf16[16,12]{1,0:T(8,128)(2,1)}, ...), condition=%wide.region_63.64_spmd, body=%wide.region_62.63_spmd.sunk | while | flops 294930 | bytes 983307 | solution.py:61
  1105.9 7.0 fusion.67
  1130.1 4.7 fusion.184
  1158.5 6.6 fusion.290
  1167.3 9.5 convolution_add_fusion.1
  1177.8 5.0 fusion.34
  1182.8 17.9 %all-reduce.29.cloned.1.call-done = bf16[256,1536]{1,0:T(8,128)(2,1)} async-done(((bf16[256,1536]{1,0:T(8,128)(2,1)}), bf16[256,1536]{1,0:T(8,128)(2,1)}) %all-reduce.29.cloned.1.call-update) | async-done | bytes 786448 | tf_op jit(solution)/shard_map/psum | solution.py:276
  1202.9 52.1 %all-reduce.23.cloned.1.call-done = f32[256,1536]{1,0:T(8,128)} async-done(((f32[256,1536]{1,0:T(8,128)}), f32[256,1536]{1,0:T(8,128)}) %all-reduce.23.cloned.1.call-update) | async-done | bytes 1572880 | tf_op jit(solution)/shard_map/psum | solution.py:157
  1255.0 4.9 broadcast_select_fusion
  1259.9 7.6 fusion
  1267.5 12.4 copy.263
  1293.4 75.9 %all-reduce.8 = (bf16[1,1536,12]{1,2,0:T(8,128)(2,1)S(1)}, bf16[1,12]{1,0:T(2,128)(2,1)S(1)}, bf16[1,12]{1,0:T(2,128)(2,1)S(1)}, bf16[1,12]{1,0:T(2,128)(2,1)S(1...) all-reduce(bf16[1,1536,12]{1,2,0:T(8,128)(2,1)S(1)} %fusion.52, ...), channel_id=1, replica_groups=mesh['section'=2,'head'=4,'seq'=16] {'seq'}, use_global_device_ids=true, to_apply=%region_81.82 | all-reduce | flops 22308 | bytes 89232 | tf_op jit(solution)/shard_map/psum | solution.py:368
  1372.8 342.9 %all-reduce.6 = (f32[1,1536]{1,0:T(1,128)}, f32[1,4,256]{2,1,0:T(4,128)}) all-reduce(f32[1,1536]{1,0:T(1,128)S(1)} %broadcast_in_dim.213, f32[1,4,256]{2,1,0:T(4,128)S(1)} %fusion.467), channel_id=1, replica_groups=mesh['section'=2,'head'=4,'seq'=16] {'head','seq'}, use_global_device_ids=true, to_apply=%region_78.79 | all-reduce | flops 2560 | bytes 20480 | tf_op jit(solution)/shard_map/psum | solution.py:376
  1719.5 7.3 broadcast_in_dim.215
  (1074 shorter events, 526.4 us)
Async XLA Ops:
  7.2 103.7 %copy-start = (bf16[1,768,1536]{2,1,0:T(8,128)(2,1)S(1)}, bf16[1,768,1536]{2,1,0:T(8,128)(2,1)}, u32[]{:S(2)}) copy-start(bf16[1,768,1536]{2,1,0:T(8,128)(2,1)} %param.36) | copy-start | bytes 7077892
  7.2 77.9 %all-gather.19.cloned.1.call-start = ((), (), s32[]{:S(2)}) async-start(), calls=%async_computation.7 | async-start | bytes 3342336 | tf_op jit(solution)/shard_map/all_gather | solution.py:22
  14.4 388.0 %copy-start.116 = (f32[1536]{0:T(1024)}, f32[1536]{0:T(1024)S(1)}, u32[]{:S(2)}) copy-start(f32[1536]{0:T(1024)S(1)} %reduce.10) | copy-start | bytes 18436
  18.6 13.3 collective-permute-start
  23.2 7.7 collective-permute-start.1
  29.6 399.5 %copy-start.122 = (f32[768]{0:T(1024)}, f32[768]{0:T(1024)S(1)}, u32[]{:S(2)}) copy-start(f32[768]{0:T(1024)S(1)} %get-tuple-element.506) | copy-start | bytes 9220
  29.7 399.5 %copy-start.126 = (f32[768]{0:T(1024)}, f32[768]{0:T(1024)S(1)}, u32[]{:S(2)}) copy-start(f32[768]{0:T(1024)S(1)} %get-tuple-element.507) | copy-start | bytes 9220
  35.0 51.8 %copy-start.31 = (f32[256,768]{0,1:T(8,128)}, f32[256,768]{0,1:T(8,128)S(1)}, u32[]{:S(2)}) copy-start(f32[256,768]{0,1:T(8,128)S(1)} %copy.209) | copy-start | bytes 2359300
  36.5 149.9 %all-reduce.19.cloned.1.call-start = ((), (), s32[]{:S(2)}) async-start(), calls=%async_computation | async-start | bytes 3145728 | tf_op jit(solution)/shard_map/psum | solution.py:157
  112.9 161.7 %all-gather.21.cloned.1.call-start = ((), (), s32[]{:S(2)}) async-start(), calls=%async_computation.8 | async-start | bytes 3342336 | tf_op jit(solution)/shard_map/all_gather | solution.py:22
  188.3 3.6 collective-permute-start.2
  199.7 19.3 %collective-permute-start.4 = (f32[3,256]{1,0:T(4,128)}, f32[3,256]{1,0:T(4,128)}, u32[]{:S(2)}, u32[]{:S(2)}) collective-permute-start(f32[3,256]{1,0:T(4,128)} %slice.577), channel_id=1, source_target_pairs={{0,1},{1,2},{2,3},{3,4},{4,5},{5,6},{6,7},{7,8},{8,9},{9,10},{10,1... | collective-permute-start | bytes 9224 | tf_op jit(solution)/shard_map/ppermute | solution.py:16
  213.4 7.3 collective-permute-start.3
  227.4 165.9 %all-reduce.21.cloned.1.call-start = ((), (), s32[]{:S(2)}) async-start(), calls=%async_computation.1 | async-start | bytes 3145728 | tf_op jit(solution)/shard_map/psum | solution.py:157
  307.9 175.2 %all-gather.23.cloned.1.call-start = ((), (), s32[]{:S(2)}) async-start(), calls=%async_computation.9 | async-start | bytes 3342336 | tf_op jit(solution)/shard_map/all_gather | solution.py:22
  396.3 3.4 collective-permute-start.5
  408.0 19.3 %collective-permute-start.7 = (f32[3,256]{1,0:T(4,128)}, f32[3,256]{1,0:T(4,128)}, u32[]{:S(2)}, u32[]{:S(2)}) collective-permute-start(f32[3,256]{1,0:T(4,128)} %slice.597), channel_id=1, source_target_pairs={{0,1},{1,2},{2,3},{3,4},{4,5},{5,6},{6,7},{7,8},{8,9},{9,10},{10,1... | collective-permute-start | bytes 9224 | tf_op jit(solution)/shard_map/ppermute | solution.py:16
  421.8 7.4 collective-permute-start.6
  435.8 164.3 %all-gather.25.cloned.1.call-start = ((), (), s32[]{:S(2)}) async-start(), calls=%async_computation.10 | async-start | bytes 3342336 | tf_op jit(solution)/shard_map/all_gather | solution.py:44
  517.0 232.1 %all-reduce.25.cloned.1.call-start = ((), (), s32[]{:S(2)}) async-start(), calls=%async_computation.3 | async-start | bytes 1572864 | tf_op jit(solution)/shard_map/psum | solution.py:276
  517.1 61.3 %copy-start.42 = (f32[256,768]{1,0:T(8,128)S(1)}, f32[256,768]{1,0:T(8,128)}, u32[]{:S(2)}) copy-start(f32[256,768]{1,0:T(8,128)} %copy-done.41) | copy-start | bytes 2359300
  517.1 61.3 %copy-start.44 = (f32[256,768]{1,0:T(8,128)S(1)}, f32[256,768]{1,0:T(8,128)}, u32[]{:S(2)}) copy-start(f32[256,768]{1,0:T(8,128)} %copy-done.43) | copy-start | bytes 2359300
  517.1 61.3 %copy-start.202 = (f32[3,768]{1,0:T(4,128)S(1)}, f32[3,768]{1,0:T(4,128)}, u32[]{:S(2)}) copy-start(f32[3,768]{1,0:T(4,128)} %copy-done.201) | copy-start | bytes 27652
  517.1 61.3 %copy-start.204 = (f32[3,768]{1,0:T(4,128)S(1)}, f32[3,768]{1,0:T(4,128)}, u32[]{:S(2)}) copy-start(f32[3,768]{1,0:T(4,128)} %copy-done.203) | copy-start | bytes 27652
  517.1 61.3 %copy-start.206 = (f32[3,768]{1,0:T(4,128)S(1)}, f32[3,768]{1,0:T(4,128)}, u32[]{:S(2)}) copy-start(f32[3,768]{1,0:T(4,128)} %copy-done.205) | copy-start | bytes 27652
  681.8 12.7 collective-permute-start.9
  693.1 6.3 collective-permute-start.8
  706.8 123.6 %all-gather.27.cloned.1.call-start = ((), (), s32[]{:S(2)}) async-start(), calls=%async_computation.11 | async-start | bytes 3342336 | tf_op jit(solution)/shard_map/all_gather | solution.py:44
  754.8 4.5 collective-permute-start.10
  783.1 189.2 %all-reduce.27.cloned.1.call-start = ((), (), s32[]{:S(2)}) async-start(), calls=%async_computation.4 | async-start | bytes 1572864 | tf_op jit(solution)/shard_map/psum | solution.py:276
  905.0 12.7 collective-permute-start.12
  916.4 6.3 collective-permute-start.11
  930.0 45.4 %copy-start.281 = (f32[256]{0:T(256)S(1)}, f32[256]{0:T(256)}, u32[]{:S(2)}) copy-start(f32[256]{0:T(256)} %copy-done.280) | copy-start | bytes 3076
  930.0 45.4 %copy-start.283 = (f32[256]{0:T(256)S(1)}, f32[256]{0:T(256)}, u32[]{:S(2)}) copy-start(f32[256]{0:T(256)} %get-tuple-element.716) | copy-start | bytes 3076
  930.0 126.2 %all-gather.29.cloned.1.call-start = ((), (), s32[]{:S(2)}) async-start(), calls=%async_computation.12 | async-start | bytes 3342336 | tf_op jit(solution)/shard_map/all_gather | solution.py:44
  979.3 4.5 collective-permute-start.13
  1008.9 191.9 %all-reduce.29.cloned.1.call-start = ((), (), s32[]{:S(2)}) async-start(), calls=%async_computation.5 | async-start | bytes 1572864 | tf_op jit(solution)/shard_map/psum | solution.py:276
  1142.2 5.5 collective-permute-start.15
  1144.8 6.3 collective-permute-start.14
  1158.5 96.5 %all-reduce.23.cloned.1.call-start = ((), (), s32[]{:S(2)}) async-start(), calls=%async_computation.2 | async-start | bytes 3145728 | tf_op jit(solution)/shard_map/psum | solution.py:157
  1167.1 552.4 %all-reduce.33.cloned.1.call-start = ((), (), s32[]{:S(2)}) async-start(), calls=%async_computation.13 | async-start | bytes 14155776 | tf_op jit(solution)/shard_map/psum | solution.py:367
  1182.8 72.1 %copy-start.247 = (f32[256]{0:T(256)S(1)}, f32[256]{0:T(256)}, u32[]{:S(2)}) copy-start(f32[256]{0:T(256)} %copy-done.245) | copy-start | bytes 3076
  1182.8 72.1 %copy-start.248 = (f32[256]{0:T(256)S(1)}, f32[256]{0:T(256)}, u32[]{:S(2)}) copy-start(f32[256]{0:T(256)} %get-tuple-element.598) | copy-start | bytes 3076
  1182.8 72.1 %copy-start.251 = (f32[256]{0:T(256)S(1)}, f32[256]{0:T(256)}, u32[]{:S(2)}) copy-start(f32[256]{0:T(256)} %copy-done.249) | copy-start | bytes 3076
  1182.8 72.1 %copy-start.282 = (f32[256]{0:T(256)S(1)}, f32[256]{0:T(256)}, u32[]{:S(2)}) copy-start(f32[256]{0:T(256)} %get-tuple-element.597) | copy-start | bytes 3076
  1280.0 449.6 %all-reduce.31.cloned.1.call-start = ((), (), s32[]{:S(2)}) async-start(), calls=%async_computation.6 | async-start | bytes 3145728 | tf_op jit(solution)/shard_map/psum | solution.py:376
  1291.6 81.1 %copy-start.207 = (f32[1536]{0:T(1024)S(1)}, f32[1536]{0:T(1024)}, u32[]{:S(2)}) copy-start(f32[1536]{0:T(1024)} %get-tuple-element.467) | copy-start | bytes 18436
  1291.6 81.1 %copy-start.208 = (f32[1536]{0:T(1024)S(1)}, f32[1536]{0:T(1024)}, u32[]{:S(2)}) copy-start(f32[1536]{0:T(1024)} %get-tuple-element.469) | copy-start | bytes 18436
  (283 other events, 1799.0 us)
Sparse Core Ops, SparseCore 0:
  36.6 48.3 all-gather.18
  113.0 73.3 all-reduce.18
  227.5 47.0 all-gather.20
  308.0 85.2 all-reduce.20
  435.9 47.1 all-gather.22
  517.1 82.9 all-gather.24
  706.9 42.1 all-reduce.24
  783.2 47.1 all-gather.26
  930.1 42.0 all-reduce.26
  1009.0 47.1 all-gather.28
  1158.6 42.1 all-reduce.28
  1203.6 51.3 all-reduce.22
  1280.1 130.9 all-reduce.32
  1417.0 131.8 all-reduce.30
where the time goes:
time: 1750 us; the launch traced here: 1740 us
  blocking collectives  631 us (36%)
  waiting for transfers between devices  455 us (26%)
  other arithmetic  281 us (16%)
  matrix products  208 us (12%)
  local copies, waits for them, and re-layouts  109 us (6%)
  starting transfers between devices  37.4 us (2%)
  between operations  17.9 us (1%)
    psum x1, blocking collectives, on_device(): shared = lax.psum((g_bc, g_conv_bc, g_norm), ('head', 'seq'))  343 us
    psum x3, waiting for transfers between devices, mixer_forward(): result = (x_rows + lax.psum(partial_out, 'head')).astype(jnp.bfloat16)  211 us
    psum x3, waiting for transfers between devices, mixer_backward(): lax.psum(d_normed.astype(jnp.bfloat16), 'head').astype(jnp.float32)  97.9 us
    all_gather x3, blocking collectives, entering_2(): lax.all_gather(a.astype(kind), axis)  97.8 us
    add x45, other arithmetic, chain_join(): later[0][:, None, None] * earlier[1] + later[1]  85.8 us
    psum x1, blocking collectives, on_device(): lax.psum(g_dt.astype(jnp.bfloat16), 'seq').astype(jnp.float32)  75.9 us
    all_gather x3, waiting for transfers between devices, prefix(): lax.all_gather(a.astype(kind), axis)  64.4 us
    all_gather x3, waiting for transfers between devices, entering_2(): lax.all_gather(a.astype(kind), axis)  63.2 us
  transfers between devices with their start and end apart: 30, of which 19 were waited for; matrix products, arithmetic and copies ran while one was open for 9% of the time, Pallas kernels for 0%

commit v1 on v0

v1 whole, which is shorter than its diff:
```python
import functools

import jax
import jax.numpy as jnp
from jax import lax
from jax.experimental import pallas as pl
from jax.experimental.pallas import tpu as pltpu
from jax.sharding import PartitionSpec as P

MESH = pl.DeviceIdType.MESH
F32 = jnp.float32
BF = jnp.bfloat16
EPS = 1e-05
INNER = 3072
ROWS = 256
WIDTH = 1536
INNER_DEV = 768
HEADS_DEV = 12
HEAD_DIM = 64
STATE = 128
RIM = 16
VMEM_CAP = 60 << 20
FIRST = (((0,), (0,)), ((), ()))
LAST = (((1,), (1,)), ((), ()))


def dot(a, b):
    return jnp.dot(a, b, preferred_element_type=F32)


def dot_first(a, b):
    return lax.dot_general(a, b, FIRST, preferred_element_type=F32)


def dot_last(a, b):
    return lax.dot_general(a, b, LAST, preferred_element_type=F32)


def two_part(a):
    high = a.astype(BF)
    return high, (a - high.astype(F32)).astype(BF)


def silu(a):
    return a * jax.nn.sigmoid(a)


def silu_slope(a):
    sigma = jax.nn.sigmoid(a)
    return sigma * (1.0 + a * (1.0 - sigma))


def spread(a):
    rows = a.shape[0]
    low_half = lax.broadcasted_iota(jnp.int32, (rows, 128), 1) < HEAD_DIM
    return jnp.concatenate(
        [
            jnp.where(low_half, a[:, 2 * j : 2 * j + 1], a[:, 2 * j + 1 : 2 * j + 2])
            for j in range(HEADS_DEV // 2)
        ],
        axis=1,
    )


def triangle(keep_after):
    t = lax.broadcasted_iota(jnp.int32, (ROWS, ROWS), 0)
    s = lax.broadcasted_iota(jnp.int32, (ROWS, ROWS), 1)
    return jnp.where((s >= t) if keep_after else (t >= s), 1.0, 0.0).astype(BF)


def running(a, keep_after):
    weights = triangle(keep_after)
    high, low = two_part(a)
    return dot(weights, high) + dot(weights, low)


S_NORM, S_GATE, S_CONV, S_BIAS, S_RATE, S_SKIP = 0, 1, 2, 6, 7, 9
STEP = 32
BLOCKS = ROWS // STEP


def softplus(a):
    return jnp.maximum(a, 0.0) + jnp.log1p(jnp.exp(-jnp.abs(a)))


def rows_at(i, more=0):
    return pl.ds(pl.multiple_of(i * STEP, STEP), STEP + more)


def tile_at(i, width=256, base=0):
    return pl.ds(pl.multiple_of(base + i * width, width), width)


def conv_rows(pre, taps):
    total = taps[0:1] * pre[RIM - 3 : RIM - 3 + STEP]
    for k in range(1, 4):
        total = total + taps[k : k + 1] * pre[RIM - 3 + k : RIM - 3 + k + STEP]
    return total


def shifted(place, distance, count):
    return lax.rem(place + distance + count, count)


def meet(targets):
    barrier = pltpu.get_barrier_semaphore()
    for target in targets:
        pl.semaphore_signal(barrier, inc=1, device_id=target, device_id_type=MESH)
    pl.semaphore_wait(barrier, len(targets))


def send(src, dst, send_sem, recv_sem, target):
    copy = pltpu.make_async_remote_copy(
        src_ref=src,
        dst_ref=dst,
        send_sem=send_sem,
        recv_sem=recv_sem,
        device_id=target,
        device_id_type=MESH,
    )
    copy.start()
    return copy


def comm_params(number):
    return pltpu.CompilerParams(
        collective_id=number, has_side_effects=True, vmem_limit_bytes=VMEM_CAP
    )


ANY = pl.BlockSpec(memory_space=pl.ANY)
VM = pl.BlockSpec(memory_space=pltpu.VMEM)


def quarter(place):
    return pl.ds(pl.multiple_of(place * 384, 384), 384)


KEPT = (
    ("normed", (ROWS + RIM, WIDTH), BF),
    ("z", (ROWS, INNER_DEV), F32),
    ("x_pre", (ROWS + RIM, INNER_DEV), F32),
    ("bc_pre", (ROWS + RIM, 256), F32),
    ("dt_pre", (ROWS, 128), F32),
    ("la", (ROWS, 128), F32),
    ("la_t", (128, ROWS), F32),
    ("xd", (ROWS, INNER_DEV), BF),
    ("bc_act", (ROWS, 256), BF),
    ("x_act", (ROWS, INNER_DEV), F32),
    ("y", (ROWS, INNER_DEV), F32),
    ("decay", (8, INNER_DEV), F32),
    ("state", (STATE, INNER_DEV), BF),
    ("scale", (ROWS, 128), F32),
    ("out", (ROWS, WIDTH), BF),
    ("following", (ROWS, WIDTH), BF),
)


def chain_load(own, decay, out_buf):
    for j in range(16):
        rows = own[8 * j : 8 * j + 8]
        out_buf[j, :, 0:384] = jnp.concatenate([rows[:, :384], rows[:, 384:]], axis=0).astype(BF)
    six = jnp.concatenate([decay[0:1, 128 * k : 128 * k + 128] for k in range(6)] * 3, axis=0)
    six = six[0:16].astype(BF)
    for j in range(16):
        out_buf[j, :, 384:512] = six


def chain_scan(forward, in_buf, back_buf):
    state = jnp.zeros((16, 384), F32)
    for step in range(16):
        i = step if forward else 15 - step
        back_buf[i] = state.astype(BF)
        part = in_buf[i].astype(F32)
        decay = jnp.concatenate(
            [
                jnp.concatenate(
                    [
                        jnp.broadcast_to(part[3 * half + k : 3 * half + k + 1, 384:512], (8, 128))
                        for k in range(3)
                    ],
                    axis=1,
                )
                for half in range(2)
            ],
            axis=0,
        )
        state = decay * state + part[:, 0:384]


def chain_unload(got_buf, state_ref):
    for j in range(8):
        first, second = got_buf[2 * j].astype(F32), got_buf[2 * j + 1].astype(F32)
        for half in range(2):
            rows = jnp.concatenate(
                [first[8 * half : 8 * half + 8], second[8 * half : 8 * half + 8]], axis=0
            )
            state_ref[16 * j : 16 * j + 16, 384 * half : 384 * half + 384] = rows.astype(BF)


def spread_send(src, dst, me, send_sem, recv_sem):
    copies = []
    for d in range(1, 16):
        to = shifted(me, d, 16)
        copies.append(send(src.at[to], dst.at[me], send_sem.at[d], recv_sem.at[d], {"seq": to}))
    dst[me] = src[me]
    return copies


def finish(copies):
    for copy in copies:
        copy.wait()


def norm_rows(v, gain):
    v = v.astype(F32)
    scale = lax.rsqrt(jnp.mean(v * v, axis=-1, keepdims=True) + EPS)
    return (v * scale * gain).astype(BF)


def forward_kernel(*refs):
    x_ref, zx_m, bd_m, out_m, small_m = refs[:5]
    kept = [{name: refs[5 + 16 * s + i] for i, (name, _, _) in enumerate(KEPT)} for s in range(2)]
    zx_t, bd_t, out_t, small_w = refs[37:41]
    v_buf, rim_buf, zx_w, bd_w, out_w = refs[41:46]
    bd_out, tail_x, scores, dt_buf, tail, low, sq, part = refs[46:54]
    chain_out, chain_in, chain_back, chain_got = refs[54:58]
    sum_in, square_out, square_in, sum_own, next_own = refs[58:63]
    w_send, w_recv, w_own, rim_send, rim_recv = refs[63:68]
    c_sems, s_sems, t_sem, v_sem = refs[68:72], refs[72:76], refs[76], refs[77]

    core, me, place = lax.axis_index("section"), lax.axis_index("seq"), lax.axis_index("head")
    other = {"section": 1 - core}
    later = shifted(me, 1, 16)
    barrier = pltpu.get_barrier_semaphore()
    targets = [other]
    targets += [{"seq": shifted(me, d, 16)} for d in range(1, 16)]
    heads = [{"head": shifted(place, d, 4)} for d in range(1, 4)]
    targets += heads
    targets += [{"head": shifted(place, d, 4), "seq": shifted(me, -1, 16)} for d in range(1, 4)]
    for target in targets:
        pl.semaphore_signal(barrier, inc=1, device_id=target, device_id_type=MESH)

    moves = [
        (bd_m, bd_w.at[core]),
        (zx_m.at[:, INNER_DEV:], zx_w.at[core, :, INNER_DEV:]),
        (zx_m.at[:, :INNER_DEV], zx_w.at[core, :, :INNER_DEV]),
        (out_m, out_w.at[core]),
    ]
    own_moves = [pltpu.make_async_copy(src, dst, w_own.at[i]) for i, (src, dst) in enumerate(moves)]
    for move in own_moves:
        move.start()
    load_v = pltpu.make_async_copy(x_ref.at[core], v_buf, v_sem)
    load_v.start()
    pl.semaphore_wait(barrier, len(targets))
    rim_copy = send(x_ref.at[core, ROWS - RIM :], rim_buf.at[0], rim_send.at[0], rim_recv.at[0], {"seq": later})
    across = [send(small_m, small_w.at[core], w_send.at[4], w_recv.at[4], other)]
    for i, (src, dst) in enumerate(moves):
        across.append(send(src, dst, w_send.at[i], w_recv.at[i], other))
    small_w[core] = small_m[...]

    def arrive(section, i):
        @pl.when(core == section)
        def _():
            own_moves[i].wait()

        @pl.when(core != section)
        def _():
            across[i + 1].wait_recv()

    load_v.wait()
    rim_copy.wait()

    @pl.when(me == 0)
    def _():
        rim_buf[0] = jnp.zeros((RIM, WIDTH), BF)

    across[0].wait_recv()
    entering = v_buf
    for s in range(2):
        k = kept[s]
        small = small_w.at[s]
        normed, z_ref, x_pre, bc_pre, la_ref, la_t_ref = (
            k["normed"], k["z"], k["x_pre"], k["bc_pre"], k["la"], k["la_t"]
        )
        xd_ref, bc_act, x_act, y_ref = k["xd"], k["bc_act"], k["x_act"], k["y"]
        gain = small[S_NORM : S_NORM + 1]
        if s:
            finish(rim_in)

            @pl.when(me == 0)
            def _():
                rim_buf[1] = jnp.zeros((RIM, WIDTH), BF)

        normed[0:RIM] = norm_rows(rim_buf[s], gain)

        @pl.loop(0, ROWS // 16)
        def _(i):
            at = pl.ds(pl.multiple_of(i * 16, 16), 16)
            normed[pl.ds(pl.multiple_of(i * 16 + RIM, 16), 16)] = norm_rows(entering[at], gain)

        arrive(s, 0)
        bd_out[...] = dot(normed[...], bd_w[s])
        bc_pre[...] = bd_out[:, : 2 * STATE]
        dt_raw = bd_out[RIM:, 2 * STATE :]
        k["dt_pre"][...] = dt_raw
        arrive(s, 1)

        @pl.loop(0, 3)
        def _(j):
            x_pre[:, tile_at(j)] = dot(normed[...], zx_w[s, :, tile_at(j, 256, INNER_DEV)])

        dt = softplus(dt_raw + small[S_BIAS : S_BIAS + 1, :128])
        dt_buf[...] = dt
        la = running(dt * small[S_RATE : S_RATE + 1, :128], False)
        la_ref[...] = la
        la_t_ref[...] = la.T
        tail[...] = jnp.exp(la[ROWS - 1 : ROWS] - la)
        decay = jnp.broadcast_to(spread(jnp.exp(la[ROWS - 8 : ROWS]))[7:8], (8, INNER_DEV))
        k["decay"][...] = decay

        @pl.loop(0, BLOCKS)
        def _(i):
            taps = small[S_CONV : S_CONV + 4]
            act = silu(conv_rows(x_pre[rows_at(i, RIM)], taps[:, :INNER_DEV]))
            x_act[rows_at(i)] = act
            xd = (act * spread(dt_buf[rows_at(i)])).astype(BF)
            xd_ref[rows_at(i)] = xd
            tail_x[rows_at(i)] = (xd.astype(F32) * spread(tail[rows_at(i)])).astype(BF)
            bc = conv_rows(bc_pre[rows_at(i, RIM)], taps[:, INNER_DEV : INNER_DEV + 256])
            bc_act[rows_at(i)] = silu(bc).astype(BF)

        b_rows, c_rows = bc_act[:, :STATE], bc_act[:, STATE:]
        chain_load(dot_first(b_rows, tail_x[...]), decay, chain_out.at[s])
        copies = spread_send(chain_out.at[s], chain_in.at[s], me, c_sems[0].at[s], c_sems[1].at[s])
        arrive(s, 2)

        @pl.loop(0, 3)
        def _(j):
            z_ref[:, tile_at(j)] = dot(normed[RIM:], zx_w[s, :, tile_at(j)])

        scores[...] = dot_last(c_rows, b_rows)

        def heads_of(half):
            span = (half + 1) * 128
            rows = slice(half * 128, span)
            t = lax.broadcasted_iota(jnp.int32, (128, span), 0) + half * 128
            causal = t >= lax.broadcasted_iota(jnp.int32, (128, span), 1)
            for pair in range(HEADS_DEV // 2):
                parts = []
                for h in (2 * pair, 2 * pair + 1):
                    gap = la_ref[rows, h : h + 1] - la_t_ref[h : h + 1, :span]
                    mixing = scores[rows, :span] * jnp.exp(jnp.where(causal, gap, -1e30))
                    cols = slice(h * HEAD_DIM, (h + 1) * HEAD_DIM)
                    parts.append(dot(mixing.astype(BF), xd_ref[:span, cols]))
                y_ref[rows, pair * 128 : pair * 128 + 128] = jnp.concatenate(parts, axis=1)

        heads_of(0)
        finish(copies)
        chain_scan(True, chain_in.at[s], chain_back.at[s])
        copies = spread_send(chain_back.at[s], chain_got.at[s], me, c_sems[2].at[s], c_sems[3].at[s])
        heads_of(1)
        finish(copies)
        chain_unload(chain_got.at[s], k["state"])

        @pl.loop(0, BLOCKS)
        def _(i):
            at = rows_at(i)
            y = y_ref[at] + spread(jnp.exp(la_ref[at])) * dot(bc_act[at, STATE:], k["state"][...])
            y_ref[at] = y
            ssd = y + small[S_SKIP : S_SKIP + 1, :INNER_DEV] * x_act[at]
            gated = ssd * silu(z_ref[at])
            sq[at] = jnp.broadcast_to(jnp.sum(gated * gated, axis=-1, keepdims=True), (STEP, 128))
            low[at] = (gated * small[S_GATE : S_GATE + 1, :INNER_DEV]).astype(BF)

        square_out[s] = sq[...].T[0:8]
        arrive(s, 3)
        if s:
            for move in store_theirs(core, (bd_w, zx_w, out_w), (bd_t, zx_t, out_t), t_sem):
                move.start()

        @pl.loop(0, 6)
        def _(j):
            part[s, :, tile_at(j)] = dot(low[...], out_w[s, :, tile_at(j)]).astype(BF)

        copies = []
        for d in range(1, 4):
            src = part.at[s, :, quarter(shifted(place, d, 4))]
            copies.append(send(src, sum_in.at[s, d], s_sems[0].at[s, d], s_sems[1].at[s, d], heads[d - 1]))
        for d in range(1, 4):
            copies.append(
                send(square_out.at[s], square_in.at[s, d], s_sems[0].at[s, d + 4], s_sems[1].at[s, d + 4], heads[d - 1])
            )
        finish(copies)
        square = square_out[s]
        for d in range(1, 4):
            square = square + square_in[s, d]
        column = lax.rsqrt(square * (1.0 / INNER) + EPS).T[:, 0:1]
        k["scale"][...] = jnp.broadcast_to(column, (ROWS, 128))

        @pl.loop(0, BLOCKS)
        def _(i):
            at = rows_at(i)
            total = part[s, at, quarter(place)].astype(F32)
            for d in range(1, 4):
                total = total + sum_in[s, d, at].astype(F32)
            total = (total * k["scale"][at][:, 0:1]).astype(BF)
            sum_own[s, at] = total
            k["out"][at, quarter(place)] = total

        copies = []
        for d in range(1, 4):
            copies.append(
                send(sum_own.at[s], k["out"].at[:, quarter(place)], s_sems[2].at[s, d], s_sems[3].at[s, d], heads[d - 1])
            )
        if s == 0:
            edge = slice(ROWS - RIM, ROWS)
            next_own[...] = (
                v_buf[edge, quarter(place)].astype(F32) + sum_own[0, edge].astype(F32)
            ).astype(BF)
            rim_in = []
            for d in range(4):
                dst = rim_buf.at[1, :, quarter(place)]
                target = {"head": shifted(place, d, 4), "seq": later}
                rim_in.append(send(next_own, dst, rim_send.at[1 + d], rim_recv.at[1 + d], target))
        finish(copies)

        @pl.loop(0, BLOCKS)
        def _(i):
            at = rows_at(i)
            k["following"][at] = (entering[at].astype(F32) + k["out"][at].astype(F32)).astype(BF)

        entering = k["following"]

    for copy in across:
        copy.wait_send()
    for move in store_theirs(core, (bd_w, zx_w, out_w), (bd_t, zx_t, out_t), t_sem):
        move.wait()


def store_theirs(core, held, dst, sem):
    return [
        pltpu.make_async_copy(held[i].at[1 - core], dst[i], sem.at[i]) for i in range(3)
    ]


def forward(x_in, zx_m, bd_m, out_m, small_m, number):
    dma = pltpu.SemaphoreType.DMA
    sds = jax.ShapeDtypeStruct
    vm = pltpu.VMEM
    got = pl.pallas_call(
        forward_kernel,
        out_shape=[sds(shape, kind) for _, shape, kind in KEPT * 2]
        + [sds(zx_m.shape, BF), sds(bd_m.shape, BF), sds(out_m.shape, BF), sds((2, 16, WIDTH), F32)],
        in_specs=[ANY] * 4 + [VM],
        out_specs=[VM] * 32 + [ANY] * 3 + [VM],
        scratch_shapes=[
            vm((ROWS, WIDTH), BF),
            vm((2, RIM, WIDTH), BF),
            vm((2, WIDTH, WIDTH), BF),
            vm((2, WIDTH, 384), BF),
            vm((2, INNER_DEV, WIDTH), BF),
            vm((ROWS + RIM, 384), F32),
            vm((ROWS, INNER_DEV), BF),
            vm((ROWS, ROWS), F32),
            vm((ROWS, 128), F32),
            vm((ROWS, 128), F32),
            vm((ROWS, INNER_DEV), BF),
            vm((ROWS, 128), F32),
            vm((2, ROWS, WIDTH), BF),
            vm((2, 16, 16, 512), BF),
            vm((2, 16, 16, 512), BF),
            vm((2, 16, 16, 384), BF),
            vm((2, 16, 16, 384), BF),
            vm((2, 4, ROWS, 384), BF),
            vm((2, 8, ROWS), F32),
            vm((2, 4, 8, ROWS), F32),
            vm((2, ROWS, 384), BF),
            vm((RIM, 384), BF),
            dma((5,)),
            dma((5,)),
            dma((4,)),
            dma((5,)),
            dma((5,)),
            dma((2, 16)),
            dma((2, 16)),
            dma((2, 16)),
            dma((2, 16)),
            dma((2, 8)),
            dma((2, 8)),
            dma((2, 4)),
            dma((2, 4)),
            dma((3,)),
            dma,
        ],
        compiler_params=comm_params(number),
        name="forward_layers",
    )(x_in, zx_m, bd_m, out_m, small_m)
    kept = [{name: got[16 * s + i] for i, (name, _, _) in enumerate(KEPT)} for s in range(2)]
    return kept, got[32:36]


ZX, OUT = 96, 48
WIDE = ZX + OUT
SUB = WIDE + 32
SLOT = ("z", "x_pre", "bc_pre", "dt_pre", "la", "la_t", "xd", "bc_act", "x_act", "y", "decay", "state", "scale", "out")
SHAPES = {name: (shape, kind) for name, shape, kind in KEPT}


def add_rows(total, more):
    return total.astype(F32) + more.astype(F32)


def backward_kernel(*refs):
    cot_ref, x_ref, last_ref = refs[:3]
    held = (refs[3:6], refs[6:9])
    small_all = refs[9]
    saved = [{name: refs[10 + 16 * s + i] for i, (name, _, _) in enumerate(KEPT)} for s in range(2)]
    grads_ref, section_ref, leaving_ref = refs[42:45]
    rest = list(refs[45:])

    def take(count):
        got = rest[:count]
        del rest[:count]
        return got

    k = dict(zip(SLOT, take(len(SLOT))))
    normed_all, v_all, d_v, g_o_buf = take(4)
    zx_w, bd_w, out_w = take(3)
    own, spare, theirs, first, mid, second, ring = take(7)
    d_y_ref, d_z_ref, d_xd, d_y_low, wide_x, wide_y = take(6)
    scores_t, d_scores_t, d_bc, terms, direct, tail_ref, dt_ref = take(7)
    ext, d_zx, d_bd, part, sum_in, d_normed_ref, sum_own = take(7)
    chain_out, chain_in, chain_back, chain_got, state_grad = take(5)
    rim_buf, taps_ref, taps_in, taps_all, norm_ref, sums_ref, small_rows, head_in = take(8)
    k_sem, n_sem, w_sem, move_sem = take(4)
    c_sems, s_sems, rim_sems, swap_sems = take(4), take(4), take(2), take(2)
    cross_sems, one_sems, two_sems, head_sems, back_sems, last_sems = (
        take(2), take(2), take(2), take(2), take(2), take(2)
    )
    theirs_free, first_free = take(2)

    core, me, place = lax.axis_index("section"), lax.axis_index("seq"), lax.axis_index("head")
    x, z = lax.div(me, 4), lax.rem(me, 4)
    a = x + core * (z - x)
    b = z + core * (x - z)

    def at_place(i, j):
        return i * (4 - 3 * core) + j * (1 + 3 * core)

    other = {"section": 1 - core}
    heads = [{"head": shifted(place, d, 4)} for d in range(1, 4)]
    near = [{"seq": at_place(a, shifted(b, d, 4))} for d in range(1, 4)]
    far = [{"seq": at_place(shifted(a, d, 4), b)} for d in range(1, 4)]
    targets = [other] + [{"seq": shifted(me, d, 16)} for d in range(1, 16)] + heads
    targets += [{"section": 1 - core, "seq": at_place(shifted(a, d, 4), b)} for d in range(1, 4)]
    barrier = pltpu.get_barrier_semaphore()
    for target in targets:
        pl.semaphore_signal(barrier, inc=1, device_id=target, device_id_type=MESH)

    def load_kept(s):
        return [
            pltpu.make_async_copy(saved[s][name], k[name], k_sem.at[i]) for i, name in enumerate(SLOT)
        ]

    def load_rows(s):
        source = x_ref.at[core] if s == 0 else saved[0]["following"]
        return [
            pltpu.make_async_copy(saved[s]["normed"], normed_all.at[s], n_sem.at[s, 0]),
            pltpu.make_async_copy(source, v_all.at[s], n_sem.at[s, 1]),
        ]

    weight_slots = (zx_w, bd_w, out_w)

    def load_weight(s, i):
        @pl.when(core == s)
        def _():
            pltpu.make_async_copy(held[0][i], weight_slots[i], w_sem.at[i]).start()

        @pl.when(core != s)
        def _():
            pltpu.make_async_copy(held[1][i], weight_slots[i], w_sem.at[i]).start()

    def wait_weight(i):
        pltpu.make_async_copy(held[0][i], weight_slots[i], w_sem.at[i]).wait()

    load_g_o = pltpu.make_async_copy(cot_ref.at[core], g_o_buf, n_sem.at[0, 2])
    load_g_o.start()
    load_weight(1, 2)
    for move in load_kept(1):
        move.start()
    load_weight(1, 0)
    load_weight(1, 1)
    for s in (1, 0):
        for move in load_rows(s):
            move.start()

    @pl.loop(0, 4)
    def _(i):
        @pl.loop(0, 4)
        def _(j):
            blank = jnp.zeros((16, INNER_DEV), BF)
            own[0, i, j, WIDE + 16 :] = blank
            own[1, i, j, WIDE + 16 :] = blank
            spare[i, j, WIDE + 16 :] = blank

    small_rows[...] = jnp.zeros_like(small_rows)
    pl.semaphore_wait(barrier, len(targets))

    def swapped(i, src, dst):
        return pltpu.make_async_remote_copy(
            src_ref=src,
            dst_ref=dst.at[core],
            send_sem=swap_sems[0].at[i],
            recv_sem=swap_sems[1].at[i],
            device_id=other,
            device_id_type=MESH,
        )

    @pl.when(core == 0)
    def _():
        swapped(0, last_ref, section_ref).start()

    @pl.when(core == 1)
    def _():
        swapped(0, saved[0]["following"], section_ref).start()

    spans = ((ZX, WIDE), (0, ZX), (WIDE, SUB))

    def cross(s, piece):
        lo, hi = spans[piece]
        return pltpu.make_async_remote_copy(
            src_ref=spare.at[:, :, lo:hi],
            dst_ref=theirs.at[:, :, lo:hi],
            send_sem=cross_sems[0].at[s, piece],
            recv_sem=cross_sems[1].at[s, piece],
            device_id=other,
            device_id_type=MESH,
        )

    def reduction(s, group):
        lo, hi = ((0, WIDE), (WIDE, SUB))[group]
        for piece in ((0, 1), (2,))[group]:
            cross(s, piece).wait_recv()

        @pl.loop(0, 4)
        def _(i):
            @pl.loop(0, 4)
            def _(j):
                own[s, i, j, lo:hi] = add_rows(own[s, i, j, lo:hi], theirs[i, j, lo:hi]).astype(BF)

        if s == 0 and group == 0:
            pl.semaphore_wait(first_free, 3)
        copies = []
        for d in range(1, 4):
            src = own.at[s, :, shifted(b, d, 4), lo:hi]
            dst = first.at[d - 1, :, lo:hi]
            copies.append(
                send(src, dst, one_sems[0].at[s, group, d], one_sems[1].at[s, group, d], near[d - 1])
            )
        yield
        finish(copies)

        @pl.loop(0, 4)
        def _(i):
            total = own[s, i, b, lo:hi].astype(F32)
            for d in range(3):
                total = total + first[d, i, lo:hi].astype(F32)
            mid[i, lo:hi] = total.astype(BF)

        copies = []
        for d in range(1, 4):
            src = mid.at[shifted(a, d, 4), lo:hi]
            dst = second.at[s, d - 1, lo:hi]
            copies.append(
                send(src, dst, two_sems[0].at[s, group, d], two_sems[1].at[s, group, d], far[d - 1])
            )
        yield
        finish(copies)
        total = mid[a, lo:hi].astype(F32)
        for d in range(3):
            total = total + second[s, d, lo:hi].astype(F32)
        ring[s, a, lo:hi] = total.astype(BF)
        if group:
            copies = []
            for d in range(1, 4):
                src = ring.at[s, a, WIDE : WIDE + 16]
                copies.append(
                    send(src, head_in.at[s, d - 1], head_sems[0].at[s, d], head_sems[1].at[s, d], heads[d - 1])
                )
            yield
            finish(copies)
            total = ring[s, a, WIDE : WIDE + 16].astype(F32)
            for d in range(3):
                total = total + head_in[s, d].astype(F32)
            ring[s, a, WIDE : WIDE + 16] = total.astype(BF)
        copies = []
        for d in range(1, 4):
            block = ring.at[s, a, lo:hi]
            copies.append(
                send(block, block, back_sems[0].at[s, group, d], back_sems[1].at[s, group, d], far[d - 1])
            )
        yield
        finish(copies)
        src = ring.at[s, :, lo:hi]

        def last(d, half, spot):
            return pltpu.make_async_remote_copy(
                src_ref=src,
                dst_ref=grads_ref.at[half, :, spot, lo:hi],
                send_sem=last_sems[0].at[s, group, d],
                recv_sem=last_sems[1].at[s, group, half, d],
                device_id={"section": s, "seq": at_place(a, shifted(b, d, 4))},
                device_id_type=MESH,
            )

        stay = pltpu.make_async_copy(src, grads_ref.at[core, :, b, lo:hi], last_sems[0].at[s, group, 0])
        for d in range(1, 4):
            last(d, core, b).start()

        @pl.when(core == s)
        def _():
            stay.start()

        @pl.when(core != s)
        def _():
            last(0, core, b).start()

        yield
        for d in range(1, 4):
            last(d, core, b).wait_send()

        @pl.when(core == s)
        def _():
            stay.wait()
            for d in range(1, 4):
                last(d, s, b).wait_recv()
            for d in range(4):
                last(d, 1 - s, b).wait_recv()

        @pl.when(core != s)
        def _():
            last(0, core, b).wait_send()

        yield

    member_rows = lax.broadcasted_iota(jnp.int32, (INNER_DEV, 128), 0)
    member_lanes = lax.broadcasted_iota(jnp.int32, (INNER_DEV, 128), 1) * HEAD_DIM
    inside = (member_rows >= member_lanes) & (member_rows < member_lanes + HEAD_DIM)
    member = jnp.where(inside, 1.0, 0.0).astype(BF)

    def sums_of(value):
        high, low = two_part(value)
        return dot(high, member) + dot(low, member)

    half_cols = [pl.ds(pl.multiple_of(h * INNER_DEV, INNER_DEV), INNER_DEV) for h in (core, 1 - core)]
    wide, loose = None, None
    load_g_o.wait()
    for s in (1, 0):
        small = small_all.at[s]
        normed, v_ref = normed_all.at[s], v_all.at[s]
        g_o_ref = g_o_buf if s else d_v.at[1]
        y_ref, z_ref, la_ref, la_t_ref = k["y"], k["z"], k["la"], k["la_t"]
        xd_ref, bc_act, x_act = k["xd"], k["bc_act"], k["x_act"]
        x_pre, bc_pre = k["x_pre"], k["bc_pre"]
        stages = (own.at[s], spare)

        sums_ref[...] = jnp.zeros_like(sums_ref)
        wait_weight(2)

        @pl.loop(0, 3)
        def _(j):
            d_xd[:, tile_at(j)] = dot_last(g_o_ref[...], out_w[tile_at(j), :])

        if s:
            load_weight(0, 2)
        finish(load_kept(s))
        if s:
            finish(load_rows(1))

        @pl.loop(0, BLOCKS)
        def _(i):
            at = rows_at(i)
            gain = small[S_GATE : S_GATE + 1, :INNER_DEV]
            scale = k["scale"][at][:, 0:1]
            act, gate, dm = x_act[at], z_ref[at], d_xd[at]
            ssd = y_ref[at] + small[S_SKIP : S_SKIP + 1, :INNER_DEV] * act
            sigma = jax.nn.sigmoid(gate)
            gate_silu = gate * sigma
            gated = ssd * gate_silu
            scaled = gated * scale
            mean = jnp.sum(g_o_ref[at].astype(F32) * k["out"][at].astype(F32), axis=-1, keepdims=True)
            mean = mean * scale * scale * (1.0 / INNER)
            wide_x[at] = (scaled * gain).astype(BF)
            d_gated = scale * gain * dm - gated * mean
            d_y = d_gated * gate_silu
            d_y_ref[at] = d_y
            d_y_low[at] = d_y.astype(BF)
            d_z_ref[at] = (d_gated * ssd * sigma * (1.0 + gate * (1.0 - sigma))).astype(BF)
            wide_y[at] = (spread(jnp.exp(la_ref[at])) * d_y).astype(BF)
            sums_ref[0:1] += jnp.sum(scaled * dm, axis=0, keepdims=True)
            sums_ref[1:2] += jnp.sum(d_y * act, axis=0, keepdims=True)

        b_rows, c_rows = bc_act[:, :STATE], bc_act[:, STATE:]
        chain_load(dot_first(c_rows, wide_y[...]), k["decay"], chain_out)
        copies = spread_send(chain_out, chain_in, me, c_sems[0].at[s], c_sems[1].at[s])

        if s == 0:
            for piece in range(3):
                cross(1, piece).wait_send()
        for stage, cols in zip(stages, half_cols):
            for j in range(2):
                got = dot_first(wide_x[:, 384 * j : 384 * j + 384], g_o_ref[:, cols]).astype(BF)
                for i in range(8):
                    sub = 8 * j + i
                    stage[sub // 4, sub % 4, ZX:WIDE] = got[OUT * i : OUT * i + OUT]
        if s == 0:
            next(loose)
            pl.semaphore_signal(theirs_free, inc=1, device_id=other, device_id_type=MESH)
            pl.semaphore_wait(theirs_free, 1)
        cross(s, 0).start()

        la = la_ref[...]
        tail_ref[...] = jnp.exp(la[ROWS - 1 : ROWS] - la)
        dt_in = k["dt_pre"][...] + small[S_BIAS : S_BIAS + 1, :128]
        dt_ref[...] = softplus(dt_in)
        scores_t[...] = dot_last(b_rows, c_rows)

        def heads_of(half):
            base = half * 128
            rows = slice(base, base + 128)
            t = lax.broadcasted_iota(jnp.int32, (128, ROWS - base), 1)
            later = t >= lax.broadcasted_iota(jnp.int32, (128, ROWS - base), 0)
            total = jnp.zeros((128, ROWS - base), F32)
            for pair in range(HEADS_DEV // 2):
                parts = []
                for h in (2 * pair, 2 * pair + 1):
                    cols = slice(h * HEAD_DIM, (h + 1) * HEAD_DIM)
                    gap = la_t_ref[h : h + 1, base:] - la_ref[rows, h : h + 1]
                    decay = jnp.exp(jnp.where(later, gap, -1e30))
                    total = total + decay * dot_last(xd_ref[rows, cols], d_y_low[base:, cols])
                    mixing = (scores_t[rows, base:] * decay).astype(BF)
                    parts.append(dot(mixing, d_y_low[base:, cols]))
                d_xd[rows, pair * 128 : pair * 128 + 128] = jnp.concatenate(parts, axis=1)
            if half:
                d_scores_t[rows, 0:128] = jnp.zeros((128, 128), BF)
            d_scores_t[rows, base:] = total.astype(BF)

        heads_of(0)
        finish(copies)
        chain_scan(False, chain_in, chain_back)
        copies = spread_send(chain_back, chain_got, me, c_sems[2].at[s], c_sems[3].at[s])
        heads_of(1)
        if s == 0:
            next(wide)
            next(loose)
            for target in near:
                pl.semaphore_signal(first_free, inc=1, device_id=target, device_id_type=MESH)
        finish(copies)
        chain_unload(chain_got, state_grad)
        norm_ref[...] = jnp.zeros_like(norm_ref)
        taps_ref[...] = jnp.zeros_like(taps_ref)

        @pl.loop(0, BLOCKS)
        def _(i):
            at = rows_at(i)
            tail = spread(tail_ref[at])
            xd = xd_ref[at].astype(F32)
            wide_x[at] = (tail * xd).astype(BF)
            state_part = tail * dot(bc_act[at, :STATE], state_grad[...])
            got = d_xd[at] + state_part
            d_xd[at] = got
            norm_ref[1:2, :INNER_DEV] += jnp.sum(xd * state_part, axis=0, keepdims=True)
            terms[at] = sums_of(d_y_low[at].astype(F32) * y_ref[at] - xd * got)
            direct[at] = sums_of(x_act[at] * got)

        d_bc[:, :STATE] = dot(d_scores_t[...], c_rows) + dot_last(wide_x[...], state_grad[...])
        d_bc[:, STATE:] = dot_first(d_scores_t[...], b_rows) + dot_last(wide_y[...], k["state"][...])
        end_wide = spread(jnp.exp(la[ROWS - 8 : ROWS]))[7:8]
        both = state_grad[...].astype(F32) * k["state"][...].astype(F32)
        tail_sum = norm_ref[1:2, :INNER_DEV] + end_wide * jnp.sum(both, axis=0, keepdims=True)
        tail_sum = sums_of(jnp.broadcast_to(tail_sum, (16, INNER_DEV)))[0:1]
        d_log = running(terms[...], True) + tail_sum
        rate = small[S_RATE : S_RATE + 1, :128]
        d_dt = direct[...] + rate * d_log
        d_dt_pre = d_dt * jax.nn.sigmoid(dt_in)
        d_bd[:, 256:] = d_dt_pre.astype(BF)
        sums_ref[2:3, :128] = jnp.sum(dt_ref[...] * d_log, axis=0, keepdims=True) * rate
        sums_ref[3:4, :128] = jnp.sum(d_dt_pre, axis=0, keepdims=True)

        @pl.loop(0, BLOCKS)
        def _(i):
            at = rows_at(i)
            taps = small[S_CONV : S_CONV + 4]
            pre = x_pre[rows_at(i, RIM)]
            d_x = spread(dt_ref[at]) * d_xd[at] + small[S_SKIP : S_SKIP + 1, :INNER_DEV] * d_y_ref[at]
            d_xc = d_x * silu_slope(conv_rows(pre, taps[:, :INNER_DEV]))
            ext[at, :INNER_DEV] = d_xc
            for t in range(4):
                moved = pre[RIM - 3 + t : RIM - 3 + t + STEP]
                taps_ref[t : t + 1, :INNER_DEV] += jnp.sum(moved * d_xc, axis=0, keepdims=True)
            pre = bc_pre[rows_at(i, RIM)]
            d_bcc = d_bc[at] * silu_slope(conv_rows(pre, taps[:, INNER_DEV : INNER_DEV + 256]))
            ext[at, INNER_DEV:] = d_bcc
            for t in range(4):
                moved = pre[RIM - 3 + t : RIM - 3 + t + STEP]
                taps_ref[t : t + 1, INNER_DEV:] += jnp.sum(moved * d_bcc, axis=0, keepdims=True)

        rim = send(
            ext.at[0:8], rim_buf, rim_sems[0].at[s], rim_sems[1].at[s], {"seq": shifted(me, -1, 16)}
        )
        if s:
            for move in load_kept(0):
                move.start()
        taps_all[...] = taps_ref[:, INNER_DEV:]

        for stage, h in zip(stages, (core, 1 - core)):

            @pl.when(h == 0)
            def _():
                @pl.loop(0, 4)
                def _(j):
                    got = dot_first(normed[RIM:, tile_at(j, 384)], d_z_ref[...]).astype(BF)
                    for i in range(4):
                        stage[j, i, 0:ZX] = got[ZX * i : ZX * i + ZX]

        rim.wait()

        @pl.when(me == 15)
        def _():
            rim_buf[...] = jnp.zeros_like(rim_buf)

        ext[ROWS : ROWS + 8] = rim_buf[...]

        @pl.loop(0, BLOCKS)
        def _(i):
            at = rows_at(i)
            taps = small[S_CONV : S_CONV + 4]
            block = ext[rows_at(i, 8)]
            d_pre = taps[0:1, : INNER_DEV + 256] * block[3 : 3 + STEP]
            for t in range(1, 4):
                d_pre = d_pre + taps[t : t + 1, : INNER_DEV + 256] * block[3 - t : 3 - t + STEP]
            d_zx[at, :INNER_DEV] = d_z_ref[at]
            d_zx[at, INNER_DEV:] = d_pre[:, :INNER_DEV].astype(BF)
            d_bd[at, :256] = d_pre[:, INNER_DEV:].astype(BF)

        if s:
            wait_weight(0)
            wait_weight(1)
        else:
            next(wide)
            next(loose)
            wait_weight(0)
            wait_weight(1)

        @pl.loop(0, 6)
        def _(j):
            got = dot_last(d_zx[...], zx_w[tile_at(j), :]) + dot_last(d_bd[...], bd_w[tile_at(j), :])
            part[:, tile_at(j)] = got.astype(BF)

        if s:
            load_weight(0, 0)
            load_weight(0, 1)
        copies = []
        for d in range(1, 4):
            src = part.at[:, quarter(shifted(place, d, 4))]
            copies.append(send(src, sum_in.at[d - 1], s_sems[0].at[s, d], s_sems[1].at[s, d], heads[d - 1]))
        for d in range(1, 4):
            copies.append(
                send(taps_all, taps_in.at[d - 1], s_sems[0].at[s, d + 4], s_sems[1].at[s, d + 4], heads[d - 1])
            )
        for stage, h in zip(stages, (core, 1 - core)):

            @pl.when(h == 1)
            def _():
                @pl.loop(0, 4)
                def _(j):
                    got = dot_first(normed[RIM:, tile_at(j, 384)], d_zx[:, INNER_DEV:]).astype(BF)
                    for i in range(4):
                        stage[j, i, 0:ZX] = got[ZX * i : ZX * i + ZX]

        cross(s, 1).start()
        for stage, cols in zip(stages, half_cols):
            got = dot_first(d_bd[...], normed[RIM:, cols])
            for i in range(16):
                stage[i // 4, i % 4, WIDE : WIDE + 16] = got[16 * i : 16 * i + 16].astype(BF)
            stage[0, 0, WIDE + 16 :] = got[256:272].astype(BF)
        if s == 0:
            next(wide)
            next(loose)
        finish(copies)
        total = taps_all[...]
        for d in range(3):
            total = total + taps_in[d]
        taps_ref[:, INNER_DEV:] = total

        @pl.loop(0, BLOCKS)
        def _(i):
            at = rows_at(i)
            total = part[at, quarter(place)].astype(F32)
            for d in range(3):
                total = total + sum_in[d, at].astype(F32)
            total = total.astype(BF)
            sum_own[at] = total
            d_normed_ref[at, quarter(place)] = total

        copies = []
        for d in range(1, 4):
            dst = d_normed_ref.at[:, quarter(place)]
            copies.append(send(sum_own, dst, s_sems[2].at[s, d], s_sems[3].at[s, d], heads[d - 1]))
        old_loose, old_wide = loose, wide
        wide = reduction(s, 0)
        next(wide)
        finish(copies)
        norm_ref[...] = jnp.zeros_like(norm_ref)

        @pl.loop(0, BLOCKS)
        def _(i):
            at = rows_at(i)
            v = v_ref[at].astype(F32)
            scale = lax.rsqrt(jnp.mean(v * v, axis=-1, keepdims=True) + EPS)
            d_normed = d_normed_ref[at].astype(F32)
            scaled = v * scale
            norm_ref[0:1] += jnp.sum(scaled * d_normed, axis=0, keepdims=True)
            weighted = d_normed * small[S_NORM : S_NORM + 1]
            mean = jnp.mean(v * weighted, axis=-1, keepdims=True) * scale * scale
            d_v[s, at] = (scale * weighted - scaled * mean + g_o_ref[at].astype(F32)).astype(BF)

        for h in range(2):
            small_rows[h, 0:1] = norm_ref[0:1, h * INNER_DEV : (h + 1) * INNER_DEV]
            small_rows[h, 1:5] = taps_ref[0:4, :INNER_DEV]
            small_rows[h, 5:9] = sums_ref[0:4]
            small_rows[h, 9:13, 0:256] = taps_ref[0:4, INNER_DEV:]
        for stage, h in zip(stages, (core, 1 - core)):
            stage[0, 1, WIDE + 16 :] = small_rows[h].astype(BF)
        cross(s, 2).start()
        loose = reduction(s, 1)

        @pl.when(core == 1 - s)
        def _():
            swapped(1, d_v.at[s], leaving_ref).start()

        @pl.when(core == s)
        def _():
            pltpu.make_async_copy(d_v.at[s], leaving_ref.at[s], move_sem.at[1]).start()

        if s:

            @pl.when(core == 0)
            def _():
                pltpu.make_async_copy(v_all.at[1], section_ref.at[0], move_sem.at[0]).start()

            finish(load_rows(0))

            @pl.when(core == 1)
            def _():
                pltpu.make_async_copy(last_ref, g_o_buf, move_sem.at[0]).start()

    @pl.when(core == 1)
    def _():
        pltpu.make_async_copy(last_ref, g_o_buf, move_sem.at[0]).wait()
        pltpu.make_async_copy(g_o_buf, section_ref.at[1], move_sem.at[0]).start()

    order = (old_loose, loose, loose, loose, loose, wide, loose, wide, wide, wide, loose, old_wide, old_loose)
    for turn in order:
        next(turn)
    for piece in range(3):
        cross(0, piece).wait_send()
    swapped(0, last_ref, section_ref).wait()
    swapped(1, d_v.at[0], leaving_ref).wait()
    pltpu.make_async_copy(d_v.at[0], leaving_ref.at[0], move_sem.at[1]).wait()
    pltpu.make_async_copy(d_v.at[0], section_ref.at[0], move_sem.at[0]).wait()


def backward(cotangent, x_in, last, held, smalls, kept, number):
    dma = pltpu.SemaphoreType.DMA
    regular = pltpu.SemaphoreType.REGULAR
    sds = jax.ShapeDtypeStruct
    vm = pltpu.VMEM
    halves = (4, 4, SUB, INNER_DEV)
    rows_low = vm((ROWS, INNER_DEV), BF)
    rows_wide = vm((ROWS, INNER_DEV), F32)
    steps = vm((ROWS, 128), F32)
    scratch = [vm(*SHAPES[name]) for name in SLOT]
    scratch += [
        vm((2, ROWS + RIM, WIDTH), BF),
        vm((2, ROWS, WIDTH), BF),
        vm((2, ROWS, WIDTH), BF),
        vm((ROWS, WIDTH), BF),
        vm((WIDTH, WIDTH), BF),
        vm((WIDTH, 384), BF),
        vm((INNER_DEV, WIDTH), BF),
        vm((2,) + halves, BF),
        vm(halves, BF),
        vm(halves, BF),
        vm((3, 4, SUB, INNER_DEV), BF),
        vm((4, SUB, INNER_DEV), BF),
        vm((2, 3, SUB, INNER_DEV), BF),
        vm((2, 4, SUB, INNER_DEV), BF),
        rows_wide, rows_low, rows_wide, rows_low, rows_low, rows_low,
        vm((ROWS, ROWS), F32),
        vm((ROWS, ROWS), BF),
        vm((ROWS, 256), F32),
        steps, steps, steps, steps,
        vm((ROWS + 8, INNER_DEV + 256), F32),
        vm((ROWS, WIDTH), BF),
        vm((ROWS, 384), BF),
        vm((ROWS, WIDTH), BF),
        vm((3, ROWS, 384), BF),
        vm((ROWS, WIDTH), BF),
        vm((ROWS, 384), BF),
        vm((16, 16, 512), BF),
        vm((16, 16, 512), BF),
        vm((16, 16, 384), BF),
        vm((16, 16, 384), BF),
        vm((STATE, INNER_DEV), BF),
        vm((8, INNER_DEV + 256), F32),
        vm((8, INNER_DEV + 256), F32),
        vm((3, 8, 256), F32),
        vm((8, 256), F32),
        vm((8, WIDTH), F32),
        vm((8, INNER_DEV), F32),
        vm((2, 16, INNER_DEV), F32),
        vm((2, 3, 16, INNER_DEV), BF),
        dma((len(SLOT),)),
        dma((2, 3)),
        dma((3,)),
        dma((2,)),
    ]
    scratch += [dma((2, 16))] * 4 + [dma((2, 8))] * 2 + [dma((2, 4))] * 2
    scratch += [dma((2,))] * 4 + [dma((2, 3))] * 2
    scratch += [dma((2, 2, 4))] * 4 + [dma((2, 4))] * 2 + [dma((2, 2, 4))] * 2
    scratch += [dma((2, 2, 4)), dma((2, 2, 2, 4)), regular, regular]
    flat = [kept[s][name] for s in range(2) for name, _, _ in KEPT]
    return pl.pallas_call(
        backward_kernel,
        out_shape=[sds((2,) + halves, BF), sds((2, ROWS, WIDTH), BF), sds((2, ROWS, WIDTH), BF)],
        in_specs=[ANY] * 9 + [VM] + [ANY] * 32,
        out_specs=[ANY] * 3,
        scratch_shapes=scratch,
        compiler_params=comm_params(number),
        name="backward_layers",
    )(cotangent, x_in, last, *held, smalls, *flat)


def widen_kernel(a_ref, zx_ref, out_ref, bc_ref, rest_ref):
    for h in range(2):
        cols = slice(h * INNER_DEV, (h + 1) * INNER_DEV)
        zx_ref[:, h, :] = a_ref[h, 0, :ZX].astype(F32)
        out_ref[:, cols] = a_ref[h, 0, ZX:WIDE].astype(F32)
        bc_ref[:, cols] = a_ref[h, 0, WIDE : WIDE + 16].astype(F32)
        rest_ref[:, cols] = a_ref[h, 0, WIDE + 16 :].astype(F32)


def widen(total):
    total = total.reshape(2, 16, SUB, INNER_DEV)
    return pl.pallas_call(
        widen_kernel,
        grid=(16,),
        out_shape=[
            jax.ShapeDtypeStruct((WIDTH, 2, INNER_DEV), F32),
            jax.ShapeDtypeStruct((INNER_DEV, WIDTH), F32),
            jax.ShapeDtypeStruct((256, WIDTH), F32),
            jax.ShapeDtypeStruct((256, WIDTH), F32),
        ],
        in_specs=[pl.BlockSpec((2, 1, SUB, INNER_DEV), lambda i: (0, i, 0, 0))],
        out_specs=[
            pl.BlockSpec((ZX, 2, INNER_DEV), lambda i: (i, 0, 0)),
            pl.BlockSpec((OUT, WIDTH), lambda i: (i, 0)),
            pl.BlockSpec((16, WIDTH), lambda i: (i, 0)),
            pl.BlockSpec((16, WIDTH), lambda i: (i, 0)),
        ],
        compiler_params=pltpu.CompilerParams(vmem_limit_bytes=VMEM_CAP),
        name="widen",
    )(total)


def pack_small(norm_gain, gate_gain, conv_x, conv_bc, dt_bias, a_log, d_skip):
    def row(a):
        return jnp.pad(a.reshape(1, -1).astype(F32), ((0, 0), (0, WIDTH - a.size)))

    taps = jnp.concatenate([conv_x, conv_bc], axis=1).astype(F32)
    rows = [
        row(norm_gain),
        row(gate_gain),
        jnp.pad(taps, ((0, 0), (0, WIDTH - taps.shape[1]))),
        row(dt_bias),
        row(-jnp.exp(a_log)),
        row(d_skip),
        row(jnp.repeat(d_skip, HEAD_DIM)),
        jnp.zeros((6, WIDTH), F32),
    ]
    return jnp.concatenate(rows, axis=0)


def on_device(
    x_in,
    norm_gain,
    w_zx,
    w_bc,
    w_dt,
    dt_bias,
    a_log,
    d_skip,
    conv_x,
    conv_bc,
    gate_gain,
    w_out,
    cotangent,
):
    small = pack_small(norm_gain[0], gate_gain[0], conv_x[0], conv_bc[0], dt_bias[0], a_log[0], d_skip[0])
    zx_m = w_zx[0].reshape(WIDTH, WIDTH)
    bd_m = jnp.concatenate([w_bc[0], w_dt[0], jnp.zeros((WIDTH, 128 - HEADS_DEV), BF)], axis=1)
    out_m = w_out[0]
    kept, (zx_t, bd_t, out_t, smalls) = forward(x_in, zx_m, bd_m, out_m, small, 0)
    held = (zx_m, bd_m, out_m, zx_t, bd_t, out_t)
    total, section_out, grads_in = backward(
        cotangent, x_in, kept[1]["following"], held, smalls, kept, 1
    )
    g_zx, g_out, g_bc, rest = widen(total)
    own = rest[16:32, :INNER_DEV]
    return (
        section_out[None],
        grads_in[None],
        rest[16:17],
        g_zx[None],
        g_bc.T[None],
        rest[0:HEADS_DEV].T[None],
        own[8:9, :HEADS_DEV],
        own[7:8, :HEADS_DEV],
        own[6].reshape(1, HEADS_DEV, HEAD_DIM).sum(axis=2),
        own[1:5][None],
        own[9:13, :256][None],
        own[5:6],
        g_out[None],
    )


def solution(mesh):
    in_specs = (
        P(None, "seq", None),
        P("section", None),
        P("section", None, None, "head"),
        P("section", None, None),
        P("section", None, "head"),
        P("section", "head"),
        P("section", "head"),
        P("section", "head"),
        P("section", None, "head"),
        P("section", None, None),
        P("section", "head"),
        P("section", "head", None),
        P(None, "seq", None),
    )
    out_specs = (
        P("section", None, "seq", None),
        P("section", None, "seq", None),
        P("section", None),
        P("section", None, None, "head"),
        P("section", None, None),
        P("section", None, "head"),
        P("section", "head"),
        P("section", "head"),
        P("section", "head"),
        P("section", None, "head"),
        P("section", None, None),
        P("section", "head"),
        P("section", "head", None),
    )
    return jax.shard_map(
        on_device, mesh=mesh, in_specs=in_specs, out_specs=out_specs, check_vma=False
    )
```

time: 1750 us -> 382 us (0.22)
  blocking collectives: 631 us -> 0 us
  waiting for transfers between devices: 455 us -> 0 us
  Pallas kernels: 0 us -> 350 us
  other arithmetic: 281 us -> 4.4 us
  matrix products: 208 us -> 0 us
  local copies, waits for them, and re-layouts: 109 us -> 26 us
  starting transfers between devices: 37.4 us -> 0 us
    psum x7 -> x0, blocking collectives: 472 us -> none  [the longest x1 343 us: on_device(): shared = lax.psum((g_bc, g_conv_bc, g_norm), ('head', 'seq'))]
    pallas_call x0 -> x3, Pallas kernels: none -> 350 us  [the longest x1 231 us: backward(): pl.pallas_call(backward_kernel, out_shape=[sds((2,) + halves, BF), sds((2...]
    psum x8 -> x0, waiting for transfers between devices: 309 us -> none  [the longest x3 211 us: mixer_forward(): result = (x_rows + lax.psum(partial_out, 'head')).astype(jnp.bfloat16)]
    dot_general x78 -> x0, matrix products: 208 us -> none  [the longest x9 51.3 us: ssd_block(): y_inner = jnp.einsum('tsh,shp->thp', mixing, x_heads, precision=HIGH)]
    all_gather x6 -> x0, blocking collectives: 158 us -> none  [the longest x3 97.8 us: entering_2(): lax.all_gather(a.astype(kind), axis)]
    all_gather x6 -> x0, waiting for transfers between devices: 128 us -> none  [the longest x3 64.4 us: prefix(): lax.all_gather(a.astype(kind), axis)]
    add x49 -> x0, other arithmetic: 86.9 us -> none  [the longest x45 85.8 us: chain_join(): later[0][:, None, None] * earlier[1] + later[1]]
    reduce_sum x28 -> x1, other arithmetic: 53.8 us -> 0.63 us  [on_device(): own[6].reshape(1, HEADS_DEV, HEAD_DIM).sum(axis=2)]
  transfers between devices with their start and end apart: 30 -> 0, of which waited for: 19 -> 0; matrix products, arithmetic and copies ran while one was open for 9% -> 0% of each run, Pallas kernels for 0% -> 0%
where the time goes in v1:
time: 382 us; the launch traced here: 381 us
  Pallas kernels  350 us (92%)
  local copies, waits for them, and re-layouts  26 us (7%)
  other arithmetic  4.4 us (1%)
    pallas_call x1, Pallas kernels, backward(): pl.pallas_call(backward_kernel, out_shape=[sds((2,) + halves, BF), sds((2...  231 us
    pallas_call x1, Pallas kernels, forward(): pl.pallas_call(forward_kernel, out_shape=[sds(shape, kind) for _, shape,...  104 us
    pallas_call x1, Pallas kernels, widen(): pl.pallas_call(widen_kernel, grid=(16,), out_shape=[jax.ShapeDtypeStruct(...  14.2 us
    unnamed x10, local copies, waits for them, and re-layouts  13.5 us

profile of v1, /device:TPU:0, one launch (start us, length us, event | category | flops | bytes accessed | tf_op | source)
XLA Modules:
  0.0 380.9 jit_solution(10250159657245906199)
XLA Ops:
  0.6 0.7 exponential_negate_fusion
  1.3 0.1 pad.35.clone
  1.4 0.7 pad.27
  2.1 0.7 pad.24
  2.7 0.7 pad.29
  3.4 0.7 broadcast_in_dim.34
  4.1 0.1 reshape_reshape.3
  4.2 0.7 fusion.3
  4.9 2.0 concatenate.11.refs_4_
  6.9 1.0 copy.26
  8.0 2.4 maximum_maximum_fusion.refs_2_.refs_4_
  10.4 5.5 %copy.29 = bf16[192,8,2,768]{3,1,2,0:T(8,128)(2,1)} copy(bf16[192,8,2,768]{3,2,1,0:T(2,128)(2,1)} %bitcast.31) | data formatting | bytes 9437184
  15.9 104.1 %forward_layers.1 = (bf16[272,1536]{1,0:T(8,128)(2,1)}, f32[256,768]{1,0:T(8,128)}, f32[272,768]{1,0:T(8,128)}, f32[272,256]{1,0:T(8,128)}, f32[256,128]{1,0:T(8...) custom-call(bf16[2,256,1536]{2,1,0:T(8,128)(2,1)} %refs_1_.1, ...), custom_call_target="tpu_custom_call" | custom-call | tf_op jit(solution)/shard_map/forward_layers/pallas_call | solution.py:451
  120.0 231.5 %backward_layers.1 = (bf16[2,4,4,176,768]{4,3,2,1,0:T(8,128)(2,1)}, bf16[2,256,1536]{2,1,0:T(8,128)(2,1)}, bf16[2,256,1536]{2,1,0:T(8,128)(2,1)}) custom-call(bf16[2,256,1536]{2,1,0:T(8,128)(2,1)} %refs_0_.3, bf16[2,256,1536]{2,1,0:T(8,128)(2,1)} %refs_1_.1, bf16[256,1536]{1,0:T(8,128)(2,1)} %get-tuple-element.56.refs_2_.refs_41_, ...), custom_call_target="tpu_custom_call" | custom-call | tf_op jit(solution)/shard_map/backward_layers/pallas_call | solution.py:1135
  351.5 14.2 %widen.1 = (f32[1536,2,768]{2,1,0:T(2,128)}, f32[768,1536]{1,0:T(8,128)}, f32[256,1536]{1,0:T(8,128)}, f32[256,1536]{1,0:T(8,128)}) custom-call(bf16[2,16,176,768]{3,2,1,0:T(8,128)(2,1)} %bitcast.30), custom_call_target="tpu_custom_call" | custom-call | tf_op jit(solution)/shard_map/widen/pallas_call | solution.py:1157
  365.7 0.0 copy-start.1
  365.7 3.1 copy.27
  368.8 1.2 fusion.5
  370.1 1.3 slice_bitcast_fusion.2
  371.4 1.4 slice.31
  372.7 1.4 fusion.4
  374.1 0.1 reshape_squeeze.7
  374.2 0.6 reduce_sum.11
  374.8 1.3 slice_bitcast_fusion.1
  376.2 0.9 slice_bitcast_fusion
  377.1 0.7 copy.28
  377.8 0.0 copy-done.1
  377.8 0.0 copy-start
  377.8 1.1 copy.32
  378.9 0.8 copy-done
  379.8 1.1 copy.33
  (4 shorter events, 0.0 us)
Async XLA Ops:
  365.7 12.1 %copy-start.1 = (bf16[2,256,1536]{2,1,0:T(8,128)(2,1)S(1)}, bf16[2,256,1536]{2,1,0:T(8,128)(2,1)}, u32[]{:S(2)}) copy-start(bf16[2,256,1536]{2,1,0:T(8,128)(2,1)} %get-tuple-element.92) | copy-start | bytes 4718596
  377.8 2.0 copy-start

commit v2 on v1

--- a/solution.py
+++ b/solution.py
@@ -219,15 +219,16 @@
 
 
 def forward_kernel(*refs):
-    x_ref, zx_m, bd_m, out_m, small_m = refs[:5]
-    kept = [{name: refs[5 + 16 * s + i] for i, (name, _, _) in enumerate(KEPT)} for s in range(2)]
-    zx_t, bd_t, out_t, small_w = refs[37:41]
-    v_buf, rim_buf, zx_w, bd_w, out_w = refs[41:46]
-    bd_out, tail_x, scores, dt_buf, tail, low, sq, part = refs[46:54]
-    chain_out, chain_in, chain_back, chain_got = refs[54:58]
-    sum_in, square_out, square_in, sum_own, next_own = refs[58:63]
-    w_send, w_recv, w_own, rim_send, rim_recv = refs[63:68]
-    c_sems, s_sems, t_sem, v_sem = refs[68:72], refs[72:76], refs[76], refs[77]
+    x_ref, zx_m, bc_m, out_m, dt_m = refs[:5]
+    norm_gain, gate_gain, conv_x, conv_bc, dt_bias, a_log, d_skip = refs[5:12]
+    kept = [{name: refs[12 + 16 * s + i] for i, (name, _, _) in enumerate(KEPT)} for s in range(2)]
+    zx_t, bc_t, out_t, small_w, dt_w = refs[44:49]
+    v_buf, rim_buf, zx_w, bc_w, out_w = refs[49:54]
+    tail_x, scores, dt_buf, tail, low, sq, part = refs[54:61]
+    chain_out, chain_in, chain_back, chain_got = refs[61:65]
+    sum_in, square_out, square_in, sum_own, next_own = refs[65:70]
+    w_send, w_recv, w_own, rim_send, rim_recv = refs[70:75]
+    c_sems, s_sems, t_sem, v_sem = refs[75:79], refs[79:83], refs[83], refs[84]
 
     core, me, place = lax.axis_index("section"), lax.axis_index("seq"), lax.axis_index("head")
     other = {"section": 1 - core}
@@ -242,7 +243,7 @@
         pl.semaphore_signal(barrier, inc=1, device_id=target, device_id_type=MESH)
 
     moves = [
-        (bd_m, bd_w.at[core]),
+        (bc_m, bc_w.at[core]),
         (zx_m.at[:, INNER_DEV:], zx_w.at[core, :, INNER_DEV:]),
         (zx_m.at[:, :INNER_DEV], zx_w.at[core, :, :INNER_DEV]),
         (out_m, out_w.at[core]),
@@ -252,12 +253,28 @@
         move.start()
     load_v = pltpu.make_async_copy(x_ref.at[core], v_buf, v_sem)
     load_v.start()
+    small_w[core] = jnp.zeros((16, WIDTH), F32)
+    small_w[core, S_NORM : S_NORM + 1] = norm_gain[...]
+    small_w[core, S_GATE : S_GATE + 1, :INNER_DEV] = gate_gain[...]
+    small_w[core, S_CONV : S_CONV + 4, :INNER_DEV] = conv_x[...].astype(F32)
+    small_w[core, S_CONV : S_CONV + 4, INNER_DEV : INNER_DEV + 256] = conv_bc[...].astype(F32)
+    small_w[core, S_BIAS : S_BIAS + 1, 0:HEADS_DEV] = dt_bias[...]
+    small_w[core, S_RATE : S_RATE + 1, 0:HEADS_DEV] = -jnp.exp(a_log[...])
+    small_w[core, 8:9, 0:HEADS_DEV] = d_skip[...]
+    skip_wide = spread(small_w[core, 8:16, 0:128])
+    small_w[core, S_SKIP : S_SKIP + 1, :INNER_DEV] = skip_wide[0:1]
+    dt_rows = jnp.concatenate([dt_m[...].astype(F32), jnp.zeros((4, WIDTH), F32)], axis=0)
+    dt_w[core, 0:16] = dt_rows.astype(BF)
+    for s in range(2):
+        dt_w[s, 16:] = jnp.zeros((112, WIDTH), BF)
     pl.semaphore_wait(barrier, len(targets))
     rim_copy = send(x_ref.at[core, ROWS - RIM :], rim_buf.at[0], rim_send.at[0], rim_recv.at[0], {"seq": later})
-    across = [send(small_m, small_w.at[core], w_send.at[4], w_recv.at[4], other)]
+    across = [
+        send(small_w.at[core], small_w.at[core], w_send.at[4], w_recv.at[4], other),
+        send(dt_w.at[core, 0:16], dt_w.at[core, 0:16], w_send.at[5], w_recv.at[5], other),
+    ]
     for i, (src, dst) in enumerate(moves):
         across.append(send(src, dst, w_send.at[i], w_recv.at[i], other))
-    small_w[core] = small_m[...]
 
     def arrive(section, i):
         @pl.when(core == section)
@@ -266,7 +283,7 @@
 
         @pl.when(core != section)
         def _():
-            across[i + 1].wait_recv()
+            across[i + 2].wait_recv()
 
     load_v.wait()
     rim_copy.wait()
@@ -276,6 +293,7 @@
         rim_buf[0] = jnp.zeros((RIM, WIDTH), BF)
 
     across[0].wait_recv()
+    across[1].wait_recv()
     entering = v_buf
     for s in range(2):
         k = kept[s]
@@ -300,9 +318,8 @@
             normed[pl.ds(pl.multiple_of(i * 16 + RIM, 16), 16)] = norm_rows(entering[at], gain)
 
         arrive(s, 0)
-        bd_out[...] = dot(normed[...], bd_w[s])
-        bc_pre[...] = bd_out[:, : 2 * STATE]
-        dt_raw = bd_out[RIM:, 2 * STATE :]
+        bc_pre[...] = dot(normed[...], bc_w[s])
+        dt_raw = dot_last(normed[RIM:], dt_w[s])
         k["dt_pre"][...] = dt_raw
         arrive(s, 1)
 
@@ -376,7 +393,7 @@
         square_out[s] = sq[...].T[0:8]
         arrive(s, 3)
         if s:
-            for move in store_theirs(core, (bd_w, zx_w, out_w), (bd_t, zx_t, out_t), t_sem):
+            for move in store_theirs(core, (bc_w, zx_w, out_w), (bc_t, zx_t, out_t), t_sem):
                 move.start()
 
         @pl.loop(0, 6)
@@ -434,7 +451,7 @@
 
     for copy in across:
         copy.wait_send()
-    for move in store_theirs(core, (bd_w, zx_w, out_w), (bd_t, zx_t, out_t), t_sem):
+    for move in store_theirs(core, (bc_w, zx_w, out_w), (bc_t, zx_t, out_t), t_sem):
         move.wait()
 
 
@@ -444,23 +461,23 @@
     ]
 
 
-def forward(x_in, zx_m, bd_m, out_m, small_m, number):
+def forward(x_in, zx_m, bc_m, out_m, dt_m, smalls, number):
     dma = pltpu.SemaphoreType.DMA
     sds = jax.ShapeDtypeStruct
     vm = pltpu.VMEM
     got = pl.pallas_call(
         forward_kernel,
         out_shape=[sds(shape, kind) for _, shape, kind in KEPT * 2]
-        + [sds(zx_m.shape, BF), sds(bd_m.shape, BF), sds(out_m.shape, BF), sds((2, 16, WIDTH), F32)],
-        in_specs=[ANY] * 4 + [VM],
-        out_specs=[VM] * 32 + [ANY] * 3 + [VM],
+        + [sds(zx_m.shape, BF), sds(bc_m.shape, BF), sds(out_m.shape, BF)]
+        + [sds((2, 16, WIDTH), F32), sds((2, 128, WIDTH), BF)],
+        in_specs=[ANY] * 4 + [VM] * 8,
+        out_specs=[VM] * 32 + [ANY] * 3 + [VM] * 2,
         scratch_shapes=[
             vm((ROWS, WIDTH), BF),
             vm((2, RIM, WIDTH), BF),
             vm((2, WIDTH, WIDTH), BF),
-            vm((2, WIDTH, 384), BF),
+            vm((2, WIDTH, 256), BF),
             vm((2, INNER_DEV, WIDTH), BF),
-            vm((ROWS + RIM, 384), F32),
             vm((ROWS, INNER_DEV), BF),
             vm((ROWS, ROWS), F32),
             vm((ROWS, 128), F32),
@@ -477,8 +494,8 @@
             vm((2, 4, 8, ROWS), F32),
             vm((2, ROWS, 384), BF),
             vm((RIM, 384), BF),
-            dma((5,)),
-            dma((5,)),
+            dma((6,)),
+            dma((6,)),
             dma((4,)),
             dma((5,)),
             dma((5,)),
@@ -495,14 +512,15 @@
         ],
         compiler_params=comm_params(number),
         name="forward_layers",
-    )(x_in, zx_m, bd_m, out_m, small_m)
+    )(x_in, zx_m, bc_m, out_m, dt_m, *smalls)
     kept = [{name: got[16 * s + i] for i, (name, _, _) in enumerate(KEPT)} for s in range(2)]
-    return kept, got[32:36]
-
-
-ZX, OUT = 96, 48
-WIDE = ZX + OUT
+    return kept, got[32:37]
+
+
+PART = 48
+EARLY, WIDE = 2 * PART, 3 * PART
 SUB = WIDE + 32
+GROUPS = ((0, EARLY), (EARLY, WIDE), (WIDE, SUB))
 SLOT = ("z", "x_pre", "bc_pre", "dt_pre", "la", "la_t", "xd", "bc_act", "x_act", "y", "decay", "state", "scale", "out")
 SHAPES = {name: (shape, kind) for name, shape, kind in KEPT}
 
@@ -514,10 +532,10 @@
 def backward_kernel(*refs):
     cot_ref, x_ref, last_ref = refs[:3]
     held = (refs[3:6], refs[6:9])
-    small_all = refs[9]
-    saved = [{name: refs[10 + 16 * s + i] for i, (name, _, _) in enumerate(KEPT)} for s in range(2)]
-    grads_ref, section_ref, leaving_ref = refs[42:45]
-    rest = list(refs[45:])
+    small_all, dt_all = refs[9:11]
+    saved = [{name: refs[11 + 16 * s + i] for i, (name, _, _) in enumerate(KEPT)} for s in range(2)]
+    grads_ref, section_ref, leaving_ref = refs[43:46]
+    rest = list(refs[46:])
 
     def take(count):
         got = rest[:count]
@@ -526,7 +544,7 @@
 
     k = dict(zip(SLOT, take(len(SLOT))))
     normed_all, v_all, d_v, g_o_buf = take(4)
-    zx_w, bd_w, out_w = take(3)
+    zx_w, bc_w, out_w = take(3)
     own, spare, theirs, first, mid, second, ring = take(7)
     d_y_ref, d_z_ref, d_xd, d_y_low, wide_x, wide_y = take(6)
     scores_t, d_scores_t, d_bc, terms, direct, tail_ref, dt_ref = take(7)
@@ -570,7 +588,7 @@
             pltpu.make_async_copy(source, v_all.at[s], n_sem.at[s, 1]),
         ]
 
-    weight_slots = (zx_w, bd_w, out_w)
+    weight_slots = (zx_w, bc_w, out_w)
 
     def load_weight(s, i):
         @pl.when(core == s)
@@ -625,10 +643,8 @@
     def _():
         swapped(0, saved[0]["following"], section_ref).start()
 
-    spans = ((ZX, WIDE), (0, ZX), (WIDE, SUB))
-
     def cross(s, piece):
-        lo, hi = spans[piece]
+        lo, hi = GROUPS[piece]
         return pltpu.make_async_remote_copy(
             src_ref=spare.at[:, :, lo:hi],
             dst_ref=theirs.at[:, :, lo:hi],
@@ -639,9 +655,8 @@
         )
 
     def reduction(s, group):
-        lo, hi = ((0, WIDE), (WIDE, SUB))[group]
-        for piece in ((0, 1), (2,))[group]:
-            cross(s, piece).wait_recv()
+        lo, hi = GROUPS[group]
+        cross(s, group).wait_recv()
 
         @pl.loop(0, 4)
         def _(i):
@@ -649,8 +664,8 @@
             def _(j):
                 own[s, i, j, lo:hi] = add_rows(own[s, i, j, lo:hi], theirs[i, j, lo:hi]).astype(BF)
 
-        if s == 0 and group == 0:
-            pl.semaphore_wait(first_free, 3)
+        if s == 0 and group < 2:
+            pl.semaphore_wait(first_free.at[group], 3)
         copies = []
         for d in range(1, 4):
             src = own.at[s, :, shifted(b, d, 4), lo:hi]
@@ -681,7 +696,7 @@
         for d in range(3):
             total = total + second[s, d, lo:hi].astype(F32)
         ring[s, a, lo:hi] = total.astype(BF)
-        if group:
+        if group == 2:
             copies = []
             for d in range(1, 4):
                 src = ring.at[s, a, WIDE : WIDE + 16]
@@ -753,8 +768,11 @@
         high, low = two_part(value)
         return dot(high, member) + dot(low, member)
 
+    half_rows = [
+        [pl.ds(pl.multiple_of(h * INNER_DEV + 384 * j, 384), 384) for j in range(2)] for h in (core, 1 - core)
+    ]
     half_cols = [pl.ds(pl.multiple_of(h * INNER_DEV, INNER_DEV), INNER_DEV) for h in (core, 1 - core)]
-    wide, loose = None, None
+    early, late, loose = None, None, None
     load_g_o.wait()
     for s in (1, 0):
         small = small_all.at[s]
@@ -808,17 +826,27 @@
         if s == 0:
             for piece in range(3):
                 cross(1, piece).wait_send()
-        for stage, cols in zip(stages, half_cols):
+        for stage, cols, rows in zip(stages, half_cols, half_rows):
             for j in range(2):
                 got = dot_first(wide_x[:, 384 * j : 384 * j + 384], g_o_ref[:, cols]).astype(BF)
                 for i in range(8):
                     sub = 8 * j + i
-                    stage[sub // 4, sub % 4, ZX:WIDE] = got[OUT * i : OUT * i + OUT]
+                    stage[sub // 4, sub % 4, 0:PART] = got[PART * i : PART * i + PART]
+            for j in range(2):
+                got = dot_first(normed[RIM:, rows[j]], d_z_ref[...]).astype(BF)
+                for i in range(8):
+                    sub = 8 * j + i
+                    stage[sub // 4, sub % 4, PART:EARLY] = got[PART * i : PART * i + PART]
         if s == 0:
             next(loose)
             pl.semaphore_signal(theirs_free, inc=1, device_id=other, device_id_type=MESH)
             pl.semaphore_wait(theirs_free, 1)
         cross(s, 0).start()
+        if s == 0:
+            next(late)
+            next(loose)
+            for target in near:
+                pl.semaphore_signal(first_free.at[1], inc=1, device_id=target, device_id_type=MESH)
 
         la = la_ref[...]
         tail_ref[...] = jnp.exp(la[ROWS - 1 : ROWS] - la)
@@ -850,12 +878,15 @@
         finish(copies)
         chain_scan(False, chain_in, chain_back)
         copies = spread_send(chain_back, chain_got, me, c_sems[2].at[s], c_sems[3].at[s])
+        if s == 0:
+            next(early)
+            old_early = early
+        early = reduction(s, 0)
+        next(early)
         heads_of(1)
         if s == 0:
-            next(wide)
+            next(late)
             next(loose)
-            for target in near:
-                pl.semaphore_signal(first_free, inc=1, device_id=target, device_id_type=MESH)
         finish(copies)
         chain_unload(chain_got, state_grad)
         norm_ref[...] = jnp.zeros_like(norm_ref)
@@ -914,16 +945,9 @@
                 move.start()
         taps_all[...] = taps_ref[:, INNER_DEV:]
 
-        for stage, h in zip(stages, (core, 1 - core)):
-
-            @pl.when(h == 0)
-            def _():
-                @pl.loop(0, 4)
-                def _(j):
-                    got = dot_first(normed[RIM:, tile_at(j, 384)], d_z_ref[...]).astype(BF)
-                    for i in range(4):
-                        stage[j, i, 0:ZX] = got[ZX * i : ZX * i + ZX]
-
+        if s == 0:
+            next(loose)
+            next(late)
         rim.wait()
 
         @pl.when(me == 15)
@@ -944,18 +968,14 @@
             d_zx[at, INNER_DEV:] = d_pre[:, :INNER_DEV].astype(BF)
             d_bd[at, :256] = d_pre[:, INNER_DEV:].astype(BF)
 
-        if s:
-            wait_weight(0)
-            wait_weight(1)
-        else:
-            next(wide)
-            next(loose)
-            wait_weight(0)
-            wait_weight(1)
+        wait_weight(0)
+        wait_weight(1)
 
         @pl.loop(0, 6)
         def _(j):
-            got = dot_last(d_zx[...], zx_w[tile_at(j), :]) + dot_last(d_bd[...], bd_w[tile_at(j), :])
+            got = dot_last(d_zx[...], zx_w[tile_at(j), :])
+            got = got + dot_last(d_bd[:, :256], bc_w[tile_at(j), :])
+            got = got + dot(d_bd[:, 256:], dt_all[s, :, tile_at(j)])
             part[:, tile_at(j)] = got.astype(BF)
 
         if s:
@@ -969,15 +989,12 @@
             copies.append(
                 send(taps_all, taps_in.at[d - 1], s_sems[0].at[s, d + 4], s_sems[1].at[s, d + 4], heads[d - 1])
             )
-        for stage, h in zip(stages, (core, 1 - core)):
-
-            @pl.when(h == 1)
-            def _():
-                @pl.loop(0, 4)
-                def _(j):
-                    got = dot_first(normed[RIM:, tile_at(j, 384)], d_zx[:, INNER_DEV:]).astype(BF)
-                    for i in range(4):
-                        stage[j, i, 0:ZX] = got[ZX * i : ZX * i + ZX]
+        for stage, rows in zip(stages, half_rows):
+            for j in range(2):
+                got = dot_first(normed[RIM:, rows[j]], d_zx[:, INNER_DEV:]).astype(BF)
+                for i in range(8):
+                    sub = 8 * j + i
+                    stage[sub // 4, sub % 4, EARLY:WIDE] = got[PART * i : PART * i + PART]
 
         cross(s, 1).start()
         for stage, cols in zip(stages, half_cols):
@@ -985,8 +1002,11 @@
             for i in range(16):
                 stage[i // 4, i % 4, WIDE : WIDE + 16] = got[16 * i : 16 * i + 16].astype(BF)
             stage[0, 0, WIDE + 16 :] = got[256:272].astype(BF)
-        if s == 0:
-            next(wide)
+        next(early)
+        if s:
+            for target in near:
+                pl.semaphore_signal(first_free.at[0], inc=1, device_id=target, device_id_type=MESH)
+        else:
             next(loose)
         finish(copies)
         total = taps_all[...]
@@ -1008,9 +1028,10 @@
         for d in range(1, 4):
             dst = d_normed_ref.at[:, quarter(place)]
             copies.append(send(sum_own, dst, s_sems[2].at[s, d], s_sems[3].at[s, d], heads[d - 1]))
-        old_loose, old_wide = loose, wide
-        wide = reduction(s, 0)
-        next(wide)
+        old_loose, old_late = loose, late
+        late = reduction(s, 1)
+        next(late)
+        next(early)
         finish(copies)
         norm_ref[...] = jnp.zeros_like(norm_ref)
 
@@ -1034,7 +1055,7 @@
         for stage, h in zip(stages, (core, 1 - core)):
             stage[0, 1, WIDE + 16 :] = small_rows[h].astype(BF)
         cross(s, 2).start()
-        loose = reduction(s, 1)
+        loose = reduction(s, 2)
 
         @pl.when(core == 1 - s)
         def _():
@@ -1061,7 +1082,8 @@
         pltpu.make_async_copy(last_ref, g_o_buf, move_sem.at[0]).wait()
         pltpu.make_async_copy(g_o_buf, section_ref.at[1], move_sem.at[0]).start()
 
-    order = (old_loose, loose, loose, loose, loose, wide, loose, wide, wide, wide, loose, old_wide, old_loose)
+    order = (early, loose, late, loose, late, loose, loose, late, loose, early, late, loose)
+    order += (old_early, old_late, old_loose)
     for turn in order:
         next(turn)
     for piece in range(3):
@@ -1072,7 +1094,7 @@
     pltpu.make_async_copy(d_v.at[0], section_ref.at[0], move_sem.at[0]).wait()
 
 
-def backward(cotangent, x_in, last, held, smalls, kept, number):
+def backward(cotangent, x_in, last, held, smalls, dt_all, kept, number):
     dma = pltpu.SemaphoreType.DMA
     regular = pltpu.SemaphoreType.REGULAR
     sds = jax.ShapeDtypeStruct
@@ -1088,7 +1110,7 @@
         vm((2, ROWS, WIDTH), BF),
         vm((ROWS, WIDTH), BF),
         vm((WIDTH, WIDTH), BF),
-        vm((WIDTH, 384), BF),
+        vm((WIDTH, 256), BF),
         vm((INNER_DEV, WIDTH), BF),
         vm((2,) + halves, BF),
         vm(halves, BF),
@@ -1129,68 +1151,82 @@
     ]
     scratch += [dma((2, 16))] * 4 + [dma((2, 8))] * 2 + [dma((2, 4))] * 2
     scratch += [dma((2,))] * 4 + [dma((2, 3))] * 2
-    scratch += [dma((2, 2, 4))] * 4 + [dma((2, 4))] * 2 + [dma((2, 2, 4))] * 2
-    scratch += [dma((2, 2, 4)), dma((2, 2, 2, 4)), regular, regular]
+    scratch += [dma((2, 3, 4))] * 4 + [dma((2, 4))] * 2 + [dma((2, 3, 4))] * 2
+    scratch += [dma((2, 3, 4)), dma((2, 3, 2, 4)), regular, regular((2,))]
     flat = [kept[s][name] for s in range(2) for name, _, _ in KEPT]
     return pl.pallas_call(
         backward_kernel,
         out_shape=[sds((2,) + halves, BF), sds((2, ROWS, WIDTH), BF), sds((2, ROWS, WIDTH), BF)],
-        in_specs=[ANY] * 9 + [VM] + [ANY] * 32,
+        in_specs=[ANY] * 9 + [VM] * 2 + [ANY] * 32,
         out_specs=[ANY] * 3,
         scratch_shapes=scratch,
         compiler_params=comm_params(number),
         name="backward_layers",
-    )(cotangent, x_in, last, *held, smalls, *flat)
-
-
-def widen_kernel(a_ref, zx_ref, out_ref, bc_ref, rest_ref):
+    )(cotangent, x_in, last, *held, smalls, dt_all, *flat)
+
+
+def widen_kernel(
+    a_ref, zx_ref, out_ref, bc_ref, dt_ref, norm_ref, bias_ref, rate_ref, skip_ref, conv_ref, conv_bc_ref, gate_ref,
+    bc_all,
+):
+    step = pl.program_id(0)
     for h in range(2):
         cols = slice(h * INNER_DEV, (h + 1) * INNER_DEV)
-        zx_ref[:, h, :] = a_ref[h, 0, :ZX].astype(F32)
-        out_ref[:, cols] = a_ref[h, 0, ZX:WIDE].astype(F32)
-        bc_ref[:, cols] = a_ref[h, 0, WIDE : WIDE + 16].astype(F32)
-        rest_ref[:, cols] = a_ref[h, 0, WIDE + 16 :].astype(F32)
+        zx_ref[h, :, 0, :] = a_ref[h, 0, PART:EARLY].astype(F32)
+        zx_ref[h, :, 1, :] = a_ref[h, 0, EARLY:WIDE].astype(F32)
+        out_ref[:, cols] = a_ref[h, 0, 0:PART].astype(F32)
+        at = pl.ds(pl.multiple_of(step * 16, 16), 16)
+        bc_all[at, cols] = a_ref[h, 0, WIDE : WIDE + 16].astype(F32)
+
+    @pl.when(step == 0)
+    def _():
+        for h in range(2):
+            cols = slice(h * INNER_DEV, (h + 1) * INNER_DEV)
+            dt_ref[:, cols] = a_ref[h, 0, WIDE + 16 :].astype(F32)[0:HEADS_DEV]
+
+    @pl.when(step == 1)
+    def _():
+        rows = a_ref[0, 0, WIDE + 16 :].astype(F32)
+        norm_ref[:, :INNER_DEV] = rows[0:1]
+        norm_ref[:, INNER_DEV:] = a_ref[1, 0, WIDE + 16 :].astype(F32)[0:1]
+        conv_ref[...] = rows[1:5]
+        gate_ref[...] = rows[5:6]
+        heads = jnp.concatenate(
+            [
+                jnp.sum(rows[0:8, h * HEAD_DIM : (h + 1) * HEAD_DIM], axis=1, keepdims=True)
+                for h in range(HEADS_DEV)
+            ],
+            axis=1,
+        )
+        skip_ref[...] = heads[6:7]
+        rate_ref[...] = rows[7:8, 0:HEADS_DEV]
+        bias_ref[...] = rows[8:9, 0:HEADS_DEV]
+        conv_bc_ref[...] = rows[9:13, 0:256]
+
+    @pl.when(step == 15)
+    def _():
+        bc_ref[...] = bc_all[...].T
 
 
 def widen(total):
     total = total.reshape(2, 16, SUB, INNER_DEV)
+    fixed = ((WIDTH, 256), (HEADS_DEV, WIDTH), (1, WIDTH)) + ((1, HEADS_DEV),) * 3
+    fixed += ((4, INNER_DEV), (4, 256), (1, INNER_DEV))
+    shapes = ((2, INNER_DEV, 2, INNER_DEV), (INNER_DEV, WIDTH)) + fixed
     return pl.pallas_call(
         widen_kernel,
         grid=(16,),
-        out_shape=[
-            jax.ShapeDtypeStruct((WIDTH, 2, INNER_DEV), F32),
-            jax.ShapeDtypeStruct((INNER_DEV, WIDTH), F32),
-            jax.ShapeDtypeStruct((256, WIDTH), F32),
-            jax.ShapeDtypeStruct((256, WIDTH), F32),
-        ],
+        out_shape=[jax.ShapeDtypeStruct(shape, F32) for shape in shapes],
         in_specs=[pl.BlockSpec((2, 1, SUB, INNER_DEV), lambda i: (0, i, 0, 0))],
         out_specs=[
-            pl.BlockSpec((ZX, 2, INNER_DEV), lambda i: (i, 0, 0)),
-            pl.BlockSpec((OUT, WIDTH), lambda i: (i, 0)),
-            pl.BlockSpec((16, WIDTH), lambda i: (i, 0)),
-            pl.BlockSpec((16, WIDTH), lambda i: (i, 0)),
-        ],
+            pl.BlockSpec((2, PART, 2, INNER_DEV), lambda i: (0, i, 0, 0)),
+            pl.BlockSpec((PART, WIDTH), lambda i: (i, 0)),
+        ]
+        + [pl.BlockSpec(shape, lambda i: (0, 0)) for shape in fixed],
+        scratch_shapes=[pltpu.VMEM((256, WIDTH), F32)],
         compiler_params=pltpu.CompilerParams(vmem_limit_bytes=VMEM_CAP),
         name="widen",
     )(total)
-
-
-def pack_small(norm_gain, gate_gain, conv_x, conv_bc, dt_bias, a_log, d_skip):
-    def row(a):
-        return jnp.pad(a.reshape(1, -1).astype(F32), ((0, 0), (0, WIDTH - a.size)))
-
-    taps = jnp.concatenate([conv_x, conv_bc], axis=1).astype(F32)
-    rows = [
-        row(norm_gain),
-        row(gate_gain),
-        jnp.pad(taps, ((0, 0), (0, WIDTH - taps.shape[1]))),
-        row(dt_bias),
-        row(-jnp.exp(a_log)),
-        row(d_skip),
-        row(jnp.repeat(d_skip, HEAD_DIM)),
-        jnp.zeros((6, WIDTH), F32),
-    ]
-    return jnp.concatenate(rows, axis=0)
 
 
 def on_device(
@@ -1208,30 +1244,28 @@
     w_out,
     cotangent,
 ):
-    small = pack_small(norm_gain[0], gate_gain[0], conv_x[0], conv_bc[0], dt_bias[0], a_log[0], d_skip[0])
     zx_m = w_zx[0].reshape(WIDTH, WIDTH)
-    bd_m = jnp.concatenate([w_bc[0], w_dt[0], jnp.zeros((WIDTH, 128 - HEADS_DEV), BF)], axis=1)
-    out_m = w_out[0]
-    kept, (zx_t, bd_t, out_t, smalls) = forward(x_in, zx_m, bd_m, out_m, small, 0)
-    held = (zx_m, bd_m, out_m, zx_t, bd_t, out_t)
+    bc_m, out_m, dt_m = w_bc[0], w_out[0], w_dt[0].T
+    small_args = (norm_gain, gate_gain, conv_x[0], conv_bc[0], dt_bias, a_log, d_skip)
+    kept, (zx_t, bc_t, out_t, smalls, dt_all) = forward(x_in, zx_m, bc_m, out_m, dt_m, small_args, 0)
+    held = (zx_m, bc_m, out_m, zx_t, bc_t, out_t)
     total, section_out, grads_in = backward(
-        cotangent, x_in, kept[1]["following"], held, smalls, kept, 1
+        cotangent, x_in, kept[1]["following"], held, smalls, dt_all, kept, 1
     )
-    g_zx, g_out, g_bc, rest = widen(total)
-    own = rest[16:32, :INNER_DEV]
+    g_zx, g_out, g_bc, g_dt, g_norm, g_bias, g_rate, g_skip, g_conv_x, g_conv_bc, g_gate = widen(total)
     return (
         section_out[None],
         grads_in[None],
-        rest[16:17],
-        g_zx[None],
-        g_bc.T[None],
-        rest[0:HEADS_DEV].T[None],
-        own[8:9, :HEADS_DEV],
-        own[7:8, :HEADS_DEV],
-        own[6].reshape(1, HEADS_DEV, HEAD_DIM).sum(axis=2),
-        own[1:5][None],
-        own[9:13, :256][None],
-        own[5:6],
+        g_norm,
+        g_zx.reshape(1, WIDTH, 2, INNER_DEV),
+        g_bc[None],
+        g_dt.T[None],
+        g_bias,
+        g_rate,
+        g_skip,
+        g_conv_x[None],
+        g_conv_bc[None],
+        g_gate,
         g_out[None],
     )
 

time: 382 us -> 313 us (0.82)
  Pallas kernels: 350 us -> 302 us
  local copies, waits for them, and re-layouts: 26 us -> 9.47 us
  other arithmetic: 4.4 us -> 0 us
    pallas_call x1, Pallas kernels: 231 us -> 184 us  [backward(): pl.pallas_call(backward_kernel, out_shape=[sds((2,) + halves, BF), sds((2...]
    broadcast_in_dim x6 -> x0, local copies, waits for them, and re-layouts: 4.26 us -> none  [the longest x1 1.34 us: on_device(): own[1:5][None]]
    slice x3 -> x0, local copies, waits for them, and re-layouts: 4.02 us -> none  [the longest x1 1.4 us: on_device(): own[5:6]]
    unnamed x10 -> x8, local copies, waits for them, and re-layouts: 13.5 us -> 9.47 us
where the time goes in v2:
time: 313 us; the launch traced here: 312 us
  Pallas kernels  302 us (96%)
  local copies, waits for them, and re-layouts  9.47 us (3%)
    pallas_call x1, Pallas kernels, backward(): pl.pallas_call(backward_kernel, out_shape=[sds((2,) + halves, BF), sds((2...  184 us
    pallas_call x1, Pallas kernels, forward(): pl.pallas_call(forward_kernel, out_shape=[sds(shape, kind) for _, shape,...  103 us
    pallas_call x1, Pallas kernels, widen(): pl.pallas_call(widen_kernel, grid=(16,), out_shape=[jax.ShapeDtypeStruct(...  15.1 us
    unnamed x8, local copies, waits for them, and re-layouts  9.47 us

profile of v2, /device:TPU:0, one launch (start us, length us, event | category | flops | bytes accessed | tf_op | source)
XLA Modules:
  0.0 312.1 jit_solution(10634330007181504297)
XLA Ops:
  0.6 5.5 %copy.27 = bf16[192,8,2,768]{3,1,2,0:T(8,128)(2,1)} copy(bf16[192,8,2,768]{3,2,1,0:T(2,128)(2,1)} %bitcast.26) | data formatting | bytes 9437184
  6.1 103.0 %forward_layers.1 = (bf16[272,1536]{1,0:T(8,128)(2,1)}, f32[256,768]{1,0:T(8,128)}, f32[272,768]{1,0:T(8,128)}, f32[272,256]{1,0:T(8,128)}, f32[256,128]{1,0:T(8...) custom-call(bf16[2,256,1536]{2,1,0:T(8,128)(2,1)} %refs_1_.1, ...), custom_call_target="tpu_custom_call" | custom-call | tf_op jit(solution)/shard_map/forward_layers/pallas_call | solution.py:468
  109.1 183.8 %backward_layers.1 = (bf16[2,4,4,176,768]{4,3,2,1,0:T(8,128)(2,1)}, bf16[2,256,1536]{2,1,0:T(8,128)(2,1)}, bf16[2,256,1536]{2,1,0:T(8,128)(2,1)}) custom-call(bf16[2,256,1536]{2,1,0:T(8,128)(2,1)} %refs_0_.3, bf16[2,256,1536]{2,1,0:T(8,128)(2,1)} %refs_1_.1, bf16[256,1536]{1,0:T(8,128)(2,1)} %get-tuple-element.64.refs_2_.refs_42_, ...), custom_call_target="tpu_custom_call" | custom-call | tf_op jit(solution)/shard_map/backward_layers/pallas_call | solution.py:1157
  293.0 0.0 copy-start.1
  293.0 15.1 %widen.1 = (f32[2,768,2,768]{3,2,1,0:T(2,128)}, f32[768,1536]{1,0:T(8,128)}, f32[1536,256]{1,0:T(8,128)}, f32[12,1536]{1,0:T(8,128)}, f32[1,1536]{1,0:T(1,128)},...) custom-call(bf16[2,16,176,768]{3,2,1,0:T(8,128)(2,1)} %bitcast.25), custom_call_target="tpu_custom_call" | custom-call | tf_op jit(solution)/shard_map/widen/pallas_call | solution.py:1216
  308.1 0.0 copy-start
  308.1 1.7 copy.26
  309.8 0.0 copy-done.1
  309.8 1.1 copy.30
  311.0 0.0 copy-done
  311.0 1.1 copy.31
Async XLA Ops:
  293.0 16.8 %copy-start.1 = (bf16[2,256,1536]{2,1,0:T(8,128)(2,1)S(1)}, bf16[2,256,1536]{2,1,0:T(8,128)(2,1)}, u32[]{:S(2)}) copy-start(bf16[2,256,1536]{2,1,0:T(8,128)(2,1)} %get-tuple-element.101) | copy-start | bytes 4718596
  308.1 2.9 copy-start

commit v3 on v2

--- a/solution.py
+++ b/solution.py
@@ -519,8 +519,9 @@
 
 PART = 48
 EARLY, WIDE = 2 * PART, 3 * PART
-SUB = WIDE + 32
-GROUPS = ((0, EARLY), (EARLY, WIDE), (WIDE, SUB))
+SUB = WIDE + 16
+GROUPS = (((0, PART), (PART, EARLY)), ((EARLY, EARLY + 32), (EARLY + 32, SUB)))
+REST = 32
 SLOT = ("z", "x_pre", "bc_pre", "dt_pre", "la", "la_t", "xd", "bc_act", "x_act", "y", "decay", "state", "scale", "out")
 SHAPES = {name: (shape, kind) for name, shape, kind in KEPT}
 
@@ -534,8 +535,8 @@
     held = (refs[3:6], refs[6:9])
     small_all, dt_all = refs[9:11]
     saved = [{name: refs[11 + 16 * s + i] for i, (name, _, _) in enumerate(KEPT)} for s in range(2)]
-    grads_ref, section_ref, leaving_ref = refs[43:46]
-    rest = list(refs[46:])
+    grads_ref, rest_ref, section_ref, leaving_ref = refs[43:47]
+    rest = list(refs[47:])
 
     def take(count):
         got = rest[:count]
@@ -550,28 +551,23 @@
     scores_t, d_scores_t, d_bc, terms, direct, tail_ref, dt_ref = take(7)
     ext, d_zx, d_bd, part, sum_in, d_normed_ref, sum_own = take(7)
     chain_out, chain_in, chain_back, chain_got, state_grad = take(5)
-    rim_buf, taps_ref, taps_in, taps_all, norm_ref, sums_ref, small_rows, head_in = take(8)
+    rim_buf, taps_ref, bc_out, bc_in, norm_ref, sums_ref, small_rows = take(7)
+    rest_out, rest_cross, rest_near, rest_far, rest_low = take(5)
     k_sem, n_sem, w_sem, move_sem = take(4)
     c_sems, s_sems, rim_sems, swap_sems = take(4), take(4), take(2), take(2)
-    cross_sems, one_sems, two_sems, head_sems, back_sems, last_sems = (
-        take(2), take(2), take(2), take(2), take(2), take(2)
-    )
+    cross_sems, one_sems, two_sems, back_sems, last_sems = take(2), take(2), take(2), take(2), take(2)
+    bc_sems, rest_sems = take(2), take(2)
     theirs_free, first_free = take(2)
 
     core, me, place = lax.axis_index("section"), lax.axis_index("seq"), lax.axis_index("head")
     x, z = lax.div(me, 4), lax.rem(me, 4)
-    a = x + core * (z - x)
-    b = z + core * (x - z)
-
-    def at_place(i, j):
-        return i * (4 - 3 * core) + j * (1 + 3 * core)
-
+    along_z = [x * 4 + shifted(z, d, 4) for d in range(1, 4)]
+    along_x = [shifted(x, d, 4) * 4 + z for d in range(1, 4)]
+    ways = ((x, z, along_z, along_x), (z, x, along_x, along_z))
     other = {"section": 1 - core}
     heads = [{"head": shifted(place, d, 4)} for d in range(1, 4)]
-    near = [{"seq": at_place(a, shifted(b, d, 4))} for d in range(1, 4)]
-    far = [{"seq": at_place(shifted(a, d, 4), b)} for d in range(1, 4)]
     targets = [other] + [{"seq": shifted(me, d, 16)} for d in range(1, 16)] + heads
-    targets += [{"section": 1 - core, "seq": at_place(shifted(a, d, 4), b)} for d in range(1, 4)]
+    targets += [{"section": 1 - core, "seq": seq} for seq in along_z + along_x]
     barrier = pltpu.get_barrier_semaphore()
     for target in targets:
         pl.semaphore_signal(barrier, inc=1, device_id=target, device_id_type=MESH)
@@ -613,15 +609,6 @@
         for move in load_rows(s):
             move.start()
 
-    @pl.loop(0, 4)
-    def _(i):
-        @pl.loop(0, 4)
-        def _(j):
-            blank = jnp.zeros((16, INNER_DEV), BF)
-            own[0, i, j, WIDE + 16 :] = blank
-            own[1, i, j, WIDE + 16 :] = blank
-            spare[i, j, WIDE + 16 :] = blank
-
     small_rows[...] = jnp.zeros_like(small_rows)
     pl.semaphore_wait(barrier, len(targets))
 
@@ -644,7 +631,7 @@
         swapped(0, saved[0]["following"], section_ref).start()
 
     def cross(s, piece):
-        lo, hi = GROUPS[piece]
+        lo, hi = GROUPS[piece][0][0], GROUPS[piece][1][1]
         return pltpu.make_async_remote_copy(
             src_ref=spare.at[:, :, lo:hi],
             dst_ref=theirs.at[:, :, lo:hi],
@@ -655,107 +642,161 @@
         )
 
     def reduction(s, group):
-        lo, hi = GROUPS[group]
+        parts = [(n, lo, hi) + ways[n] for n, (lo, hi) in enumerate(GROUPS[group])]
+        low, high = parts[0][1], parts[1][2]
         cross(s, group).wait_recv()
 
         @pl.loop(0, 4)
         def _(i):
             @pl.loop(0, 4)
             def _(j):
-                own[s, i, j, lo:hi] = add_rows(own[s, i, j, lo:hi], theirs[i, j, lo:hi]).astype(BF)
-
-        if s == 0 and group < 2:
-            pl.semaphore_wait(first_free.at[group], 3)
+                own[s, i, j, low:high] = add_rows(own[s, i, j, low:high], theirs[i, j, low:high]).astype(BF)
+
+        if s == 0:
+            pl.semaphore_wait(first_free.at[group], 6)
         copies = []
-        for d in range(1, 4):
-            src = own.at[s, :, shifted(b, d, 4), lo:hi]
-            dst = first.at[d - 1, :, lo:hi]
-            copies.append(
-                send(src, dst, one_sems[0].at[s, group, d], one_sems[1].at[s, group, d], near[d - 1])
-            )
+        for d in range(3):
+            for n, lo, hi, a, b, near, far in parts:
+                src = own.at[s, :, shifted(b, d + 1, 4), lo:hi]
+                dst = first.at[d, :, lo:hi]
+                sems = one_sems[0].at[s, group, n, d], one_sems[1].at[s, group, n, d]
+                copies.append(send(src, dst, *sems, {"seq": near[d]}))
         yield
         finish(copies)
 
         @pl.loop(0, 4)
         def _(i):
-            total = own[s, i, b, lo:hi].astype(F32)
-            for d in range(3):
-                total = total + first[d, i, lo:hi].astype(F32)
-            mid[i, lo:hi] = total.astype(BF)
+            for n, lo, hi, a, b, near, far in parts:
+                total = own[s, i, b, lo:hi].astype(F32)
+                for d in range(3):
+                    total = total + first[d, i, lo:hi].astype(F32)
+                mid[i, lo:hi] = total.astype(BF)
 
         copies = []
-        for d in range(1, 4):
-            src = mid.at[shifted(a, d, 4), lo:hi]
-            dst = second.at[s, d - 1, lo:hi]
-            copies.append(
-                send(src, dst, two_sems[0].at[s, group, d], two_sems[1].at[s, group, d], far[d - 1])
-            )
+        for d in range(3):
+            for n, lo, hi, a, b, near, far in parts:
+                src = mid.at[shifted(a, d + 1, 4), lo:hi]
+                dst = second.at[s, d, lo:hi]
+                sems = two_sems[0].at[s, group, n, d], two_sems[1].at[s, group, n, d]
+                copies.append(send(src, dst, *sems, {"seq": far[d]}))
         yield
         finish(copies)
-        total = mid[a, lo:hi].astype(F32)
-        for d in range(3):
-            total = total + second[s, d, lo:hi].astype(F32)
-        ring[s, a, lo:hi] = total.astype(BF)
-        if group == 2:
-            copies = []
-            for d in range(1, 4):
-                src = ring.at[s, a, WIDE : WIDE + 16]
-                copies.append(
-                    send(src, head_in.at[s, d - 1], head_sems[0].at[s, d], head_sems[1].at[s, d], heads[d - 1])
-                )
-            yield
-            finish(copies)
-            total = ring[s, a, WIDE : WIDE + 16].astype(F32)
+        copies = []
+        for n, lo, hi, a, b, near, far in parts:
+            total = mid[a, lo:hi].astype(F32)
             for d in range(3):
-                total = total + head_in[s, d].astype(F32)
-            ring[s, a, WIDE : WIDE + 16] = total.astype(BF)
-        copies = []
-        for d in range(1, 4):
-            block = ring.at[s, a, lo:hi]
-            copies.append(
-                send(block, block, back_sems[0].at[s, group, d], back_sems[1].at[s, group, d], far[d - 1])
-            )
+                total = total + second[s, d, lo:hi].astype(F32)
+            ring[s, a, lo:hi] = total.astype(BF)
+            for d in range(3):
+                block = ring.at[s, a, lo:hi]
+                sems = back_sems[0].at[s, group, n, d], back_sems[1].at[s, group, n, d]
+                copies.append(send(block, block, *sems, {"seq": far[d]}))
         yield
         finish(copies)
-        src = ring.at[s, :, lo:hi]
-
-        def last(d, half, spot):
+
+        def last(part, d, half):
+            n, lo, hi, a, b, near, far = part
             return pltpu.make_async_remote_copy(
-                src_ref=src,
-                dst_ref=grads_ref.at[half, :, spot, lo:hi],
-                send_sem=last_sems[0].at[s, group, d],
-                recv_sem=last_sems[1].at[s, group, half, d],
-                device_id={"section": s, "seq": at_place(a, shifted(b, d, 4))},
+                src_ref=ring.at[s, :, lo:hi],
+                dst_ref=grads_ref.at[half, :, b, lo:hi],
+                send_sem=last_sems[0].at[s, group, n, d],
+                recv_sem=last_sems[1].at[s, group, n, half, d],
+                device_id={"section": s, "seq": near[d] if d < 3 else me},
                 device_id_type=MESH,
             )
 
-        stay = pltpu.make_async_copy(src, grads_ref.at[core, :, b, lo:hi], last_sems[0].at[s, group, 0])
-        for d in range(1, 4):
-            last(d, core, b).start()
+        def stay(part):
+            n, lo, hi, a, b, near, far = part
+            sem = last_sems[0].at[s, group, n, 3]
+            return pltpu.make_async_copy(ring.at[s, :, lo:hi], grads_ref.at[core, :, b, lo:hi], sem)
+
+        for d in range(3):
+            for part in parts:
+                last(part, d, core).start()
 
         @pl.when(core == s)
         def _():
-            stay.start()
+            for part in parts:
+                stay(part).start()
 
         @pl.when(core != s)
         def _():
-            last(0, core, b).start()
+            for part in parts:
+                last(part, 3, core).start()
 
         yield
-        for d in range(1, 4):
-            last(d, core, b).wait_send()
+        for part in parts:
+            for d in range(3):
+                last(part, d, core).wait_send()
 
         @pl.when(core == s)
         def _():
-            stay.wait()
-            for d in range(1, 4):
-                last(d, s, b).wait_recv()
-            for d in range(4):
-                last(d, 1 - s, b).wait_recv()
+            for part in parts:
+                stay(part).wait()
+                for d in range(3):
+                    last(part, d, s).wait_recv()
+                for d in range(4):
+                    last(part, d, 1 - s).wait_recv()
 
         @pl.when(core != s)
         def _():
-            last(0, core, b).wait_send()
+            for part in parts:
+                last(part, 3, core).wait_send()
+
+        yield
+
+    def reduction_rest(s):
+        def move(src, dst, i, target):
+            return send(src, dst, rest_sems[0].at[s, i], rest_sems[1].at[s, i], target)
+
+        def gather(bufs, first_sem, peers):
+            return [move(rest_low.at[s], bufs.at[s, d], first_sem + d, {"seq": peers[d]}) for d in range(3)]
+
+        copy = move(rest_out.at[1 - core], rest_cross.at[s], 0, other)
+        yield
+        copy.wait()
+        total = add_rows(rest_out[core], rest_cross[s])
+        rest_low[s] = total.astype(BF)
+        copies = gather(rest_near, 1, along_z)
+        yield
+        finish(copies)
+        for d in range(3):
+            total = total + rest_near[s, d].astype(F32)
+        rest_low[s] = total.astype(BF)
+        copies = gather(rest_far, 4, along_x)
+        yield
+        finish(copies)
+        for d in range(3):
+            total = total + rest_far[s, d].astype(F32)
+        rest_low[s] = total.astype(BF)
+
+        def deliver():
+            return pltpu.make_async_remote_copy(
+                src_ref=rest_low.at[s],
+                dst_ref=rest_ref.at[core],
+                send_sem=rest_sems[0].at[s, 7],
+                recv_sem=rest_sems[1].at[s, 7],
+                device_id=other,
+                device_id_type=MESH,
+            )
+
+        @pl.when(core != s)
+        def _():
+            deliver().start()
+
+        @pl.when(core == s)
+        def _():
+            rest_ref[core] = rest_low[s]
+
+        yield
+
+        @pl.when(core != s)
+        def _():
+            deliver().wait_send()
+
+        @pl.when(core == s)
+        def _():
+            deliver().wait_recv()
 
         yield
 
@@ -773,6 +814,7 @@
     ]
     half_cols = [pl.ds(pl.multiple_of(h * INNER_DEV, INNER_DEV), INNER_DEV) for h in (core, 1 - core)]
     early, late, loose = None, None, None
+    old_early, old_late = None, None
     load_g_o.wait()
     for s in (1, 0):
         small = small_all.at[s]
@@ -824,7 +866,7 @@
         copies = spread_send(chain_out, chain_in, me, c_sems[0].at[s], c_sems[1].at[s])
 
         if s == 0:
-            for piece in range(3):
+            for piece in range(2):
                 cross(1, piece).wait_send()
         for stage, cols, rows in zip(stages, half_cols, half_rows):
             for j in range(2):
@@ -838,15 +880,13 @@
                     sub = 8 * j + i
                     stage[sub // 4, sub % 4, PART:EARLY] = got[PART * i : PART * i + PART]
         if s == 0:
-            next(loose)
-            pl.semaphore_signal(theirs_free, inc=1, device_id=other, device_id_type=MESH)
             pl.semaphore_wait(theirs_free, 1)
         cross(s, 0).start()
         if s == 0:
             next(late)
+            for seq in along_z + along_x:
+                pl.semaphore_signal(first_free.at[1], inc=1, device_id={"seq": seq}, device_id_type=MESH)
             next(loose)
-            for target in near:
-                pl.semaphore_signal(first_free.at[1], inc=1, device_id=target, device_id_type=MESH)
 
         la = la_ref[...]
         tail_ref[...] = jnp.exp(la[ROWS - 1 : ROWS] - la)
@@ -878,16 +918,13 @@
         finish(copies)
         chain_scan(False, chain_in, chain_back)
         copies = spread_send(chain_back, chain_got, me, c_sems[2].at[s], c_sems[3].at[s])
-        if s == 0:
-            next(early)
-            old_early = early
-        early = reduction(s, 0)
+        old_early, early = early, reduction(s, 0)
         next(early)
         heads_of(1)
+        finish(copies)
         if s == 0:
             next(late)
             next(loose)
-        finish(copies)
         chain_unload(chain_got, state_grad)
         norm_ref[...] = jnp.zeros_like(norm_ref)
         taps_ref[...] = jnp.zeros_like(taps_ref)
@@ -911,6 +948,18 @@
         both = state_grad[...].astype(F32) * k["state"][...].astype(F32)
         tail_sum = norm_ref[1:2, :INNER_DEV] + end_wide * jnp.sum(both, axis=0, keepdims=True)
         tail_sum = sums_of(jnp.broadcast_to(tail_sum, (16, INNER_DEV)))[0:1]
+
+        @pl.loop(0, BLOCKS)
+        def _(i):
+            at = rows_at(i)
+            taps = small[S_CONV : S_CONV + 4, INNER_DEV : INNER_DEV + 256]
+            d_bcc = d_bc[at] * silu_slope(conv_rows(bc_pre[rows_at(i, RIM)], taps))
+            d_bc[at] = d_bcc
+            bc_out[at] = d_bcc.astype(BF)
+
+        copies = [
+            send(bc_out, bc_in.at[d], bc_sems[0].at[s, d], bc_sems[1].at[s, d], heads[d]) for d in range(3)
+        ]
         d_log = running(terms[...], True) + tail_sum
         rate = small[S_RATE : S_RATE + 1, :128]
         d_dt = direct[...] + rate * d_log
@@ -930,9 +979,17 @@
             for t in range(4):
                 moved = pre[RIM - 3 + t : RIM - 3 + t + STEP]
                 taps_ref[t : t + 1, :INNER_DEV] += jnp.sum(moved * d_xc, axis=0, keepdims=True)
+
+        finish(copies)
+
+        @pl.loop(0, BLOCKS)
+        def _(i):
+            at = rows_at(i)
+            d_bcc = d_bc[at]
+            for d in range(3):
+                d_bcc = d_bcc + bc_in[d, at].astype(F32)
+            ext[at, INNER_DEV:] = d_bcc
             pre = bc_pre[rows_at(i, RIM)]
-            d_bcc = d_bc[at] * silu_slope(conv_rows(pre, taps[:, INNER_DEV : INNER_DEV + 256]))
-            ext[at, INNER_DEV:] = d_bcc
             for t in range(4):
                 moved = pre[RIM - 3 + t : RIM - 3 + t + STEP]
                 taps_ref[t : t + 1, INNER_DEV:] += jnp.sum(moved * d_bcc, axis=0, keepdims=True)
@@ -943,11 +1000,14 @@
         if s:
             for move in load_kept(0):
                 move.start()
-        taps_all[...] = taps_ref[:, INNER_DEV:]
 
         if s == 0:
             next(loose)
             next(late)
+        else:
+            next(early)
+            for seq in along_z + along_x:
+                pl.semaphore_signal(first_free.at[0], inc=1, device_id={"seq": seq}, device_id_type=MESH)
         rim.wait()
 
         @pl.when(me == 15)
@@ -974,7 +1034,7 @@
         @pl.loop(0, 6)
         def _(j):
             got = dot_last(d_zx[...], zx_w[tile_at(j), :])
-            got = got + dot_last(d_bd[:, :256], bc_w[tile_at(j), :])
+            got = got + dot_last(d_bd[:, :256], bc_w[tile_at(j), :]) * 0.25
             got = got + dot(d_bd[:, 256:], dt_all[s, :, tile_at(j)])
             part[:, tile_at(j)] = got.astype(BF)
 
@@ -985,10 +1045,6 @@
         for d in range(1, 4):
             src = part.at[:, quarter(shifted(place, d, 4))]
             copies.append(send(src, sum_in.at[d - 1], s_sems[0].at[s, d], s_sems[1].at[s, d], heads[d - 1]))
-        for d in range(1, 4):
-            copies.append(
-                send(taps_all, taps_in.at[d - 1], s_sems[0].at[s, d + 4], s_sems[1].at[s, d + 4], heads[d - 1])
-            )
         for stage, rows in zip(stages, half_rows):
             for j in range(2):
                 got = dot_first(normed[RIM:, rows[j]], d_zx[:, INNER_DEV:]).astype(BF)
@@ -996,23 +1052,14 @@
                     sub = 8 * j + i
                     stage[sub // 4, sub % 4, EARLY:WIDE] = got[PART * i : PART * i + PART]
 
-        cross(s, 1).start()
-        for stage, cols in zip(stages, half_cols):
+        for n, (stage, cols) in enumerate(zip(stages, half_cols)):
             got = dot_first(d_bd[...], normed[RIM:, cols])
             for i in range(16):
-                stage[i // 4, i % 4, WIDE : WIDE + 16] = got[16 * i : 16 * i + 16].astype(BF)
-            stage[0, 0, WIDE + 16 :] = got[256:272].astype(BF)
+                stage[i // 4, i % 4, WIDE:SUB] = got[16 * i : 16 * i + 16].astype(BF)
+            rest_out[core if n == 0 else 1 - core, 0:16] = got[256:272].astype(BF)
+        cross(s, 1).start()
         next(early)
-        if s:
-            for target in near:
-                pl.semaphore_signal(first_free.at[0], inc=1, device_id=target, device_id_type=MESH)
-        else:
-            next(loose)
         finish(copies)
-        total = taps_all[...]
-        for d in range(3):
-            total = total + taps_in[d]
-        taps_ref[:, INNER_DEV:] = total
 
         @pl.loop(0, BLOCKS)
         def _(i):
@@ -1028,11 +1075,13 @@
         for d in range(1, 4):
             dst = d_normed_ref.at[:, quarter(place)]
             copies.append(send(sum_own, dst, s_sems[2].at[s, d], s_sems[3].at[s, d], heads[d - 1]))
-        old_loose, old_late = loose, late
-        late = reduction(s, 1)
-        next(late)
+        old_late, late = late, reduction(s, 1)
         next(early)
+        if s == 0:
+            next(late)
         finish(copies)
+        if s == 0:
+            next(early)
         norm_ref[...] = jnp.zeros_like(norm_ref)
 
         @pl.loop(0, BLOCKS)
@@ -1052,10 +1101,12 @@
             small_rows[h, 1:5] = taps_ref[0:4, :INNER_DEV]
             small_rows[h, 5:9] = sums_ref[0:4]
             small_rows[h, 9:13, 0:256] = taps_ref[0:4, INNER_DEV:]
-        for stage, h in zip(stages, (core, 1 - core)):
-            stage[0, 1, WIDE + 16 :] = small_rows[h].astype(BF)
-        cross(s, 2).start()
-        loose = reduction(s, 2)
+            rest_out[h, 16:] = small_rows[h].astype(BF)
+        old_loose, loose = loose, reduction_rest(s)
+        next(loose)
+        if s:
+            next(late)
+            pl.semaphore_signal(theirs_free, inc=1, device_id=other, device_id_type=MESH)
 
         @pl.when(core == 1 - s)
         def _():
@@ -1082,11 +1133,9 @@
         pltpu.make_async_copy(last_ref, g_o_buf, move_sem.at[0]).wait()
         pltpu.make_async_copy(g_o_buf, section_ref.at[1], move_sem.at[0]).start()
 
-    order = (early, loose, late, loose, late, loose, loose, late, loose, early, late, loose)
-    order += (old_early, old_late, old_loose)
-    for turn in order:
+    for turn in (loose, late, loose, late, loose, late, loose, early, late, old_early, old_late, old_loose):
         next(turn)
-    for piece in range(3):
+    for piece in range(2):
         cross(0, piece).wait_send()
     swapped(0, last_ref, section_ref).wait()
     swapped(1, d_v.at[0], leaving_ref).wait()
@@ -1138,27 +1187,36 @@
         vm((STATE, INNER_DEV), BF),
         vm((8, INNER_DEV + 256), F32),
         vm((8, INNER_DEV + 256), F32),
-        vm((3, 8, 256), F32),
-        vm((8, 256), F32),
+        vm((ROWS, 256), BF),
+        vm((3, ROWS, 256), BF),
         vm((8, WIDTH), F32),
         vm((8, INNER_DEV), F32),
         vm((2, 16, INNER_DEV), F32),
-        vm((2, 3, 16, INNER_DEV), BF),
+        vm((2, REST, INNER_DEV), BF),
+        vm((2, REST, INNER_DEV), BF),
+        vm((2, 3, REST, INNER_DEV), BF),
+        vm((2, 3, REST, INNER_DEV), BF),
+        vm((2, REST, INNER_DEV), BF),
         dma((len(SLOT),)),
         dma((2, 3)),
         dma((3,)),
         dma((2,)),
     ]
     scratch += [dma((2, 16))] * 4 + [dma((2, 8))] * 2 + [dma((2, 4))] * 2
-    scratch += [dma((2,))] * 4 + [dma((2, 3))] * 2
-    scratch += [dma((2, 3, 4))] * 4 + [dma((2, 4))] * 2 + [dma((2, 3, 4))] * 2
-    scratch += [dma((2, 3, 4)), dma((2, 3, 2, 4)), regular, regular((2,))]
+    scratch += [dma((2,))] * 4 + [dma((2, 2))] * 2
+    scratch += [dma((2, 2, 2, 4))] * 7 + [dma((2, 2, 2, 2, 4))]
+    scratch += [dma((2, 3))] * 2 + [dma((2, 8))] * 2 + [regular, regular((2,))]
     flat = [kept[s][name] for s in range(2) for name, _, _ in KEPT]
     return pl.pallas_call(
         backward_kernel,
-        out_shape=[sds((2,) + halves, BF), sds((2, ROWS, WIDTH), BF), sds((2, ROWS, WIDTH), BF)],
+        out_shape=[
+            sds((2,) + halves, BF),
+            sds((2, REST, INNER_DEV), BF),
+            sds((2, ROWS, WIDTH), BF),
+            sds((2, ROWS, WIDTH), BF),
+        ],
         in_specs=[ANY] * 9 + [VM] * 2 + [ANY] * 32,
-        out_specs=[ANY] * 3,
+        out_specs=[ANY, VM, ANY, ANY],
         scratch_shapes=scratch,
         compiler_params=comm_params(number),
         name="backward_layers",
@@ -1166,8 +1224,8 @@
 
 
 def widen_kernel(
-    a_ref, zx_ref, out_ref, bc_ref, dt_ref, norm_ref, bias_ref, rate_ref, skip_ref, conv_ref, conv_bc_ref, gate_ref,
-    bc_all,
+    a_ref, rest_ref, zx_ref, out_ref, bc_ref, dt_ref, norm_ref, bias_ref, rate_ref, skip_ref, conv_ref, conv_bc_ref,
+    gate_ref, bc_all,
 ):
     step = pl.program_id(0)
     for h in range(2):
@@ -1176,19 +1234,17 @@
         zx_ref[h, :, 1, :] = a_ref[h, 0, EARLY:WIDE].astype(F32)
         out_ref[:, cols] = a_ref[h, 0, 0:PART].astype(F32)
         at = pl.ds(pl.multiple_of(step * 16, 16), 16)
-        bc_all[at, cols] = a_ref[h, 0, WIDE : WIDE + 16].astype(F32)
+        bc_all[at, cols] = a_ref[h, 0, WIDE:SUB].astype(F32)
 
     @pl.when(step == 0)
     def _():
-        for h in range(2):
-            cols = slice(h * INNER_DEV, (h + 1) * INNER_DEV)
-            dt_ref[:, cols] = a_ref[h, 0, WIDE + 16 :].astype(F32)[0:HEADS_DEV]
-
-    @pl.when(step == 1)
-    def _():
-        rows = a_ref[0, 0, WIDE + 16 :].astype(F32)
+        rows = rest_ref[0].astype(F32)
+        more = rest_ref[1].astype(F32)
+        dt_ref[:, :INNER_DEV] = rows[0:HEADS_DEV]
+        dt_ref[:, INNER_DEV:] = more[0:HEADS_DEV]
+        rows = rows[16:]
         norm_ref[:, :INNER_DEV] = rows[0:1]
-        norm_ref[:, INNER_DEV:] = a_ref[1, 0, WIDE + 16 :].astype(F32)[0:1]
+        norm_ref[:, INNER_DEV:] = more[16:17]
         conv_ref[...] = rows[1:5]
         gate_ref[...] = rows[5:6]
         heads = jnp.concatenate(
@@ -1208,7 +1264,7 @@
         bc_ref[...] = bc_all[...].T
 
 
-def widen(total):
+def widen(total, rest):
     total = total.reshape(2, 16, SUB, INNER_DEV)
     fixed = ((WIDTH, 256), (HEADS_DEV, WIDTH), (1, WIDTH)) + ((1, HEADS_DEV),) * 3
     fixed += ((4, INNER_DEV), (4, 256), (1, INNER_DEV))
@@ -1217,7 +1273,10 @@
         widen_kernel,
         grid=(16,),
         out_shape=[jax.ShapeDtypeStruct(shape, F32) for shape in shapes],
-        in_specs=[pl.BlockSpec((2, 1, SUB, INNER_DEV), lambda i: (0, i, 0, 0))],
+        in_specs=[
+            pl.BlockSpec((2, 1, SUB, INNER_DEV), lambda i: (0, i, 0, 0)),
+            pl.BlockSpec((2, REST, INNER_DEV), lambda i: (0, 0, 0)),
+        ],
         out_specs=[
             pl.BlockSpec((2, PART, 2, INNER_DEV), lambda i: (0, i, 0, 0)),
             pl.BlockSpec((PART, WIDTH), lambda i: (i, 0)),
@@ -1226,7 +1285,7 @@
         scratch_shapes=[pltpu.VMEM((256, WIDTH), F32)],
         compiler_params=pltpu.CompilerParams(vmem_limit_bytes=VMEM_CAP),
         name="widen",
-    )(total)
+    )(total, rest)
 
 
 def on_device(
@@ -1249,10 +1308,10 @@
     small_args = (norm_gain, gate_gain, conv_x[0], conv_bc[0], dt_bias, a_log, d_skip)
     kept, (zx_t, bc_t, out_t, smalls, dt_all) = forward(x_in, zx_m, bc_m, out_m, dt_m, small_args, 0)
     held = (zx_m, bc_m, out_m, zx_t, bc_t, out_t)
-    total, section_out, grads_in = backward(
+    total, rest, section_out, grads_in = backward(
         cotangent, x_in, kept[1]["following"], held, smalls, dt_all, kept, 1
     )
-    g_zx, g_out, g_bc, g_dt, g_norm, g_bias, g_rate, g_skip, g_conv_x, g_conv_bc, g_gate = widen(total)
+    g_zx, g_out, g_bc, g_dt, g_norm, g_bias, g_rate, g_skip, g_conv_x, g_conv_bc, g_gate = widen(total, rest)
     return (
         section_out[None],
         grads_in[None],

time: 313 us -> 295 us (0.942)
  Pallas kernels: 302 us -> 284 us
    pallas_call x1, Pallas kernels: 184 us -> 166 us  [backward(): pl.pallas_call(backward_kernel, out_shape=[sds((2,) + halves, BF), sds((2...]
where the time goes in v3:
time: 295 us
  Pallas kernels  284 us (96%)
  local copies, waits for them, and re-layouts  9.47 us (3%)
    pallas_call x1, Pallas kernels, backward(): pl.pallas_call(backward_kernel, out_shape=[sds((2,) + halves, BF), sds((2...  166 us
    pallas_call x1, Pallas kernels, forward(): pl.pallas_call(forward_kernel, out_shape=[sds(shape, kind) for _, shape,...  103 us
    pallas_call x1, Pallas kernels, widen(): pl.pallas_call(widen_kernel, grid=(16,), out_shape=[jax.ShapeDtypeStruct(...  15 us
    unnamed x8, local copies, waits for them, and re-layouts  9.47 us

profile of v3, /device:TPU:0, one launch (start us, length us, event | category | flops | bytes accessed | tf_op | source)
XLA Modules:
  0.0 294.5 jit_solution(6335040352523390702)
XLA Ops:
  0.6 5.5 %copy.27 = bf16[192,8,2,768]{3,1,2,0:T(8,128)(2,1)} copy(bf16[192,8,2,768]{3,2,1,0:T(2,128)(2,1)} %bitcast.26) | data formatting | bytes 9437184
  6.1 103.1 %forward_layers.1 = (bf16[272,1536]{1,0:T(8,128)(2,1)}, f32[256,768]{1,0:T(8,128)}, f32[272,768]{1,0:T(8,128)}, f32[272,256]{1,0:T(8,128)}, f32[256,128]{1,0:T(8...) custom-call(bf16[2,256,1536]{2,1,0:T(8,128)(2,1)} %refs_1_.1, ...), custom_call_target="tpu_custom_call" | custom-call | tf_op jit(solution)/shard_map/forward_layers/pallas_call | solution.py:468
  109.2 166.3 %backward_layers.1 = (bf16[2,4,4,160,768]{4,3,2,1,0:T(8,128)(2,1)}, bf16[2,32,768]{2,1,0:T(8,128)(2,1)}, bf16[2,256,1536]{2,1,0:T(8,128)(2,1)}, bf16[2,256,1536]{2,1,0:T(8,128)(2,1)}) custom-call(bf16[2,256,1536]{2,1,0:T(8,128)(2,1)} %refs_0_.3, bf16[2,256,1536]{2,1,0:T(8,128)(2,1)} %refs_1_.1, bf16[256,1536]{1,0:T(8,128)(2,1)} %get-tuple-element.65.refs_2_.refs_42_, ...), custom_call_target="tpu_custom_call" | custom-call | tf_op jit(solution)/shard_map/backward_layers/pallas_call | solution.py:1210
  275.5 0.0 copy-start.1
  275.5 15.0 %widen.1 = (f32[2,768,2,768]{3,2,1,0:T(2,128)}, f32[768,1536]{1,0:T(8,128)}, f32[1536,256]{1,0:T(8,128)}, f32[12,1536]{1,0:T(8,128)}, f32[1,1536]{1,0:T(1,128)},...) custom-call(bf16[2,16,160,768]{3,2,1,0:T(8,128)(2,1)} %bitcast.25, ...), custom_call_target="tpu_custom_call" | custom-call | tf_op jit(solution)/shard_map/widen/pallas_call | solution.py:1272
  290.5 0.0 copy-start
  290.5 1.7 copy.26
  292.2 0.0 copy-done.1
  292.2 1.1 copy.30
  293.4 0.0 copy-done
  293.4 1.1 copy.31
Async XLA Ops:
  275.5 16.7 %copy-start.1 = (bf16[2,256,1536]{2,1,0:T(8,128)(2,1)S(1)}, bf16[2,256,1536]{2,1,0:T(8,128)(2,1)}, u32[]{:S(2)}) copy-start(bf16[2,256,1536]{2,1,0:T(8,128)(2,1)} %get-tuple-element.102) | copy-start | bytes 4718596
  290.5 2.9 copy-start

commit v4 on v3

--- a/solution.py
+++ b/solution.py
@@ -221,14 +221,15 @@
 def forward_kernel(*refs):
     x_ref, zx_m, bc_m, out_m, dt_m = refs[:5]
     norm_gain, gate_gain, conv_x, conv_bc, dt_bias, a_log, d_skip = refs[5:12]
-    kept = [{name: refs[12 + 16 * s + i] for i, (name, _, _) in enumerate(KEPT)} for s in range(2)]
-    zx_t, bc_t, out_t, small_w, dt_w = refs[44:49]
-    v_buf, rim_buf, zx_w, bc_w, out_w = refs[49:54]
-    tail_x, scores, dt_buf, tail, low, sq, part = refs[54:61]
-    chain_out, chain_in, chain_back, chain_got = refs[61:65]
-    sum_in, square_out, square_in, sum_own, next_own = refs[65:70]
-    w_send, w_recv, w_own, rim_send, rim_recv = refs[70:75]
-    c_sems, s_sems, t_sem, v_sem = refs[75:79], refs[79:83], refs[83], refs[84]
+    stored = [{name: refs[12 + 16 * s + i] for i, (name, _, _) in enumerate(KEPT)} for s in range(2)]
+    zx_t, bc_t, out_t, small_w, dt_w, part_ref = refs[44:50]
+    v_buf, rim_buf, zx_w, bc_w, out_w = refs[50:55]
+    tail_x, scores, dt_buf, tail, low, sq, part = refs[55:62]
+    chain_out, chain_in, chain_back, chain_got = refs[62:66]
+    sum_in, square_out, square_in, sum_own, next_own = refs[66:71]
+    w_send, w_recv, w_own, rim_send, rim_recv = refs[71:76]
+    c_sems, s_sems, t_sem, v_sem, k_sem = refs[76:80], refs[80:84], refs[84], refs[85], refs[86]
+    kept = [{name: refs[87 + 16 * s + i] for i, (name, _, _) in enumerate(KEPT)} for s in range(2)]
 
     core, me, place = lax.axis_index("section"), lax.axis_index("seq"), lax.axis_index("head")
     other = {"section": 1 - core}
@@ -274,7 +275,18 @@
         send(dt_w.at[core, 0:16], dt_w.at[core, 0:16], w_send.at[5], w_recv.at[5], other),
     ]
     for i, (src, dst) in enumerate(moves):
-        across.append(send(src, dst, w_send.at[i], w_recv.at[i], other))
+        across.append(
+            pltpu.make_async_remote_copy(
+                src_ref=src,
+                dst_ref=dst,
+                send_sem=w_send.at[i],
+                recv_sem=w_recv.at[i],
+                device_id=other,
+                device_id_type=MESH,
+            )
+        )
+    across[2].start()
+    across[3].start()
 
     def arrive(section, i):
         @pl.when(core == section)
@@ -294,7 +306,16 @@
 
     across[0].wait_recv()
     across[1].wait_recv()
-    entering = v_buf
+    def store(s, names):
+        moves = []
+        for i, (name, _, _) in enumerate(KEPT):
+            if name in names:
+                moves.append(pltpu.make_async_copy(kept[s][name], stored[s][name], k_sem.at[s, i]))
+        return moves
+
+    first_names = ("normed", "x_pre", "bc_pre", "dt_pre", "la", "la_t", "xd", "bc_act", "x_act", "decay")
+    next_names = ("z", "y", "state")
+    last_names = ("scale", "out", "following")
     for s in range(2):
         k = kept[s]
         small = small_w.at[s]
@@ -311,11 +332,12 @@
                 rim_buf[1] = jnp.zeros((RIM, WIDTH), BF)
 
         normed[0:RIM] = norm_rows(rim_buf[s], gain)
-
-        @pl.loop(0, ROWS // 16)
-        def _(i):
-            at = pl.ds(pl.multiple_of(i * 16, 16), 16)
-            normed[pl.ds(pl.multiple_of(i * 16 + RIM, 16), 16)] = norm_rows(entering[at], gain)
+        if s == 0:
+
+            @pl.loop(0, ROWS // 16)
+            def _(i):
+                at = pl.ds(pl.multiple_of(i * 16, 16), 16)
+                normed[pl.ds(pl.multiple_of(i * 16 + RIM, 16), 16)] = norm_rows(v_buf[at], gain)
 
         arrive(s, 0)
         bc_pre[...] = dot(normed[...], bc_w[s])
@@ -327,6 +349,9 @@
         def _(j):
             x_pre[:, tile_at(j)] = dot(normed[...], zx_w[s, :, tile_at(j, 256, INNER_DEV)])
 
+        if s == 0:
+            across[3].wait_send()
+            across[4].start()
         dt = softplus(dt_raw + small[S_BIAS : S_BIAS + 1, :128])
         dt_buf[...] = dt
         la = running(dt * small[S_RATE : S_RATE + 1, :128], False)
@@ -348,6 +373,10 @@
             bc_act[rows_at(i)] = silu(bc).astype(BF)
 
         b_rows, c_rows = bc_act[:, :STATE], bc_act[:, STATE:]
+        if s == 0:
+            across[5].start()
+        for move in store(s, first_names):
+            move.start()
         chain_load(dot_first(b_rows, tail_x[...]), decay, chain_out.at[s])
         copies = spread_send(chain_out.at[s], chain_in.at[s], me, c_sems[0].at[s], c_sems[1].at[s])
         arrive(s, 2)
@@ -380,77 +409,100 @@
         finish(copies)
         chain_unload(chain_got.at[s], k["state"])
 
-        @pl.loop(0, BLOCKS)
-        def _(i):
-            at = rows_at(i)
-            y = y_ref[at] + spread(jnp.exp(la_ref[at])) * dot(bc_act[at, STATE:], k["state"][...])
-            y_ref[at] = y
-            ssd = y + small[S_SKIP : S_SKIP + 1, :INNER_DEV] * x_act[at]
-            gated = ssd * silu(z_ref[at])
-            sq[at] = jnp.broadcast_to(jnp.sum(gated * gated, axis=-1, keepdims=True), (STEP, 128))
-            low[at] = (gated * small[S_GATE : S_GATE + 1, :INNER_DEV]).astype(BF)
-
-        square_out[s] = sq[...].T[0:8]
-        arrive(s, 3)
+        copies = []
+        for half in range(2):
+            rows = slice(half * 128, half * 128 + 128)
+
+            @pl.loop(half * BLOCKS // 2, (half + 1) * BLOCKS // 2)
+            def _(i):
+                at = rows_at(i)
+                y = y_ref[at] + spread(jnp.exp(la_ref[at])) * dot(bc_act[at, STATE:], k["state"][...])
+                y_ref[at] = y
+                ssd = y + small[S_SKIP : S_SKIP + 1, :INNER_DEV] * x_act[at]
+                gated = ssd * silu(z_ref[at])
+                if s == 0:
+                    sq[at] = jnp.broadcast_to(jnp.sum(gated * gated, axis=-1, keepdims=True), (STEP, 128))
+                low[at] = (gated * small[S_GATE : S_GATE + 1, :INNER_DEV]).astype(BF)
+
+            if s == 0:
+                square_out[half] = sq[rows].T[0:8]
+            if half == 0:
+                arrive(s, 3)
+                if s:
+                    for move in store_theirs(core, (bc_w, zx_w, out_w), (bc_t, zx_t, out_t), t_sem):
+                        move.start()
+
+            @pl.loop(0, 6)
+            def _(j):
+                part[rows, tile_at(j)] = dot(low[rows], out_w[s, :, tile_at(j)]).astype(BF)
+
+            if s:
+                continue
+            batch = []
+            for d in range(3):
+                src = part.at[rows, quarter(shifted(place, d + 1, 4))]
+                sems = s_sems[0].at[half, d], s_sems[1].at[half, d]
+                batch.append(send(src, sum_in.at[d, rows], *sems, heads[d]))
+                sems = s_sems[0].at[half, d + 3], s_sems[1].at[half, d + 3]
+                batch.append(send(square_out.at[half], square_in.at[half, d], *sems, heads[d]))
+            copies.append(batch)
+
+        for move in store(s, next_names):
+            move.start()
         if s:
-            for move in store_theirs(core, (bc_w, zx_w, out_w), (bc_t, zx_t, out_t), t_sem):
-                move.start()
-
-        @pl.loop(0, 6)
-        def _(j):
-            part[s, :, tile_at(j)] = dot(low[...], out_w[s, :, tile_at(j)]).astype(BF)
-
-        copies = []
-        for d in range(1, 4):
-            src = part.at[s, :, quarter(shifted(place, d, 4))]
-            copies.append(send(src, sum_in.at[s, d], s_sems[0].at[s, d], s_sems[1].at[s, d], heads[d - 1]))
-        for d in range(1, 4):
-            copies.append(
-                send(square_out.at[s], square_in.at[s, d], s_sems[0].at[s, d + 4], s_sems[1].at[s, d + 4], heads[d - 1])
-            )
-        finish(copies)
-        square = square_out[s]
-        for d in range(1, 4):
-            square = square + square_in[s, d]
-        column = lax.rsqrt(square * (1.0 / INNER) + EPS).T[:, 0:1]
-        k["scale"][...] = jnp.broadcast_to(column, (ROWS, 128))
-
-        @pl.loop(0, BLOCKS)
-        def _(i):
-            at = rows_at(i)
-            total = part[s, at, quarter(place)].astype(F32)
-            for d in range(1, 4):
-                total = total + sum_in[s, d, at].astype(F32)
-            total = (total * k["scale"][at][:, 0:1]).astype(BF)
-            sum_own[s, at] = total
-            k["out"][at, quarter(place)] = total
-
-        copies = []
-        for d in range(1, 4):
-            copies.append(
-                send(sum_own.at[s], k["out"].at[:, quarter(place)], s_sems[2].at[s, d], s_sems[3].at[s, d], heads[d - 1])
-            )
-        if s == 0:
-            edge = slice(ROWS - RIM, ROWS)
-            next_own[...] = (
-                v_buf[edge, quarter(place)].astype(F32) + sum_own[0, edge].astype(F32)
-            ).astype(BF)
-            rim_in = []
-            for d in range(4):
-                dst = rim_buf.at[1, :, quarter(place)]
-                target = {"head": shifted(place, d, 4), "seq": later}
-                rim_in.append(send(next_own, dst, rim_send.at[1 + d], rim_recv.at[1 + d], target))
-        finish(copies)
-
-        @pl.loop(0, BLOCKS)
-        def _(i):
-            at = rows_at(i)
-            k["following"][at] = (entering[at].astype(F32) + k["out"][at].astype(F32)).astype(BF)
-
-        entering = k["following"]
-
-    for copy in across:
-        copy.wait_send()
+            break
+        for half in range(2):
+            rows = slice(half * 128, half * 128 + 128)
+            finish(copies[half])
+            square = square_out[half]
+            for d in range(3):
+                square = square + square_in[half, d]
+            column = lax.rsqrt(square * (1.0 / INNER) + EPS).T[:, 0:1]
+            k["scale"][rows] = jnp.broadcast_to(column, (128, 128))
+
+            @pl.loop(half * BLOCKS // 2, (half + 1) * BLOCKS // 2)
+            def _(i):
+                at = rows_at(i)
+                total = part[at, quarter(place)].astype(F32)
+                for d in range(3):
+                    total = total + sum_in[d, at].astype(F32)
+                total = (total * k["scale"][at][:, 0:1]).astype(BF)
+                sum_own[at] = total
+                k["out"][at, quarter(place)] = total
+
+            copies[half] = []
+            for d in range(3):
+                sems = s_sems[2].at[half, d], s_sems[3].at[half, d]
+                dst = k["out"].at[rows, quarter(place)]
+                copies[half].append(send(sum_own.at[rows], dst, *sems, heads[d]))
+        edge = slice(ROWS - RIM, ROWS)
+        next_own[...] = (v_buf[edge, quarter(place)].astype(F32) + sum_own[edge].astype(F32)).astype(BF)
+        rim_in = []
+        for d in range(4):
+            dst = rim_buf.at[1, :, quarter(place)]
+            target = {"head": shifted(place, d, 4), "seq": later}
+            rim_in.append(send(next_own, dst, rim_send.at[1 + d], rim_recv.at[1 + d], target))
+        for half in range(2):
+            finish(copies[half])
+
+            @pl.loop(half * 8, half * 8 + 8)
+            def _(i):
+                at = pl.ds(pl.multiple_of(i * 16, 16), 16)
+                following = (v_buf[at].astype(F32) + k["out"][at].astype(F32)).astype(BF)
+                k["following"][at] = following
+                at = pl.ds(pl.multiple_of(i * 16 + RIM, 16), 16)
+                kept[1]["normed"][at] = norm_rows(following, small_w[1, S_NORM : S_NORM + 1])
+
+        for move in store(s, last_names):
+            move.start()
+
+    store_part = pltpu.make_async_copy(part, part_ref, v_sem)
+    store_part.start()
+    finish(store(0, first_names + next_names + last_names))
+    finish(store(1, first_names + next_names))
+    store_part.wait()
+    for i in (0, 1, 2, 4, 5):
+        across[i].wait_send()
     for move in store_theirs(core, (bc_w, zx_w, out_w), (bc_t, zx_t, out_t), t_sem):
         move.wait()
 
@@ -469,9 +521,9 @@
         forward_kernel,
         out_shape=[sds(shape, kind) for _, shape, kind in KEPT * 2]
         + [sds(zx_m.shape, BF), sds(bc_m.shape, BF), sds(out_m.shape, BF)]
-        + [sds((2, 16, WIDTH), F32), sds((2, 128, WIDTH), BF)],
+        + [sds((2, 16, WIDTH), F32), sds((2, 128, WIDTH), BF), sds((ROWS, WIDTH), BF)],
         in_specs=[ANY] * 4 + [VM] * 8,
-        out_specs=[VM] * 32 + [ANY] * 3 + [VM] * 2,
+        out_specs=[ANY] * 35 + [VM] * 2 + [ANY],
         scratch_shapes=[
             vm((ROWS, WIDTH), BF),
             vm((2, RIM, WIDTH), BF),
@@ -484,15 +536,15 @@
             vm((ROWS, 128), F32),
             vm((ROWS, INNER_DEV), BF),
             vm((ROWS, 128), F32),
-            vm((2, ROWS, WIDTH), BF),
+            vm((ROWS, WIDTH), BF),
             vm((2, 16, 16, 512), BF),
             vm((2, 16, 16, 512), BF),
             vm((2, 16, 16, 384), BF),
             vm((2, 16, 16, 384), BF),
-            vm((2, 4, ROWS, 384), BF),
-            vm((2, 8, ROWS), F32),
-            vm((2, 4, 8, ROWS), F32),
-            vm((2, ROWS, 384), BF),
+            vm((3, ROWS, 384), BF),
+            vm((2, 8, 128), F32),
+            vm((2, 3, 8, 128), F32),
+            vm((ROWS, 384), BF),
             vm((RIM, 384), BF),
             dma((6,)),
             dma((6,)),
@@ -503,18 +555,20 @@
             dma((2, 16)),
             dma((2, 16)),
             dma((2, 16)),
-            dma((2, 8)),
-            dma((2, 8)),
-            dma((2, 4)),
-            dma((2, 4)),
+            dma((2, 6)),
+            dma((2, 6)),
+            dma((2, 3)),
+            dma((2, 3)),
             dma((3,)),
             dma,
-        ],
+            dma((2, len(KEPT))),
+        ]
+        + [vm(shape, kind) for _, shape, kind in KEPT * 2],
         compiler_params=comm_params(number),
         name="forward_layers",
     )(x_in, zx_m, bc_m, out_m, dt_m, *smalls)
     kept = [{name: got[16 * s + i] for i, (name, _, _) in enumerate(KEPT)} for s in range(2)]
-    return kept, got[32:37]
+    return kept, got[32:38]
 
 
 PART = 48
@@ -531,7 +585,7 @@
 
 
 def backward_kernel(*refs):
-    cot_ref, x_ref, last_ref = refs[:3]
+    cot_ref, x_ref, part_ref = refs[:3]
     held = (refs[3:6], refs[6:9])
     small_all, dt_all = refs[9:11]
     saved = [{name: refs[11 + 16 * s + i] for i, (name, _, _) in enumerate(KEPT)} for s in range(2)]
@@ -557,6 +611,8 @@
     c_sems, s_sems, rim_sems, swap_sems = take(4), take(4), take(2), take(2)
     cross_sems, one_sems, two_sems, back_sems, last_sems = take(2), take(2), take(2), take(2), take(2)
     bc_sems, rest_sems = take(2), take(2)
+    row_out, row_in, final_in, final_own = take(4)
+    row_sems, final_sems = take(2), take(4)
     theirs_free, first_free = take(2)
 
     core, me, place = lax.axis_index("section"), lax.axis_index("seq"), lax.axis_index("head")
@@ -568,13 +624,16 @@
     heads = [{"head": shifted(place, d, 4)} for d in range(1, 4)]
     targets = [other] + [{"seq": shifted(me, d, 16)} for d in range(1, 16)] + heads
     targets += [{"section": 1 - core, "seq": seq} for seq in along_z + along_x]
+    targets += [{"section": 1 - core, "head": shifted(place, d, 4)} for d in range(1, 4)]
     barrier = pltpu.get_barrier_semaphore()
     for target in targets:
         pl.semaphore_signal(barrier, inc=1, device_id=target, device_id_type=MESH)
 
     def load_kept(s):
         return [
-            pltpu.make_async_copy(saved[s][name], k[name], k_sem.at[i]) for i, name in enumerate(SLOT)
+            pltpu.make_async_copy(saved[s][name], k[name], k_sem.at[i])
+            for i, name in enumerate(SLOT)
+            if s == 0 or name not in ("scale", "out")
         ]
 
     def load_rows(s):
@@ -610,8 +669,6 @@
             move.start()
 
     small_rows[...] = jnp.zeros_like(small_rows)
-    pl.semaphore_wait(barrier, len(targets))
-
     def swapped(i, src, dst):
         return pltpu.make_async_remote_copy(
             src_ref=src,
@@ -622,13 +679,18 @@
             device_id_type=MESH,
         )
 
-    @pl.when(core == 0)
-    def _():
-        swapped(0, last_ref, section_ref).start()
-
-    @pl.when(core == 1)
-    def _():
-        swapped(0, saved[0]["following"], section_ref).start()
+    def final(d, micro):
+        return pltpu.make_async_remote_copy(
+            src_ref=final_own,
+            dst_ref=section_ref.at[micro, :, quarter(place)],
+            send_sem=final_sems[2].at[d],
+            recv_sem=final_sems[3].at[micro, d],
+            device_id={"section": 1, "head": shifted(place, d + 1, 4)},
+            device_id_type=MESH,
+        )
+
+    def final_stay():
+        return pltpu.make_async_copy(final_own, section_ref.at[1, :, quarter(place)], move_sem.at[0])
 
     def cross(s, piece):
         lo, hi = GROUPS[piece][0][0], GROUPS[piece][1][1]
@@ -650,7 +712,7 @@
         def _(i):
             @pl.loop(0, 4)
             def _(j):
-                own[s, i, j, low:high] = add_rows(own[s, i, j, low:high], theirs[i, j, low:high]).astype(BF)
+                own[s, i, j, low:high] = own[s, i, j, low:high] + theirs[i, j, low:high]
 
         if s == 0:
             pl.semaphore_wait(first_free.at[group], 6)
@@ -838,6 +900,39 @@
         if s:
             finish(load_rows(1))
 
+            @pl.loop(0, BLOCKS)
+            def _(i):
+                at = rows_at(i)
+                gain = small[S_GATE : S_GATE + 1, :INNER_DEV]
+                ssd = y_ref[at] + small[S_SKIP : S_SKIP + 1, :INNER_DEV] * x_act[at]
+                gated = ssd * silu(z_ref[at])
+                square = jnp.sum(gated * gated, axis=-1, keepdims=True)
+                mean = jnp.sum(gated * gain * d_xd[at], axis=-1, keepdims=True)
+                lane = lax.broadcasted_iota(jnp.int32, (STEP, 128), 1)
+                tail_ref[at] = jnp.where(lane == 0, square, mean)
+
+            row_out[...] = tail_ref[...].T[0:8]
+            pl.semaphore_wait(barrier, len(targets))
+            copies = [
+                send(row_out, row_in.at[d], row_sems[0].at[d], row_sems[1].at[d], heads[d]) for d in range(3)
+            ]
+            final_copies = []
+            for d in range(3):
+                src = part_ref.at[:, quarter(shifted(place, d + 1, 4))]
+                sems = final_sems[0].at[d], final_sems[1].at[d]
+                final_copies.append(send(src, final_in.at[d], *sems, heads[d]))
+            load_final = pltpu.make_async_copy(part_ref.at[:, quarter(place)], final_own, move_sem.at[0])
+            load_final.start()
+            finish(copies)
+            total = row_out[...]
+            for d in range(3):
+                total = total + row_in[d]
+            total = jnp.concatenate([total] * 16, axis=0).T
+            scale = lax.rsqrt(total[:, 0:1] * (1.0 / INNER) + EPS)
+            mean = total[:, 1:2] * scale * scale * scale * (1.0 / INNER)
+            lane = lax.broadcasted_iota(jnp.int32, (ROWS, 128), 1)
+            k["scale"][...] = jnp.where(lane == 0, scale, mean)
+
         @pl.loop(0, BLOCKS)
         def _(i):
             at = rows_at(i)
@@ -849,8 +944,11 @@
             gate_silu = gate * sigma
             gated = ssd * gate_silu
             scaled = gated * scale
-            mean = jnp.sum(g_o_ref[at].astype(F32) * k["out"][at].astype(F32), axis=-1, keepdims=True)
-            mean = mean * scale * scale * (1.0 / INNER)
+            if s:
+                mean = k["scale"][at][:, 1:2]
+            else:
+                mean = jnp.sum(g_o_ref[at].astype(F32) * k["out"][at].astype(F32), axis=-1, keepdims=True)
+                mean = mean * scale * scale * (1.0 / INNER)
             wide_x[at] = (scaled * gain).astype(BF)
             d_gated = scale * gain * dm - gated * mean
             d_y = d_gated * gate_silu
@@ -864,6 +962,11 @@
         b_rows, c_rows = bc_act[:, :STATE], bc_act[:, STATE:]
         chain_load(dot_first(c_rows, wide_y[...]), k["decay"], chain_out)
         copies = spread_send(chain_out, chain_in, me, c_sems[0].at[s], c_sems[1].at[s])
+        if s:
+
+            @pl.when(core == 1)
+            def _():
+                swapped(0, saved[0]["following"], section_ref).start()
 
         if s == 0:
             for piece in range(2):
@@ -925,6 +1028,31 @@
         if s == 0:
             next(late)
             next(loose)
+        if s:
+            load_final.wait()
+            finish(final_copies)
+
+            @pl.loop(0, BLOCKS)
+            def _(i):
+                at = rows_at(i)
+                total = final_own[at].astype(F32)
+                for d in range(3):
+                    total = total + final_in[d, at].astype(F32)
+                total = (total * k["scale"][at][:, 0:1]).astype(BF).astype(F32)
+                final_own[at] = (v_ref[at, quarter(place)].astype(F32) + total).astype(BF)
+
+            for d in range(3):
+                final(d, core).start()
+
+            @pl.when(core == 1)
+            def _():
+                final_stay().start()
+
+            @pl.when(core == 0)
+            def _():
+                final(3, core).start()
+                pltpu.make_async_copy(v_all.at[1], section_ref.at[0], move_sem.at[0]).start()
+
         chain_unload(chain_got, state_grad)
         norm_ref[...] = jnp.zeros_like(norm_ref)
         taps_ref[...] = jnp.zeros_like(taps_ref)
@@ -1117,33 +1245,35 @@
             pltpu.make_async_copy(d_v.at[s], leaving_ref.at[s], move_sem.at[1]).start()
 
         if s:
-
-            @pl.when(core == 0)
-            def _():
-                pltpu.make_async_copy(v_all.at[1], section_ref.at[0], move_sem.at[0]).start()
-
             finish(load_rows(0))
-
-            @pl.when(core == 1)
-            def _():
-                pltpu.make_async_copy(last_ref, g_o_buf, move_sem.at[0]).start()
-
-    @pl.when(core == 1)
-    def _():
-        pltpu.make_async_copy(last_ref, g_o_buf, move_sem.at[0]).wait()
-        pltpu.make_async_copy(g_o_buf, section_ref.at[1], move_sem.at[0]).start()
 
     for turn in (loose, late, loose, late, loose, late, loose, early, late, old_early, old_late, old_loose):
         next(turn)
     for piece in range(2):
         cross(0, piece).wait_send()
-    swapped(0, last_ref, section_ref).wait()
+    for d in range(3):
+        final(d, core).wait_send()
+
+    @pl.when(core == 0)
+    def _():
+        swapped(0, d_v.at[0], section_ref).wait_recv()
+        pltpu.make_async_copy(v_all.at[1], section_ref.at[0], move_sem.at[0]).wait()
+        final(3, core).wait_send()
+
+    @pl.when(core == 1)
+    def _():
+        swapped(0, saved[0]["following"], section_ref).wait_send()
+        final_stay().wait()
+        for d in range(3):
+            final(d, 1).wait_recv()
+        for d in range(4):
+            final(d, 0).wait_recv()
+
     swapped(1, d_v.at[0], leaving_ref).wait()
     pltpu.make_async_copy(d_v.at[0], leaving_ref.at[0], move_sem.at[1]).wait()
-    pltpu.make_async_copy(d_v.at[0], section_ref.at[0], move_sem.at[0]).wait()
-
-
-def backward(cotangent, x_in, last, held, smalls, dt_all, kept, number):
+
+
+def backward(cotangent, x_in, part, held, smalls, dt_all, kept, number):
     dma = pltpu.SemaphoreType.DMA
     regular = pltpu.SemaphoreType.REGULAR
     sds = jax.ShapeDtypeStruct
@@ -1205,7 +1335,9 @@
     scratch += [dma((2, 16))] * 4 + [dma((2, 8))] * 2 + [dma((2, 4))] * 2
     scratch += [dma((2,))] * 4 + [dma((2, 2))] * 2
     scratch += [dma((2, 2, 2, 4))] * 7 + [dma((2, 2, 2, 2, 4))]
-    scratch += [dma((2, 3))] * 2 + [dma((2, 8))] * 2 + [regular, regular((2,))]
+    scratch += [dma((2, 3))] * 2 + [dma((2, 8))] * 2
+    scratch += [vm((8, ROWS), F32), vm((3, 8, ROWS), F32), vm((3, ROWS, 384), BF), vm((ROWS, 384), BF)]
+    scratch += [dma((3,))] * 4 + [dma((4,)), dma((2, 4)), regular, regular((2,))]
     flat = [kept[s][name] for s in range(2) for name, _, _ in KEPT]
     return pl.pallas_call(
         backward_kernel,
@@ -1220,21 +1352,42 @@
         scratch_shapes=scratch,
         compiler_params=comm_params(number),
         name="backward_layers",
-    )(cotangent, x_in, last, *held, smalls, dt_all, *flat)
+    )(cotangent, x_in, part, *held, smalls, dt_all, *flat)
 
 
 def widen_kernel(
     a_ref, rest_ref, zx_ref, out_ref, bc_ref, dt_ref, norm_ref, bias_ref, rate_ref, skip_ref, conv_ref, conv_bc_ref,
-    gate_ref, bc_all,
+    gate_ref, bc_all, wide, sem,
 ):
     step = pl.program_id(0)
+    slot = lax.rem(step, 2)
+
+    def moves(step, slot):
+        return [
+            pltpu.make_async_copy(
+                wide.at[slot, h, kind],
+                zx_ref.at[pl.ds(h * INNER_DEV + step * 2 * PART, 2 * PART), kind, :],
+                sem.at[slot, h, kind],
+            )
+            for h in range(2)
+            for kind in range(2)
+        ]
+
+    @pl.when(step >= 2)
+    def _():
+        finish(moves(step - 2, slot))
+
     for h in range(2):
         cols = slice(h * INNER_DEV, (h + 1) * INNER_DEV)
-        zx_ref[h, :, 0, :] = a_ref[h, 0, PART:EARLY].astype(F32)
-        zx_ref[h, :, 1, :] = a_ref[h, 0, EARLY:WIDE].astype(F32)
-        out_ref[:, cols] = a_ref[h, 0, 0:PART].astype(F32)
-        at = pl.ds(pl.multiple_of(step * 16, 16), 16)
-        bc_all[at, cols] = a_ref[h, 0, WIDE:SUB].astype(F32)
+        for n in range(2):
+            rows = slice(n * PART, n * PART + PART)
+            wide[slot, h, 0, rows] = a_ref[h, n, PART:EARLY].astype(F32)
+            wide[slot, h, 1, rows] = a_ref[h, n, EARLY:WIDE].astype(F32)
+            out_ref[rows, cols] = a_ref[h, n, 0:PART].astype(F32)
+            at = pl.ds(pl.multiple_of(step * 32 + n * 16, 16), 16)
+            bc_all[at, cols] = a_ref[h, n, WIDE:SUB].astype(F32)
+    for move in moves(step, slot):
+        move.start()
 
     @pl.when(step == 0)
     def _():
@@ -1259,30 +1412,36 @@
         bias_ref[...] = rows[8:9, 0:HEADS_DEV]
         conv_bc_ref[...] = rows[9:13, 0:256]
 
-    @pl.when(step == 15)
+    @pl.when(step == 7)
     def _():
         bc_ref[...] = bc_all[...].T
+        finish(moves(step - 1, 1 - slot))
+        finish(moves(step, slot))
 
 
 def widen(total, rest):
     total = total.reshape(2, 16, SUB, INNER_DEV)
     fixed = ((WIDTH, 256), (HEADS_DEV, WIDTH), (1, WIDTH)) + ((1, HEADS_DEV),) * 3
     fixed += ((4, INNER_DEV), (4, 256), (1, INNER_DEV))
-    shapes = ((2, INNER_DEV, 2, INNER_DEV), (INNER_DEV, WIDTH)) + fixed
+    shapes = ((WIDTH, 2, INNER_DEV), (INNER_DEV, WIDTH)) + fixed
     return pl.pallas_call(
         widen_kernel,
-        grid=(16,),
+        grid=(8,),
         out_shape=[jax.ShapeDtypeStruct(shape, F32) for shape in shapes],
         in_specs=[
-            pl.BlockSpec((2, 1, SUB, INNER_DEV), lambda i: (0, i, 0, 0)),
+            pl.BlockSpec((2, 2, SUB, INNER_DEV), lambda i: (0, i, 0, 0)),
             pl.BlockSpec((2, REST, INNER_DEV), lambda i: (0, 0, 0)),
         ],
         out_specs=[
-            pl.BlockSpec((2, PART, 2, INNER_DEV), lambda i: (0, i, 0, 0)),
-            pl.BlockSpec((PART, WIDTH), lambda i: (i, 0)),
+            ANY,
+            pl.BlockSpec((2 * PART, WIDTH), lambda i: (i, 0)),
         ]
         + [pl.BlockSpec(shape, lambda i: (0, 0)) for shape in fixed],
-        scratch_shapes=[pltpu.VMEM((256, WIDTH), F32)],
+        scratch_shapes=[
+            pltpu.VMEM((256, WIDTH), F32),
+            pltpu.VMEM((2, 2, 2, 2 * PART, INNER_DEV), F32),
+            pltpu.SemaphoreType.DMA((2, 2, 2)),
+        ],
         compiler_params=pltpu.CompilerParams(vmem_limit_bytes=VMEM_CAP),
         name="widen",
     )(total, rest)
@@ -1306,17 +1465,17 @@
     zx_m = w_zx[0].reshape(WIDTH, WIDTH)
     bc_m, out_m, dt_m = w_bc[0], w_out[0], w_dt[0].T
     small_args = (norm_gain, gate_gain, conv_x[0], conv_bc[0], dt_bias, a_log, d_skip)
-    kept, (zx_t, bc_t, out_t, smalls, dt_all) = forward(x_in, zx_m, bc_m, out_m, dt_m, small_args, 0)
+    kept, (zx_t, bc_t, out_t, smalls, dt_all, part) = forward(x_in, zx_m, bc_m, out_m, dt_m, small_args, 0)
     held = (zx_m, bc_m, out_m, zx_t, bc_t, out_t)
     total, rest, section_out, grads_in = backward(
-        cotangent, x_in, kept[1]["following"], held, smalls, dt_all, kept, 1
+        cotangent, x_in, part, held, smalls, dt_all, kept, 1
     )
     g_zx, g_out, g_bc, g_dt, g_norm, g_bias, g_rate, g_skip, g_conv_x, g_conv_bc, g_gate = widen(total, rest)
     return (
         section_out[None],
         grads_in[None],
         g_norm,
-        g_zx.reshape(1, WIDTH, 2, INNER_DEV),
+        g_zx[None],
         g_bc[None],
         g_dt.T[None],
         g_bias,

time: 295 us -> 268 us (0.908)
  Pallas kernels: 284 us -> 257 us
    pallas_call x1, Pallas kernels: 103 us -> 76.8 us  [forward(): pl.pallas_call(forward_kernel, out_shape=[sds(shape, kind) for _, shape,...]
    pallas_call x1, Pallas kernels: 15 us -> 11.5 us  [widen(): pl.pallas_call(widen_kernel, grid=(8,), out_shape=[jax.ShapeDtypeStruct(s...]
where the time goes in v4:
time: 268 us
  Pallas kernels  257 us (96%)
  local copies, waits for them, and re-layouts  9.47 us (4%)
    pallas_call x1, Pallas kernels, backward(): pl.pallas_call(backward_kernel, out_shape=[sds((2,) + halves, BF), sds((2...  169 us
    pallas_call x1, Pallas kernels, forward(): pl.pallas_call(forward_kernel, out_shape=[sds(shape, kind) for _, shape,...  76.8 us
    pallas_call x1, Pallas kernels, widen(): pl.pallas_call(widen_kernel, grid=(8,), out_shape=[jax.ShapeDtypeStruct(s...  11.5 us
    unnamed x8, local copies, waits for them, and re-layouts  9.47 us

profile of v4, /device:TPU:0, one launch (start us, length us, event | category | flops | bytes accessed | tf_op | source)
XLA Modules:
  0.0 267.6 jit_solution(12303855335842304093)
XLA Ops:
  0.6 5.5 %copy.27 = bf16[192,8,2,768]{3,1,2,0:T(8,128)(2,1)} copy(bf16[192,8,2,768]{3,2,1,0:T(2,128)(2,1)} %bitcast.26) | data formatting | bytes 9437184
  6.1 76.8 %forward_layers.1 = (bf16[272,1536]{1,0:T(8,128)(2,1)}, f32[256,768]{1,0:T(8,128)}, f32[272,768]{1,0:T(8,128)}, f32[272,256]{1,0:T(8,128)}, f32[256,128]{1,0:T(8...) custom-call(bf16[2,256,1536]{2,1,0:T(8,128)(2,1)} %refs_1_.1, ...), custom_call_target="tpu_custom_call" | custom-call | tf_op jit(solution)/shard_map/forward_layers/pallas_call | solution.py:520
  82.9 169.2 %backward_layers.1 = (bf16[2,4,4,160,768]{4,3,2,1,0:T(8,128)(2,1)}, bf16[2,32,768]{2,1,0:T(8,128)(2,1)}, bf16[2,256,1536]{2,1,0:T(8,128)(2,1)}, bf16[2,256,1536]{2,1,0:T(8,128)(2,1)}) custom-call(bf16[2,256,1536]{2,1,0:T(8,128)(2,1)} %refs_0_.3, bf16[2,256,1536]{2,1,0:T(8,128)(2,1)} %refs_1_.1, bf16[256,1536]{1,0:T(8,128)(2,1)} %get-tuple-element.66.refs_2_, ...), custom_call_target="tpu_custom_call" | custom-call | tf_op jit(solution)/shard_map/backward_layers/pallas_call | solution.py:1342
  252.1 0.0 copy-start.1
  252.1 11.5 %widen.1 = (f32[1536,2,768]{2,1,0:T(2,128)}, f32[768,1536]{1,0:T(8,128)}, f32[1536,256]{1,0:T(8,128)}, f32[12,1536]{1,0:T(8,128)}, f32[1,1536]{1,0:T(1,128)}, /*...) custom-call(bf16[2,16,160,768]{3,2,1,0:T(8,128)(2,1)} %bitcast.25, ...), custom_call_target="tpu_custom_call" | custom-call | tf_op jit(solution)/shard_map/widen/pallas_call | solution.py:1427
  263.6 0.0 copy-start
  263.6 1.7 copy.26
  265.3 0.0 copy-done.1
  265.3 1.1 copy.30
  266.5 0.0 copy-done
  266.5 1.1 copy.31
Async XLA Ops:
  252.1 13.2 %copy-start.1 = (bf16[2,256,1536]{2,1,0:T(8,128)(2,1)S(1)}, bf16[2,256,1536]{2,1,0:T(8,128)(2,1)}, u32[]{:S(2)}) copy-start(bf16[2,256,1536]{2,1,0:T(8,128)(2,1)} %get-tuple-element.104) | copy-start | bytes 4718596
  263.6 2.9 %copy-start = (bf16[2,256,1536]{2,1,0:T(8,128)(2,1)S(1)}, bf16[2,256,1536]{2,1,0:T(8,128)(2,1)}, u32[]{:S(2)}) copy-start(bf16[2,256,1536]{2,1,0:T(8,128)(2,1)} %get-tuple-element.105) | copy-start | bytes 4718596

commit v5 on v4

--- a/solution.py
+++ b/solution.py
@@ -75,7 +75,7 @@
 
 
 S_NORM, S_GATE, S_CONV, S_BIAS, S_RATE, S_SKIP = 0, 1, 2, 6, 7, 9
-STEP = 32
+STEP = 64
 BLOCKS = ROWS // STEP
 
 
@@ -1021,10 +1021,10 @@
         finish(copies)
         chain_scan(False, chain_in, chain_back)
         copies = spread_send(chain_back, chain_got, me, c_sems[2].at[s], c_sems[3].at[s])
+        heads_of(1)
+        finish(copies)
         old_early, early = early, reduction(s, 0)
         next(early)
-        heads_of(1)
-        finish(copies)
         if s == 0:
             next(late)
             next(loose)
@@ -1129,11 +1129,11 @@
             for move in load_kept(0):
                 move.start()
 
+        next(early)
         if s == 0:
             next(loose)
             next(late)
         else:
-            next(early)
             for seq in along_z + along_x:
                 pl.semaphore_signal(first_free.at[0], inc=1, device_id={"seq": seq}, device_id_type=MESH)
         rim.wait()
@@ -1208,8 +1208,6 @@
         if s == 0:
             next(late)
         finish(copies)
-        if s == 0:
-            next(early)
         norm_ref[...] = jnp.zeros_like(norm_ref)
 
         @pl.loop(0, BLOCKS)

time: 268 us -> 265 us (0.989)
  Pallas kernels: 257 us -> 254 us
where the time goes in v5:
time: 265 us; the launch traced here: 264 us
  Pallas kernels  254 us (96%)
  local copies, waits for them, and re-layouts  9.47 us (4%)
    pallas_call x1, Pallas kernels, backward(): pl.pallas_call(backward_kernel, out_shape=[sds((2,) + halves, BF), sds((2...  167 us
    pallas_call x1, Pallas kernels, forward(): pl.pallas_call(forward_kernel, out_shape=[sds(shape, kind) for _, shape,...  75.1 us
    pallas_call x1, Pallas kernels, widen(): pl.pallas_call(widen_kernel, grid=(8,), out_shape=[jax.ShapeDtypeStruct(s...  11.5 us
    unnamed x8, local copies, waits for them, and re-layouts  9.47 us

profile of v5, /device:TPU:0, one launch (start us, length us, event | category | flops | bytes accessed | tf_op | source)
XLA Modules:
  0.0 264.1 jit_solution(10827539372520340168)
XLA Ops:
  0.6 5.5 %copy.27 = bf16[192,8,2,768]{3,1,2,0:T(8,128)(2,1)} copy(bf16[192,8,2,768]{3,2,1,0:T(2,128)(2,1)} %bitcast.26) | data formatting | bytes 9437184
  6.1 75.1 %forward_layers.1 = (bf16[272,1536]{1,0:T(8,128)(2,1)}, f32[256,768]{1,0:T(8,128)}, f32[272,768]{1,0:T(8,128)}, f32[272,256]{1,0:T(8,128)}, f32[256,128]{1,0:T(8...) custom-call(bf16[2,256,1536]{2,1,0:T(8,128)(2,1)} %refs_1_.1, ...), custom_call_target="tpu_custom_call" | custom-call | tf_op jit(solution)/shard_map/forward_layers/pallas_call | solution.py:520
  81.2 167.4 %backward_layers.1 = (bf16[2,4,4,160,768]{4,3,2,1,0:T(8,128)(2,1)}, bf16[2,32,768]{2,1,0:T(8,128)(2,1)}, bf16[2,256,1536]{2,1,0:T(8,128)(2,1)}, bf16[2,256,1536]{2,1,0:T(8,128)(2,1)}) custom-call(bf16[2,256,1536]{2,1,0:T(8,128)(2,1)} %refs_0_.3, bf16[2,256,1536]{2,1,0:T(8,128)(2,1)} %refs_1_.1, bf16[256,1536]{1,0:T(8,128)(2,1)} %get-tuple-element.66.refs_2_, ...), custom_call_target="tpu_custom_call" | custom-call | tf_op jit(solution)/shard_map/backward_layers/pallas_call | solution.py:1340
  248.6 0.0 copy-start.1
  248.6 11.5 %widen.1 = (f32[1536,2,768]{2,1,0:T(2,128)}, f32[768,1536]{1,0:T(8,128)}, f32[1536,256]{1,0:T(8,128)}, f32[12,1536]{1,0:T(8,128)}, f32[1,1536]{1,0:T(1,128)}, /*...) custom-call(bf16[2,16,160,768]{3,2,1,0:T(8,128)(2,1)} %bitcast.25, ...), custom_call_target="tpu_custom_call" | custom-call | tf_op jit(solution)/shard_map/widen/pallas_call | solution.py:1425
  260.1 0.0 copy-start
  260.1 1.7 copy.26
  261.8 0.0 copy-done.1
  261.8 1.1 copy.30
  263.0 0.0 copy-done
  263.0 1.1 copy.31
Async XLA Ops:
  248.6 13.2 %copy-start.1 = (bf16[2,256,1536]{2,1,0:T(8,128)(2,1)S(1)}, bf16[2,256,1536]{2,1,0:T(8,128)(2,1)}, u32[]{:S(2)}) copy-start(bf16[2,256,1536]{2,1,0:T(8,128)(2,1)} %get-tuple-element.104) | copy-start | bytes 4718596
  260.1 2.9 %copy-start = (bf16[2,256,1536]{2,1,0:T(8,128)(2,1)S(1)}, bf16[2,256,1536]{2,1,0:T(8,128)(2,1)}, u32[]{:S(2)}) copy-start(bf16[2,256,1536]{2,1,0:T(8,128)(2,1)} %get-tuple-element.105) | copy-start | bytes 4718596

commit v6 on v5

--- a/solution.py
+++ b/solution.py
@@ -1391,8 +1391,9 @@
     def _():
         rows = rest_ref[0].astype(F32)
         more = rest_ref[1].astype(F32)
-        dt_ref[:, :INNER_DEV] = rows[0:HEADS_DEV]
-        dt_ref[:, INNER_DEV:] = more[0:HEADS_DEV]
+        for h in range(HEADS_DEV):
+            dt_ref[h, :, :INNER_DEV] = rows[h : h + 1]
+            dt_ref[h, :, INNER_DEV:] = more[h : h + 1]
         rows = rows[16:]
         norm_ref[:, :INNER_DEV] = rows[0:1]
         norm_ref[:, INNER_DEV:] = more[16:17]
@@ -1419,7 +1420,7 @@
 
 def widen(total, rest):
     total = total.reshape(2, 16, SUB, INNER_DEV)
-    fixed = ((WIDTH, 256), (HEADS_DEV, WIDTH), (1, WIDTH)) + ((1, HEADS_DEV),) * 3
+    fixed = ((WIDTH, 256), (HEADS_DEV, 1, WIDTH), (1, WIDTH)) + ((1, HEADS_DEV),) * 3
     fixed += ((4, INNER_DEV), (4, 256), (1, INNER_DEV))
     shapes = ((WIDTH, 2, INNER_DEV), (INNER_DEV, WIDTH)) + fixed
     return pl.pallas_call(
@@ -1434,7 +1435,7 @@
             ANY,
             pl.BlockSpec((2 * PART, WIDTH), lambda i: (i, 0)),
         ]
-        + [pl.BlockSpec(shape, lambda i: (0, 0)) for shape in fixed],
+        + [pl.BlockSpec(shape, lambda i, n=len(shape): (0,) * n) for shape in fixed],
         scratch_shapes=[
             pltpu.VMEM((256, WIDTH), F32),
             pltpu.VMEM((2, 2, 2, 2 * PART, INNER_DEV), F32),
@@ -1475,7 +1476,7 @@
         g_norm,
         g_zx[None],
         g_bc[None],
-        g_dt.T[None],
+        g_dt.transpose(1, 2, 0),
         g_bias,
         g_rate,
         g_skip,

time: 265 us -> 264 us (level)
    unnamed x8 -> x7, local copies, waits for them, and re-layouts: 9.47 us -> 8.56 us
where the time goes in v6:
time: 264 us; the launch traced here: 263 us
  Pallas kernels  254 us (96%)
  local copies, waits for them, and re-layouts  8.56 us (3%)
    pallas_call x1, Pallas kernels, backward(): pl.pallas_call(backward_kernel, out_shape=[sds((2,) + halves, BF), sds((2...  167 us
    pallas_call x1, Pallas kernels, forward(): pl.pallas_call(forward_kernel, out_shape=[sds(shape, kind) for _, shape,...  75.1 us
    pallas_call x1, Pallas kernels, widen(): pl.pallas_call(widen_kernel, grid=(8,), out_shape=[jax.ShapeDtypeStruct(s...  11.5 us
    unnamed x7, local copies, waits for them, and re-layouts  8.56 us

profile of v6, /device:TPU:0, one launch (start us, length us, event | category | flops | bytes accessed | tf_op | source)
XLA Modules:
  0.0 263.2 jit_solution(7963964890932179782)
XLA Ops:
  0.6 5.5 %copy.26 = bf16[192,8,2,768]{3,1,2,0:T(8,128)(2,1)} copy(bf16[192,8,2,768]{3,2,1,0:T(2,128)(2,1)} %bitcast.24) | data formatting | bytes 9437184
  6.1 75.1 %forward_layers.1 = (bf16[272,1536]{1,0:T(8,128)(2,1)}, f32[256,768]{1,0:T(8,128)}, f32[272,768]{1,0:T(8,128)}, f32[272,256]{1,0:T(8,128)}, f32[256,128]{1,0:T(8...) custom-call(bf16[2,256,1536]{2,1,0:T(8,128)(2,1)} %refs_1_.1, ...), custom_call_target="tpu_custom_call" | custom-call | tf_op jit(solution)/shard_map/forward_layers/pallas_call | solution.py:520
  81.2 167.4 %backward_layers.1 = (bf16[2,4,4,160,768]{4,3,2,1,0:T(8,128)(2,1)}, bf16[2,32,768]{2,1,0:T(8,128)(2,1)}, bf16[2,256,1536]{2,1,0:T(8,128)(2,1)}, bf16[2,256,1536]{2,1,0:T(8,128)(2,1)}) custom-call(bf16[2,256,1536]{2,1,0:T(8,128)(2,1)} %refs_0_.3, bf16[2,256,1536]{2,1,0:T(8,128)(2,1)} %refs_1_.1, bf16[256,1536]{1,0:T(8,128)(2,1)} %get-tuple-element.66.refs_2_, ...), custom_call_target="tpu_custom_call" | custom-call | tf_op jit(solution)/shard_map/backward_layers/pallas_call | solution.py:1340
  248.6 0.0 copy-start.1
  248.6 11.5 %widen.1 = (f32[1536,2,768]{2,1,0:T(2,128)}, f32[768,1536]{1,0:T(8,128)}, f32[1536,256]{1,0:T(8,128)}, f32[12,1,1536]{2,1,0:T(1,128)}, f32[1,1536]{1,0:T(1,128)}...) custom-call(bf16[2,16,160,768]{3,2,1,0:T(8,128)(2,1)} %bitcast.23, ...), custom_call_target="tpu_custom_call" | custom-call | tf_op jit(solution)/shard_map/widen/pallas_call | solution.py:1426
  260.1 0.0 copy-start
  260.1 0.0 copy-done.1
  260.1 1.1 copy.29
  261.3 0.8 copy-done
  262.1 1.1 copy.30
Async XLA Ops:
  248.6 11.5 %copy-start.1 = (bf16[2,256,1536]{2,1,0:T(8,128)(2,1)S(1)}, bf16[2,256,1536]{2,1,0:T(8,128)(2,1)}, u32[]{:S(2)}) copy-start(bf16[2,256,1536]{2,1,0:T(8,128)(2,1)} %get-tuple-element.104) | copy-start | bytes 4718596
  260.1 2.0 copy-start
